TPU v7x, 32 devices: a whole 2x2x4 slice. The times are simulated.
32 devices in a mesh: dp: 8 (over y, x, core), seq: 4 (over z).
Axes of the slice: x: 2, y: 2, z: 4, core: 2. Of those that a mesh axis runs over, the one named last changes fastest.
Arguments:
- tokens: bfloat16 [64, 256, 768], P('dp', 'seq'), may hold values from -6 to 6
- lengths: int32 [64], P('dp'), may hold values from 193 to 197, as said below
- w_qkv: bfloat16 [768, 2304], P(('dp', 'seq')), may hold values from -0.25 to 0.25
- w_out: bfloat16 [768, 768], P(('dp', 'seq')), may hold values from -0.75 to 0.75
- router: bfloat16 [768, 8], P(('dp', 'seq')), may hold values from -0.109375 to 0.109375
- gain_one: bfloat16 [768], P(('dp', 'seq')), may hold values from 0.5 to 1.5
- shift_one: bfloat16 [768], P(('dp', 'seq')), may hold values from -0.59765625 to 0.59765625
- gain_two: bfloat16 [768], P(('dp', 'seq')), may hold values from 0.5 to 1.5
- shift_two: bfloat16 [768], P(('dp', 'seq')), may hold values from -0.59765625 to 0.59765625
- w_up: bfloat16 [8, 768, 3072], P('dp', None, 'seq'), may hold values from -2 to 2
- w_down: bfloat16 [8, 3072, 768], P('dp', 'seq'), may hold values from -1.75 to 1.75
- cotangent: bfloat16 [64, 256, 768], P('dp', 'seq'), may hold values from -6 to 6
Outputs:
- block_out: bfloat16 [64, 256, 768], P('dp', 'seq')
- grad_input: float32 [64, 256, 768], P('dp', 'seq')
- grad_qkv: float32 [768, 2304], P(('dp', 'seq'))
- grad_out_w: float32 [768, 768], P(('dp', 'seq'))
- grad_router: float32 [768, 8], P(('dp', 'seq'))
- grad_gain_one: float32 [768], P(('dp', 'seq'))
- grad_shift_one: float32 [768], P(('dp', 'seq'))
- grad_gain_two: float32 [768], P(('dp', 'seq'))
- grad_shift_two: float32 [768], P(('dp', 'seq'))
- grad_up: float32 [8, 768, 3072], P('dp', None, 'seq')
- grad_down: float32 [8, 3072, 768], P('dp', 'seq')
Inputs may be any that keep to these rules, and one draw needn't show every extreme that they name: `lengths`: each image's count of valid tokens, which are its first positions; some image has exactly 197.
All inputs are finite; a program needn't handle non-finite values.
Results may differ from a plain program's by a relative error of at most 0.025.
Values may be sent and summed in bfloat16 or wider, within the bound.
A program may use at most 128 MiB of HBM per device.

v0:
```python
import jax
import jax.numpy as jnp
from jax import lax
from jax.sharding import PartitionSpec as P

H = 12
HD = 64
MB = 2


def combined_all(shard, axis, combine):
    everything = jax.tree.map(
        lambda part, kind: lax.all_gather(part.astype(kind), axis),
        shard,
        (jnp.bfloat16, jnp.bfloat16, jnp.bfloat16),
    )

    def take(k):
        return jax.tree.map(lambda part, own: part[k].astype(own.dtype), everything, shard)

    return lax.fori_loop(
        1, lax.axis_size(axis), lambda k, so_far: combine(so_far, take(k)), take(0)
    )


def layer_norm(values, gain_vec, shift_vec):
    centred = values - jnp.mean(values, axis=-1, keepdims=True)
    inverse = lax.rsqrt(jnp.mean(centred * centred, axis=-1, keepdims=True) + 1e-06)
    unit_rows = centred * inverse
    return (unit_rows * gain_vec + shift_vec, unit_rows, inverse)


def layer_norm_back(grad_rows, unit_rows, inverse, gain_vec):
    model_width = grad_rows.shape[-1]
    scaled = grad_rows * gain_vec
    centred = scaled - jnp.mean(scaled, axis=-1, keepdims=True)
    correction = unit_rows * jnp.mean(scaled * unit_rows, axis=-1, keepdims=True)
    grad_gain = jnp.sum((grad_rows * unit_rows).reshape(-1, model_width), axis=0)
    grad_shift = jnp.sum(grad_rows.reshape(-1, model_width), axis=0)
    return (inverse * (centred - correction), grad_gain, grad_shift)


def gelu_tanh(values):
    return jax.nn.gelu(values, approximate=True)


def merge_slots(earlier, later):
    highest = jnp.maximum(earlier[0], later[0])
    left_scale = jnp.exp(earlier[0] - highest)
    right_scale = jnp.exp(later[0] - highest)
    return (
        highest,
        earlier[1] * left_scale + later[1] * right_scale,
        earlier[2] * left_scale[:, :, None] + later[2] * right_scale[:, :, None],
    )


def gather_params(w_qkv, w_out, router, gain_one, shift_one, gain_two, shift_two):
    return (
        lax.all_gather(w_qkv, ("dp", "seq"), axis=0, tiled=True),
        lax.all_gather(w_out, ("dp", "seq"), axis=0, tiled=True),
        lax.all_gather(router, ("dp", "seq"), axis=0, tiled=True),
        lax.all_gather(gain_one, ("dp", "seq"), axis=0, tiled=True),
        lax.all_gather(shift_one, ("dp", "seq"), axis=0, tiled=True),
        lax.all_gather(gain_two, ("dp", "seq"), axis=0, tiled=True),
        lax.all_gather(shift_two, ("dp", "seq"), axis=0, tiled=True),
    )


def attention_scores(queries, keys_all, key_valid):
    scores = jnp.einsum(
        "bqhd,bkhd->bhqk", queries, keys_all, preferred_element_type=jnp.float32
    ) * HD ** (-0.5)
    return jnp.where(key_valid[:, None, None, :], scores, -1000000000.0)


def forward_batch(tokens_part, lengths_part, params, w_up, w_down):
    w_qkv, w_out, router, gain_one, shift_one, gain_two, shift_two = params
    groups = lax.axis_size("seq")
    seq_place = lax.axis_index("seq")
    images, block_len, model_width = tokens_part.shape
    length_all = block_len * groups
    heads_dev = H // groups
    per_head = heads_dev * HD
    positions = seq_place * block_len + jnp.arange(block_len, dtype=jnp.int32)
    valid_own = positions[None, :] < lengths_part[:, None]
    key_valid = jnp.arange(length_all, dtype=jnp.int32)[None, :] < lengths_part[:, None]
    inputs = tokens_part.astype(jnp.float32)
    normed, unit_one, inverse_one = layer_norm(
        inputs, gain_one.astype(jnp.float32), shift_one.astype(jnp.float32)
    )
    normed_low = normed.astype(jnp.bfloat16)
    mixed_qkv = jnp.einsum(
        "btd,de->bte", normed_low, w_qkv, preferred_element_type=jnp.float32
    ).astype(jnp.bfloat16)
    mixed_qkv = mixed_qkv.reshape(images, block_len, 3, groups, per_head)
    spread = lax.all_to_all(mixed_qkv, "seq", split_axis=3, concat_axis=1, tiled=True)
    queries = spread[:, :, 0, 0].reshape(images, length_all, heads_dev, HD)
    keys_all = spread[:, :, 1, 0].reshape(images, length_all, heads_dev, HD)
    values_all = spread[:, :, 2, 0].reshape(images, length_all, heads_dev, HD)
    scores = attention_scores(queries, keys_all, key_valid)
    highest = jnp.max(scores, axis=-1, keepdims=True)
    exponent = jnp.exp(scores - highest)
    totals = jnp.sum(exponent, axis=-1, keepdims=True)
    attn_probs = exponent / totals
    log_total = highest + jnp.log(totals)
    attended = jnp.einsum(
        "bhqk,bkhd->bqhd",
        attn_probs.astype(jnp.bfloat16),
        values_all,
        preferred_element_type=jnp.float32,
    )
    attended = attended.astype(jnp.bfloat16).reshape(images, length_all, per_head)
    attn_tok = lax.all_to_all(attended, "seq", split_axis=1, concat_axis=2, tiled=True)
    branch = jnp.einsum("btd,de->bte", attn_tok, w_out, preferred_element_type=jnp.float32)
    middle = inputs + branch
    normed_two, unit_two, inverse_two = layer_norm(
        middle, gain_two.astype(jnp.float32), shift_two.astype(jnp.float32)
    )
    normed_two_low = normed_two.astype(jnp.bfloat16)
    logits = jnp.einsum("btd,de->bte", normed_two_low, router, preferred_element_type=jnp.float32)
    block_peak = jnp.floor(jnp.max(jnp.where(valid_own[:, :, None], logits, -1000000000.0), axis=1))
    dispatch = jnp.where(valid_own[:, :, None], jnp.exp(logits - block_peak[:, None, :]), 0.0)
    numerator = jnp.einsum(
        "bte,btd->bed",
        dispatch.astype(jnp.bfloat16),
        normed_two_low,
        preferred_element_type=jnp.float32,
    )
    slot_top, denominator, numer_all = combined_all(
        (block_peak, jnp.sum(dispatch, axis=1), numerator), "seq", merge_slots
    )
    slot_vals = numer_all / denominator[:, :, None]
    factor = jnp.exp(block_peak - slot_top)
    slot_rows = lax.all_to_all(
        slot_vals.astype(jnp.bfloat16), "dp", split_axis=1, concat_axis=0, tiled=True
    )
    hidden = jnp.einsum("red,edf->ref", slot_rows, w_up, preferred_element_type=jnp.float32)
    active = gelu_tanh(hidden).astype(jnp.bfloat16)
    partial_value = jnp.einsum("ref,efd->red", active, w_down, preferred_element_type=jnp.float32)
    expert_rows = lax.psum(partial_value.astype(jnp.bfloat16), "seq")
    expert_out = lax.all_to_all(expert_rows, "dp", split_axis=0, concat_axis=1, tiled=True)
    combine = jax.nn.softmax(logits, axis=-1)
    combine_low = combine.astype(jnp.bfloat16)
    moe_out = jnp.einsum(
        "bte,bed->btd", combine_low, expert_out, preferred_element_type=jnp.float32
    )
    result = (middle + moe_out).astype(jnp.bfloat16)
    kept_state = (
        unit_one,
        inverse_one,
        normed_low,
        queries,
        keys_all,
        values_all,
        key_valid,
        log_total,
        attn_tok,
        unit_two,
        inverse_two,
        normed_two_low,
        dispatch,
        factor,
        denominator,
        slot_vals,
        slot_rows,
        hidden,
        active,
        expert_out,
        combine,
        combine_low,
    )
    return (result, kept_state)


def backward_batch(cot_part, params, w_up, w_down, kept_state):
    (
        unit_one,
        inverse_one,
        normed_low,
        queries,
        keys_all,
        values_all,
        key_valid,
        log_total,
        attn_tok,
        unit_two,
        inverse_two,
        normed_two_low,
        dispatch,
        factor,
        denominator,
        slot_vals,
        slot_rows,
        hidden,
        active,
        expert_out,
        combine,
        combine_low,
    ) = kept_state
    w_qkv, w_out, router, gain_one, shift_one, gain_two, shift_two = params
    groups = lax.axis_size("seq")
    images, block_len, model_width = cot_part.shape
    length_all = block_len * groups
    heads_dev = H // groups
    per_head = heads_dev * HD
    score_scale = HD ** (-0.5)
    d_combine = jnp.einsum("btd,bed->bte", cot_part, expert_out, preferred_element_type=jnp.float32)
    slot_part = jnp.einsum(
        "bte,btd->bed", combine_low, cot_part, preferred_element_type=jnp.float32
    )
    d_expert = lax.psum(slot_part.astype(jnp.bfloat16), "seq")
    d_rows = lax.all_to_all(d_expert, "dp", split_axis=1, concat_axis=0, tiled=True)
    d_active = jnp.einsum("red,efd->ref", d_rows, w_down, preferred_element_type=jnp.float32)
    grad_down = jnp.einsum("ref,red->efd", active, d_rows, preferred_element_type=jnp.float32)
    gelu_back = jax.vjp(gelu_tanh, hidden)[1]
    d_hidden = gelu_back(d_active)[0].astype(jnp.bfloat16)
    grad_up = jnp.einsum("red,ref->edf", slot_rows, d_hidden, preferred_element_type=jnp.float32)
    d_slot_part = jnp.einsum("ref,edf->red", d_hidden, w_up, preferred_element_type=jnp.float32)
    d_slot_rows = lax.psum(d_slot_part.astype(jnp.bfloat16), "seq")
    d_slots = lax.all_to_all(d_slot_rows, "dp", split_axis=0, concat_axis=1, tiled=True)
    d_slots_wide = d_slots.astype(jnp.float32)
    coefficient = factor / denominator
    inner_dot = jnp.sum(slot_vals * d_slots_wide, axis=-1)
    projected = jnp.einsum(
        "btd,bed->bte", normed_two_low, d_slots, preferred_element_type=jnp.float32
    )
    d_logits = coefficient[:, None, :] * (projected - inner_dot[:, None, :]) * dispatch
    d_logits = d_logits + combine * (
        d_combine - jnp.sum(combine * d_combine, axis=-1, keepdims=True)
    )
    d_logits_low = d_logits.astype(jnp.bfloat16)
    scaled_slots = coefficient[:, :, None] * d_slots_wide
    dispatch_low = lax.optimization_barrier(dispatch.astype(jnp.bfloat16)).astype(jnp.float32)
    d_normed_two = jnp.einsum(
        "bte,bed->btd", dispatch_low, scaled_slots, precision=lax.Precision.HIGHEST
    )
    d_normed_two = d_normed_two + jnp.einsum(
        "bte,de->btd", d_logits_low, router, preferred_element_type=jnp.float32
    )
    grad_router = jnp.einsum(
        "btd,bte->de", normed_two_low, d_logits_low, preferred_element_type=jnp.float32
    )
    d_mid_norm, grad_gain_two, grad_shift_two = layer_norm_back(
        d_normed_two, unit_two, inverse_two, gain_two.astype(jnp.float32)
    )
    d_middle = cot_part.astype(jnp.float32) + d_mid_norm
    d_branch = d_middle.astype(jnp.bfloat16)
    grad_out_w = jnp.einsum("btd,bte->de", attn_tok, d_branch, preferred_element_type=jnp.float32)
    d_attn_tok = jnp.einsum(
        "bte,de->btd", d_branch, w_out, preferred_element_type=jnp.float32
    ).astype(jnp.bfloat16)
    d_heads = lax.all_to_all(
        d_attn_tok.reshape(images, block_len, groups, per_head),
        "seq",
        split_axis=2,
        concat_axis=1,
        tiled=True,
    )
    d_attended = d_heads.reshape(images, length_all, heads_dev, HD)
    attn_probs = jnp.exp(attention_scores(queries, keys_all, key_valid) - log_total)
    d_values = jnp.einsum(
        "bhqk,bqhd->bkhd",
        attn_probs.astype(jnp.bfloat16),
        d_attended,
        preferred_element_type=jnp.float32,
    )
    d_probs = jnp.einsum(
        "bqhd,bkhd->bhqk", d_attended, values_all, preferred_element_type=jnp.float32
    )
    d_scores = attn_probs * (d_probs - jnp.sum(attn_probs * d_probs, axis=-1, keepdims=True))
    d_scores = d_scores.astype(jnp.bfloat16)
    d_queries = (
        jnp.einsum("bhqk,bkhd->bqhd", d_scores, keys_all, preferred_element_type=jnp.float32)
        * score_scale
    )
    d_keys = (
        jnp.einsum("bhqk,bqhd->bkhd", d_scores, queries, preferred_element_type=jnp.float32)
        * score_scale
    )
    stacked = jnp.stack([d_queries, d_keys, d_values], axis=2).astype(jnp.bfloat16)
    stacked = stacked.reshape(images, length_all, 3, 1, per_head)
    d_mixed = lax.all_to_all(stacked, "seq", split_axis=1, concat_axis=3, tiled=True).reshape(
        images, block_len, 3 * model_width
    )
    grad_qkv = jnp.einsum("btd,bte->de", normed_low, d_mixed, preferred_element_type=jnp.float32)
    d_normed_one = jnp.einsum("bte,de->btd", d_mixed, w_qkv, preferred_element_type=jnp.float32)
    d_in_norm, grad_gain_one, grad_shift_one = layer_norm_back(
        d_normed_one, unit_one, inverse_one, gain_one.astype(jnp.float32)
    )
    grad_input = d_middle + d_in_norm
    local_grads = (
        grad_qkv,
        grad_out_w,
        grad_router,
        grad_gain_one,
        grad_shift_one,
        grad_gain_two,
        grad_shift_two,
    )
    return (grad_input, local_grads, grad_up, grad_down)


def local(
    tokens,
    lengths,
    w_qkv,
    w_out,
    router,
    gain_one,
    shift_one,
    gain_two,
    shift_two,
    w_up,
    w_down,
    cotangent,
):
    per_batch = tokens.shape[0] // MB
    block_outs = []
    input_grads = []
    share_sums = None
    up_sum = jnp.zeros(w_up.shape, jnp.float32)
    down_sum = jnp.zeros(w_down.shape, jnp.float32)
    for batch_index in range(MB):
        first_row = batch_index * per_batch
        tokens_part = tokens[first_row : first_row + per_batch]
        lengths_part = lengths[first_row : first_row + per_batch]
        cot_part = cotangent[first_row : first_row + per_batch]
        params = gather_params(w_qkv, w_out, router, gain_one, shift_one, gain_two, shift_two)
        result, kept_state = forward_batch(tokens_part, lengths_part, params, w_up, w_down)
        params_back = gather_params(w_qkv, w_out, router, gain_one, shift_one, gain_two, shift_two)
        grad_input, local_grads, grad_up, grad_down = backward_batch(
            cot_part, params_back, w_up, w_down, kept_state
        )
        shares = (
            lax.psum_scatter(local_grads[0], ("dp", "seq"), scatter_dimension=0, tiled=True),
            lax.psum_scatter(local_grads[1], ("dp", "seq"), scatter_dimension=0, tiled=True),
            lax.psum_scatter(local_grads[2], ("dp", "seq"), scatter_dimension=0, tiled=True),
            lax.psum_scatter(local_grads[3], ("dp", "seq"), scatter_dimension=0, tiled=True),
            lax.psum_scatter(local_grads[4], ("dp", "seq"), scatter_dimension=0, tiled=True),
            lax.psum_scatter(local_grads[5], ("dp", "seq"), scatter_dimension=0, tiled=True),
            lax.psum_scatter(local_grads[6], ("dp", "seq"), scatter_dimension=0, tiled=True),
        )
        block_outs.append(result)
        input_grads.append(grad_input)
        share_sums = shares if share_sums is None else jax.tree.map(jnp.add, share_sums, shares)
        up_sum = up_sum + grad_up
        down_sum = down_sum + grad_down
    return (
        jnp.concatenate(block_outs, axis=0),
        jnp.concatenate(input_grads, axis=0),
        share_sums[0],
        share_sums[1],
        share_sums[2],
        share_sums[3],
        share_sums[4],
        share_sums[5],
        share_sums[6],
        up_sum,
        down_sum,
    )


def solution(mesh):
    return jax.shard_map(
        local,
        mesh=mesh,
        in_specs=(
            P("dp", "seq", None),
            P("dp"),
            P(("dp", "seq"), None),
            P(("dp", "seq"), None),
            P(("dp", "seq"), None),
            P(("dp", "seq")),
            P(("dp", "seq")),
            P(("dp", "seq")),
            P(("dp", "seq")),
            P("dp", None, "seq"),
            P("dp", "seq", None),
            P("dp", "seq", None),
        ),
        out_specs=(
            P("dp", "seq", None),
            P("dp", "seq", None),
            P(("dp", "seq"), None),
            P(("dp", "seq"), None),
            P(("dp", "seq"), None),
            P(("dp", "seq")),
            P(("dp", "seq")),
            P(("dp", "seq")),
            P(("dp", "seq")),
            P("dp", None, "seq"),
            P("dp", "seq", None),
        ),
        check_vma=False,
    )
```

profile of v0, /device:TPU:0, one launch (start us, length us, event | category | flops | bytes accessed | tf_op | source)
XLA Modules:
  0.0 818.2 jit_solution(4062475512826185900)
XLA Ops:
  11.3 42.2 %all-reduce.10 = (bf16[768]{0:T(1024)(128)(2,1)S(1)}, bf16[768]{0:T(1024)(128)(2,1)S(1)}, bf16[768]{0:T(1024)(128)(2,1)S(1)}, bf16[768]{0:T(1024)(128)(2,1)S(1)}) all-reduce(bf16[768]{0:T(1024)(128)(2,1)S(1)} %dynamic-update-slice.1, bf16[768]{0:T(1024)(128)(2,1)S(1)} %dynamic-update-slice, ...), channel_id=1, replica_groups=mesh['dp'=8,'seq'=4] {'dp','seq'}, use_global_device_ids=true, to_apply=%add.1 | all-reduce | flops 3072 | bytes 12288
  56.9 16.9 %all-gather.14.cloned.1.call-done = bf16[768,2304]{1,0:T(8,128)(2,1)} async-done(((bf16[24,2304]{1,0:T(8,128)(2,1)}), bf16[768,2304]{1,0:T(8,128)(2,1)}) %all-gather.14.cloned.1.call-update) | async-done | bytes 3538960 | tf_op jit(solution)/shard_map/all_gather | solution.py:60
  73.8 4.3 convolution_convert_fusion
  78.1 3.5 reshape.522
  83.0 3.7 all-to-all-start.4
  88.1 94.7 %all-gather.6 = bf16[32,24,8]{1,2,0:T(8,128)(2,1)S(1)} all-gather(bf16[1,24,8]{1,2,0:T(8,128)(2,1)S(1)} %bitcast.446), channel_id=1, replica_groups=mesh['dp'=8,'seq'=4] {'dp','seq'}, dimensions={0}, use_global_device_ids=true | all-gather | bytes 12672 | tf_op jit(solution)/shard_map/all_gather | solution.py:62
  186.2 4.2 convolution_convert_fusion.1
  190.4 4.4 reshape.516
  197.6 4.3 all-to-all-start
  210.9 23.7 %all-to-all-done = bf16[4,64,3,4,192]{4,1,2,0,3:T(8,128)(2,1)} async-done(((bf16[4,64,3,4,192]{4,1,2,0,3:T(8,128)(2,1)}), bf16[4,64,3,4,192]{4,1,2,0,3:T(8,128)(2,1)}, u32[]{:S(2)}, u32[]{:S(2)}) %all-to-all-start) | async-done | bytes 1179680 | tf_op jit(solution)/shard_map/all_to_all | solution.py:97
  234.6 4.4 all-to-all-start.5
  252.5 4.8 all-to-all-start.1
  261.9 8.3 %all-to-all-done.1 = bf16[4,256,192]{2,0,1:T(4,128)(2,1)S(1)} async-done(((bf16[4,256,192]{2,0,1:T(4,128)(2,1)}), bf16[4,256,192]{2,0,1:T(4,128)(2,1)S(1)}, u32[]{:S(2)}, u32[]{:S(2)}) %all-to-all-start.1) | async-done | bytes 393248 | tf_op jit(solution)/shard_map/all_to_all | solution.py:114
  277.3 9.0 %all-gather.9 = bf16[4,4,8]{2,1,0:T(4,128)(2,1)S(1)} all-gather(bf16[1,4,8]{2,1,0:T(4,128)(2,1)S(1)} %get-tuple-element.469), channel_id=5, replica_groups=mesh['dp'=8,'seq'=4] {'seq'}, dimensions={0}, use_global_device_ids=true | all-gather | bytes 320 | tf_op jit(solution)/shard_map/all_gather | solution.py:13
  288.2 8.1 all-gather.10
  296.5 13.6 %all-gather.5 = bf16[16,8,768]{2,1,0:T(8,128)(2,1)S(1)} all-gather(bf16[4,8,768]{2,1,0:T(8,128)(2,1)S(1)} %convolution_convert_fusion.6), channel_id=7, replica_groups=mesh['dp'=8,'seq'=4] {'seq'}, dimensions={0}, use_global_device_ids=true | all-gather | bytes 245760 | tf_op jit(solution)/shard_map/all_gather | solution.py:13
  310.8 8.6 %while.39 = (s32[]{:T(128)}, f32[4,8]{1,0:T(4,128)}, f32[4,8]{1,0:T(4,128)S(1)}, f32[4,8,768]{2,1,0:T(8,128)}, bf16[4,4,8]{2,1,0:T(4,128)(2,1)}, /*index=5*/bf16...) while((s32[]{:T(128)}, f32[4,8]{1,0:T(4,128)}, ...), condition=%wide.region_24.25_spmd, body=%wide.region_23.24_spmd.sunk | while | flops 98565 | bytes 247063 | solution.py:21
  321.0 4.5 all-to-all-start.6
  327.4 9.0 %all-gather.7 = bf16[4,4,8]{2,1,0:T(4,128)(2,1)S(1)} all-gather(bf16[1,4,8]{2,1,0:T(4,128)(2,1)S(1)} %get-tuple-element.467), channel_id=2, replica_groups=mesh['dp'=8,'seq'=4] {'seq'}, dimensions={0}, use_global_device_ids=true | all-gather | bytes 320 | tf_op jit(solution)/shard_map/all_gather | solution.py:13
  337.8 8.1 all-gather.8
  347.7 13.6 %all-gather.2 = bf16[16,8,768]{2,1,0:T(8,128)(2,1)S(1)} all-gather(bf16[4,8,768]{2,1,0:T(8,128)(2,1)S(1)} %convolution_convert_fusion.7), channel_id=4, replica_groups=mesh['dp'=8,'seq'=4] {'seq'}, dimensions={0}, use_global_device_ids=true | all-gather | bytes 245760 | tf_op jit(solution)/shard_map/all_gather | solution.py:13
  362.0 8.8 %while.38 = (s32[]{:T(128)}, f32[4,8]{1,0:T(4,128)}, f32[4,8]{1,0:T(4,128)}, f32[4,8,768]{2,1,0:T(8,128)}, bf16[4,4,8]{2,1,0:T(4,128)(2,1)}, /*index=5*/bf16[4,4...) while((s32[]{:T(128)}, f32[4,8]{1,0:T(4,128)}, f32[4,8]{1,0:T(4,128)}, ...), condition=%wide.region_11.12_spmd, body=%wide.region_10.11_spmd.sunk | while | flops 98565 | bytes 247063 | solution.py:21
  377.6 4.2 all-to-all-start.2
  392.6 27.7 %all-reduce.18.cloned.1.call-done = (bf16[4,8,768]{2,1,0:T(8,128)(2,1)}, bf16[4,8,768]{2,1,0:T(8,128)(2,1)}) async-done(((bf16[4,8,768]{2,1,0:T(8,128)(2,1)}, bf16[4,8,768]{2,1,0:T(8,128)(2,1)}), (bf16[4,8,768]{2,1,0:T(8,128)(2,1)}, bf16[4,8,768]{2,1,0:T(8,128)(2,1)})) %all-reduce.18.cloned.1.call-update) | async-done | bytes 98320 | tf_op jit(solution)/shard_map/psum | solution.py:212
  421.7 4.0 all-to-all-start.12
  430.6 4.0 all-to-all-start.8
  447.1 34.7 %all-reduce.16.cloned.1.call-done = (bf16[32,1,768]{2,0,1:T(8,128)(2,1)}, bf16[32,1,768]{2,0,1:T(8,128)(2,1)}, bf16[32,1,768]{2,0,1:T(8,128)(2,1)}, bf16[32,1,768]{2,0,1:T(8,128)(2,1)}) async-done(((bf16[32,1,768]{2,0,1:T(8,128)(2,1)}, bf16[32,1,768]{2,0,1:T(8,128)(2,1)}, bf16[32,1,768]{2,0,1:T(8,128)(2,1)}, bf16[32,1,768]{2,0,1:T(8,128)(2,1)}), (bf16[32,1,768]{2,0,1:T(8,128)(2,1)}, ...) | async-done | bytes 196624 | tf_op jit(solution)/shard_map/psum | solution.py:141
  484.5 3.7 all-to-all-start.13
  496.4 4.2 all-to-all-start.7
  505.5 3.9 all-to-all-start.3
  514.3 3.3 all-to-all-start.9
  528.9 3.6 multiply_reduce_fusion.3
  532.6 3.2 multiply_add_fusion.1
  542.2 4.1 all-to-all-start.14
  556.9 4.1 all-to-all-done.14
  561.0 4.3 all-to-all-start.10
  567.3 3.4 fusion.33
  582.8 3.5 pad_maximum_fusion.1
  586.4 5.2 all-to-all-start.15
  606.7 3.4 pad_maximum_fusion
  610.1 23.9 %all-to-all-done.15 = bf16[4,256,3,1,192]{4,0,3,2,1:T(4,128)(2,1)} async-done(((bf16[4,256,3,1,192]{4,0,3,2,1:T(4,128)(2,1)}), bf16[4,256,3,1,192]{4,0,3,2,1:T(4,128)(2,1)}, u32[]{:S(2)}, u32[]{:S(2)}) %all-to-all-start.15) | async-done | bytes 1179680 | tf_op jit(solution)/shard_map/all_to_all | solution.py:283
  634.0 4.4 all-to-all-start.11
  645.7 32.5 %all-to-all-done.11 = bf16[4,256,3,1,192]{4,0,3,2,1:T(4,128)(2,1)} async-done(((bf16[4,256,3,1,192]{4,0,3,2,1:T(4,128)(2,1)}), bf16[4,256,3,1,192]{4,0,3,2,1:T(4,128)(2,1)}, u32[]{:S(2)}, u32[]{:S(2)}) %all-to-all-start.11) | async-done | bytes 1179680 | tf_op jit(solution)/shard_map/all_to_all | solution.py:283
  682.3 4.0 reshape.530
  688.9 4.2 bitcast_add_fusion
  706.7 3.4 fusion.10
  712.7 37.7 %all-reduce.9 = (f32[768,8]{0,1:T(8,128)S(1)}, f32[768]{0:T(1024)S(1)}, f32[768]{0:T(1024)S(1)}, f32[768]{0:T(1024)S(1)}, f32[768]{0:T(1024)S(1)}) all-reduce(f32[768,8]{0,1:T(8,128)S(1)} %copy-done.76, f32[768]{0:T(1024)S(1)} %add.369, f32[768]{0:T(1024)S(1)} %add.370, ...), channel_id=17, replica_groups=mesh['dp'=8,'seq'=4] {'dp','seq'}, use_global_device_ids=true, to_apply=%region_48.49.clone | all-reduce | flops 9216 | bytes 73728
  756.7 54.2 %reduce-scatter.4.cloned.1.call-done = f32[24,2304]{1,0:T(8,128)} async-done(((f32[768,2304]{1,0:T(8,128)}), f32[24,2304]{1,0:T(8,128)}) %reduce-scatter.4.cloned.1.call-update) | async-done | bytes 221200 | tf_op jit(solution)/shard_map/reduce_scatter | solution.py:336
  (497 shorter events, 228.0 us)
Async XLA Ops:
  7.2 383.5 %copy-start = (bf16[1,768,768]{2,1,0:T(8,128)(2,1)S(1)}, bf16[1,768,768]{2,1,0:T(8,128)(2,1)}, u32[]{:S(2)}) copy-start(bf16[1,768,768]{2,1,0:T(8,128)(2,1)} %param.26) | copy-start | bytes 3538948
  7.2 66.6 %all-gather.14.cloned.1.call-start = ((), (), s32[]{:S(2)}) async-start(), calls=%async_computation.18 | async-start | bytes 3649536 | tf_op jit(solution)/shard_map/all_gather | solution.py:60
  53.5 20.3 %copy-start.119 = (f32[768]{0:T(1024)}, f32[768]{0:T(1024)S(1)}, u32[]{:S(2)}) copy-start(f32[768]{0:T(1024)S(1)} %convert_element_type.388) | copy-start | bytes 9220
  53.5 20.3 %copy-start.89 = (f32[768]{0:T(1024)}, f32[768]{0:T(1024)S(1)}, u32[]{:S(2)}) copy-start(f32[768]{0:T(1024)S(1)} %convert_element_type.387) | copy-start | bytes 9220
  54.8 18.9 %copy-start.97 = (f32[4,64]{1,0:T(4,128)}, f32[4,64]{1,0:T(4,128)S(1)}, u32[]{:S(2)}) copy-start(f32[4,64]{1,0:T(4,128)S(1)} %get-tuple-element.496) | copy-start | bytes 3076
  56.9 16.9 %copy-start.104 = (f32[4,64]{1,0:T(4,128)}, f32[4,64]{1,0:T(4,128)S(1)}, u32[]{:S(2)}) copy-start(f32[4,64]{1,0:T(4,128)S(1)} %add_rsqrt_fusion.1) | copy-start | bytes 3076
  83.0 103.2 %copy-start.9 = (bf16[8,64,768]{2,1,0:T(8,128)(2,1)S(1)}, bf16[8,64,768]{2,1,0:T(8,128)(2,1)}, u32[]{:S(2)}) copy-start(bf16[8,64,768]{2,1,0:T(8,128)(2,1)} %param.16) | copy-start | bytes 2359300
  83.0 114.6 %all-to-all-start.4 = ((bf16[4,64,3,4,192]{4,1,2,0,3:T(8,128)(2,1)}), bf16[4,64,3,4,192]{4,1,2,0,3:T(8,128)(2,1)S(1)}, u32[]{:S(2)}, u32[]{:S(2)}) async-start(bf16[4,64,3,4,192]{4,1,2,0,3:T(8,128)(2,1)} %copy.192), calls=%async_computation.4 | async-start | bytes 3145728 | tf_op jit(solution)/shard_map/all_to_all | solution.py:97
  86.7 184.4 %all-gather.16.cloned.1.call-start = ((), (), s32[]{:S(2)}) async-start(), calls=%async_computation.19 | async-start | bytes 1216512 | tf_op jit(solution)/shard_map/all_gather | solution.py:61
  88.1 187.2 %copy-start.80 = (f32[768]{0:T(1024)}, f32[768]{0:T(1024)S(1)}, u32[]{:S(2)}) copy-start(f32[768]{0:T(1024)S(1)} %convert_element_type.394) | copy-start | bytes 9220
  197.6 37.0 %all-to-all-start = ((bf16[4,64,3,4,192]{4,1,2,0,3:T(8,128)(2,1)}), bf16[4,64,3,4,192]{4,1,2,0,3:T(8,128)(2,1)}, u32[]{:S(2)}, u32[]{:S(2)}) async-start(bf16[4,64,3,4,192]{4,1,2,0,3:T(8,128)(2,1)} %copy.179), calls=%async_computation | async-start | bytes 3145728 | tf_op jit(solution)/shard_map/all_to_all | solution.py:97
  234.6 17.9 %all-to-all-start.5 = ((bf16[4,256,192]{2,0,1:T(4,128)(2,1)}), bf16[4,256,192]{2,0,1:T(4,128)(2,1)}, u32[]{:S(2)}, u32[]{:S(2)}) async-start(bf16[4,256,192]{2,0,1:T(4,128)(2,1)} %copy.198), calls=%async_computation.5 | async-start | bytes 1048576 | tf_op jit(solution)/shard_map/all_to_all | solution.py:114
  252.5 17.6 %all-to-all-start.1 = ((bf16[4,256,192]{2,0,1:T(4,128)(2,1)}), bf16[4,256,192]{2,0,1:T(4,128)(2,1)S(1)}, u32[]{:S(2)}, u32[]{:S(2)}) async-start(bf16[4,256,192]{2,0,1:T(4,128)(2,1)} %copy.185), calls=%async_computation.1 | async-start | bytes 1048576 | tf_op jit(solution)/shard_map/all_to_all | solution.py:114
  275.0 35.8 %copy-start.87 = (f32[4,64]{1,0:T(4,128)}, f32[4,64]{1,0:T(4,128)S(1)}, u32[]{:S(2)}) copy-start(f32[4,64]{1,0:T(4,128)S(1)} %broadcast_multiply_fusion.8) | copy-start | bytes 3076
  275.3 35.5 %copy-start.94 = (f32[4,64]{1,0:T(4,128)}, f32[4,64]{1,0:T(4,128)S(1)}, u32[]{:S(2)}) copy-start(f32[4,64]{1,0:T(4,128)S(1)} %add_rsqrt_fusion) | copy-start | bytes 3076
  276.4 20.0 %copy-start.16 = (bf16[4,64,768]{2,1,0:T(8,128)(2,1)}, bf16[4,64,768]{2,1,0:T(8,128)(2,1)S(1)}, u32[]{:S(2)}) copy-start(bf16[4,64,768]{2,1,0:T(8,128)(2,1)S(1)} %get-tuple-element.461) | copy-start | bytes 1179652
  276.7 19.6 %copy-start.62 = (f32[4,64,8]{1,2,0:T(8,128)}, f32[4,64,8]{1,2,0:T(8,128)S(1)}, u32[]{:S(2)}) copy-start(f32[4,64,8]{1,2,0:T(8,128)S(1)} %get-tuple-element.483) | copy-start | bytes 24580
  286.3 24.5 %copy-start.100 = (bf16[4,4,8]{2,1,0:T(4,128)(2,1)}, bf16[4,4,8]{2,1,0:T(4,128)(2,1)S(1)}, u32[]{:S(2)}) copy-start(bf16[4,4,8]{2,1,0:T(4,128)(2,1)S(1)} %all-gather.9) | copy-start | bytes 772
  321.0 56.6 %all-to-all-start.6 = ((bf16[4,8,768]{2,0,1:T(4,128)(2,1)}), bf16[4,8,768]{2,0,1:T(4,128)(2,1)}, u32[]{:S(2)}, u32[]{:S(2)}) async-start(bf16[4,8,768]{2,0,1:T(4,128)(2,1)} %copy.201), calls=%async_computation.6 | async-start | bytes 98304 | tf_op jit(solution)/shard_map/all_to_all | solution.py:135
  326.8 19.7 %copy-start.65 = (f32[4,64,8]{1,2,0:T(8,128)}, f32[4,64,8]{1,2,0:T(8,128)S(1)}, u32[]{:S(2)}) copy-start(f32[4,64,8]{1,2,0:T(8,128)S(1)} %get-tuple-element.485) | copy-start | bytes 24580
  377.6 9.3 %all-to-all-start.2 = ((bf16[4,8,768]{2,0,1:T(4,128)(2,1)}), bf16[4,8,768]{2,0,1:T(4,128)(2,1)}, u32[]{:S(2)}, u32[]{:S(2)}) async-start(bf16[4,8,768]{2,0,1:T(4,128)(2,1)} %copy.189), calls=%async_computation.2 | async-start | bytes 98304 | tf_op jit(solution)/shard_map/all_to_all | solution.py:135
  381.8 38.5 %all-reduce.18.cloned.1.call-start = ((), (), s32[]{:S(2)}) async-start(), calls=%async_computation.23 | async-start | bytes 196608 | tf_op jit(solution)/shard_map/psum | solution.py:212
  421.7 8.9 %all-to-all-start.12 = ((bf16[4,8,768]{2,0,1:T(4,128)(2,1)}), bf16[4,8,768]{2,0,1:T(4,128)(2,1)}, u32[]{:S(2)}, u32[]{:S(2)}) async-start(bf16[4,8,768]{2,0,1:T(4,128)(2,1)} %copy.217), calls=%async_computation.12 | async-start | bytes 98304 | tf_op jit(solution)/shard_map/all_to_all | solution.py:213
  430.6 9.9 %all-to-all-start.8 = ((bf16[4,8,768]{2,0,1:T(4,128)(2,1)}), bf16[4,8,768]{2,0,1:T(4,128)(2,1)}, u32[]{:S(2)}, u32[]{:S(2)}) async-start(bf16[4,8,768]{2,0,1:T(4,128)(2,1)} %copy.204), calls=%async_computation.8 | async-start | bytes 98304 | tf_op jit(solution)/shard_map/all_to_all | solution.py:213
  434.6 47.2 %all-reduce.16.cloned.1.call-start = ((), (), s32[]{:S(2)}) async-start(), calls=%async_computation.22 | async-start | bytes 393216 | tf_op jit(solution)/shard_map/psum | solution.py:141
  444.0 59.2 %copy-start.78 = (bf16[4,64,8]{1,2,0:T(8,128)(2,1)S(1)}, bf16[4,64,8]{1,2,0:T(8,128)(2,1)}, u32[]{:S(2)}) copy-start(bf16[4,64,8]{1,2,0:T(8,128)(2,1)} %copy-done.77) | copy-start | bytes 12292
  444.0 60.7 %copy-start.21 = (f32[4,8,768]{2,1,0:T(8,128)S(1)}, f32[4,8,768]{2,1,0:T(8,128)}, u32[]{:S(2)}) copy-start(f32[4,8,768]{2,1,0:T(8,128)} %get-tuple-element.369) | copy-start | bytes 294916
  444.0 65.5 %copy-start.17 = (bf16[4,64,768]{2,1,0:T(8,128)(2,1)S(1)}, bf16[4,64,768]{2,1,0:T(8,128)(2,1)}, u32[]{:S(2)}) copy-start(bf16[4,64,768]{2,1,0:T(8,128)(2,1)} %copy-done.16) | copy-start | bytes 1179652
  444.0 65.5 %copy-start.63 = (f32[4,64,8]{1,2,0:T(8,128)S(1)}, f32[4,64,8]{1,2,0:T(8,128)}, u32[]{:S(2)}) copy-start(f32[4,64,8]{1,2,0:T(8,128)} %copy-done.62) | copy-start | bytes 24580
  482.4 40.5 %copy-start.22 = (f32[4,8,768]{2,1,0:T(8,128)S(1)}, f32[4,8,768]{2,1,0:T(8,128)}, u32[]{:S(2)}) copy-start(f32[4,8,768]{2,1,0:T(8,128)} %get-tuple-element.367) | copy-start | bytes 294916
  482.4 40.5 %copy-start.70 = (f32[4,8]{1,0:T(4,128)S(1)}, f32[4,8]{1,0:T(4,128)}, u32[]{:S(2)}) copy-start(f32[4,8]{1,0:T(4,128)} %get-tuple-element.368) | copy-start | bytes 388
  484.5 11.3 %all-to-all-start.13 = ((bf16[8,2,1536]{2,1,0:T(2,128)(2,1)}), bf16[8,2,1536]{2,1,0:T(2,128)(2,1)S(1)}, u32[]{:S(2)}, u32[]{:S(2)}) async-start(bf16[8,2,1536]{2,1,0:T(2,128)(2,1)} %reshape.622), calls=%async_computation.13 | async-start | bytes 98304 | tf_op jit(solution)/shard_map/all_to_all | solution.py:221
  496.4 9.1 %all-to-all-start.7 = ((bf16[8,2,1536]{2,1,0:T(2,128)(2,1)}), bf16[8,2,1536]{2,1,0:T(2,128)(2,1)S(1)}, u32[]{:S(2)}, u32[]{:S(2)}) async-start(bf16[8,2,1536]{2,1,0:T(2,128)(2,1)} %reshape.618), calls=%async_computation.7 | async-start | bytes 98304 | tf_op jit(solution)/shard_map/all_to_all | solution.py:142
  500.6 24.6 %copy-start.19 = (bf16[4,64,768]{2,1,0:T(8,128)(2,1)S(1)}, bf16[4,64,768]{2,1,0:T(8,128)(2,1)}, u32[]{:S(2)}) copy-start(bf16[4,64,768]{2,1,0:T(8,128)(2,1)} %get-tuple-element.460) | copy-start | bytes 1179652
  500.6 24.6 %copy-start.66 = (f32[4,64,8]{1,2,0:T(8,128)S(1)}, f32[4,64,8]{1,2,0:T(8,128)}, u32[]{:S(2)}) copy-start(f32[4,64,8]{1,2,0:T(8,128)} %copy-done.65) | copy-start | bytes 24580
  505.5 8.8 %all-to-all-start.3 = ((bf16[8,2,1536]{2,1,0:T(2,128)(2,1)}), bf16[8,2,1536]{2,1,0:T(2,128)(2,1)S(1)}, u32[]{:S(2)}, u32[]{:S(2)}) async-start(bf16[8,2,1536]{2,1,0:T(2,128)(2,1)} %reshape.620), calls=%async_computation.3 | async-start | bytes 98304 | tf_op jit(solution)/shard_map/all_to_all | solution.py:142
  511.3 17.6 %copy-start.53 = (bf16[8,4,1,768]{3,1,0,2:T(4,128)(2,1)}, bf16[8,4,1,768]{3,1,0,2:T(4,128)(2,1)S(1)}, u32[]{:S(2)}) copy-start(bf16[8,4,1,768]{3,1,0,2:T(4,128)(2,1)S(1)} %all_to_all.219) | copy-start | bytes 147460
  514.3 8.2 %all-to-all-start.9 = ((bf16[8,2,1536]{2,1,0:T(2,128)(2,1)}), bf16[8,2,1536]{2,1,0:T(2,128)(2,1)S(1)}, u32[]{:S(2)}, u32[]{:S(2)}) async-start(bf16[8,2,1536]{2,1,0:T(2,128)(2,1)} %reshape.624), calls=%async_computation.9 | async-start | bytes 98304 | tf_op jit(solution)/shard_map/all_to_all | solution.py:221
  542.2 18.8 %all-to-all-start.14 = ((bf16[4,64,4,192]{3,1,0,2:T(8,128)(2,1)}), bf16[4,64,4,192]{3,1,0,2:T(8,128)(2,1)}, u32[]{:S(2)}, u32[]{:S(2)}) async-start(bf16[4,64,4,192]{3,1,0,2:T(8,128)(2,1)} %copy.220), calls=%async_computation.14 | async-start | bytes 1048576 | tf_op jit(solution)/shard_map/all_to_all | solution.py:253
  546.3 210.4 %reduce-scatter.6.cloned.1.call-start = ((), (), s32[]{:S(2)}) async-start(), calls=%async_computation.21 | async-start | bytes 2433024 | tf_op jit(solution)/shard_map/reduce_scatter | solution.py:337
  561.0 25.4 %all-to-all-start.10 = ((bf16[4,64,4,192]{3,1,0,2:T(8,128)(2,1)}), bf16[4,64,4,192]{3,1,0,2:T(8,128)(2,1)}, u32[]{:S(2)}, u32[]{:S(2)}) async-start(bf16[4,64,4,192]{3,1,0,2:T(8,128)(2,1)} %copy.207), calls=%async_computation.10 | async-start | bytes 1048576 | tf_op jit(solution)/shard_map/all_to_all | solution.py:253
  586.4 47.6 %all-to-all-start.15 = ((bf16[4,256,3,1,192]{4,0,3,2,1:T(4,128)(2,1)}), bf16[4,256,3,1,192]{4,0,3,2,1:T(4,128)(2,1)}, u32[]{:S(2)}, u32[]{:S(2)}) async-start(bf16[4,256,3,1,192]{4,0,3,2,1:T(4,128)(2,1)} %pad_maximum_fusion.1), calls=%async_computation.15 | async-start | bytes 3145728 | tf_op jit(solution)/shard_map/all_to_all | solution.py:283
  634.0 44.3 %all-to-all-start.11 = ((bf16[4,256,3,1,192]{4,0,3,2,1:T(4,128)(2,1)}), bf16[4,256,3,1,192]{4,0,3,2,1:T(4,128)(2,1)}, u32[]{:S(2)}, u32[]{:S(2)}) async-start(bf16[4,256,3,1,192]{4,0,3,2,1:T(4,128)(2,1)} %pad_maximum_fusion), calls=%async_computation.11 | async-start | bytes 3145728 | tf_op jit(solution)/shard_map/all_to_all | solution.py:283
  638.3 172.7 %reduce-scatter.4.cloned.1.call-start = ((), (), s32[]{:S(2)}) async-start(), calls=%async_computation.20 | async-start | bytes 7299072 | tf_op jit(solution)/shard_map/reduce_scatter | solution.py:336
  645.7 43.1 %copy-start.23 = (bf16[4,64,2304]{2,1,0:T(8,128)(2,1)}, bf16[4,64,2304]{2,1,0:T(8,128)(2,1)S(1)}, u32[]{:S(2)}) copy-start(bf16[4,64,2304]{2,1,0:T(8,128)(2,1)S(1)} %reshape.535) | copy-start | bytes 3538948
  710.4 43.0 %copy-start.11 = (f32[4,64,768]{2,1,0:T(8,128)S(1)}, f32[4,64,768]{2,1,0:T(8,128)}, u32[]{:S(2)}) copy-start(f32[4,64,768]{2,1,0:T(8,128)} %get-tuple-element.454) | copy-start | bytes 2359300
  710.4 43.0 %copy-start.14 = (f32[4,64,768]{2,1,0:T(8,128)S(1)}, f32[4,64,768]{2,1,0:T(8,128)}, u32[]{:S(2)}) copy-start(f32[4,64,768]{2,1,0:T(8,128)} %copy-done.12) | copy-start | bytes 2359300
  753.4 57.6 %copy-start.1 = (bf16[1,768,768]{2,1,0:T(8,128)(2,1)S(1)}, bf16[1,768,768]{2,1,0:T(8,128)(2,1)}, u32[]{:S(2)}) copy-start(bf16[1,768,768]{2,1,0:T(8,128)(2,1)} %param.26) | copy-start | bytes 3538948
  (109 other events, 439.3 us)
Sparse Core Ops, SparseCore 0:
  10.8 62.8 all-gather.13
  90.4 64.2 all-gather.15
  386.2 34.0 all-reduce.17
  446.6 35.2 all-reduce.15
  557.0 122.6 reduce-scatter.5
  693.2 117.7 reduce-scatter.3
where the time goes:
time: 831 us; the launch traced here: 818 us
  waiting for transfers between devices  237 us (29%)
  blocking collectives  236 us (28%)
  local copies, waits for them, and re-layouts  102 us (12%)
  matrix products  94 us (11%)
  starting transfers between devices  67.4 us (8%)
  other arithmetic  65.2 us (8%)
  between operations  16.2 us (2%)
    all_gather x1, blocking collectives, gather_params(): lax.all_gather(router, ('dp', 'seq'), axis=0, tiled=True)  94.7 us
    unnamed x2, blocking collectives  79.8 us
    all_gather x6, blocking collectives, combined_all(): lax.all_gather(part.astype(kind), axis)  61.4 us
    all_to_all x2, waiting for transfers between devices, backward_batch(): lax.all_to_all(stacked, 'seq', split_axis=1, concat_axis=3, tiled=True)  56.4 us
    reduce_scatter x1, waiting for transfers between devices, local(): lax.psum_scatter(local_grads[0], ('dp', 'seq'), scatter_dimension=0, tile...  54.2 us
    psum x1, waiting for transfers between devices, forward_batch(): expert_rows = lax.psum(partial_value.astype(jnp.bfloat16), 'seq')  34.7 us
    psum x1, waiting for transfers between devices, backward_batch(): d_expert = lax.psum(slot_part.astype(jnp.bfloat16), 'seq')  27.7 us
    all_to_all x2, waiting for transfers between devices, forward_batch(): lax.all_to_all(mixed_qkv, 'seq', split_axis=3, concat_axis=1, tiled=True)  23.7 us
  transfers between devices with their start and end apart: 22, of which 15 were waited for; matrix products, arithmetic and copies ran while one was open for 23% of the time, Pallas kernels for 0%

commit v1 on v0

v1 whole, which is shorter than its diff:
```python
import jax
import jax.numpy as jnp
from jax import lax
from jax.sharding import PartitionSpec as P

H = 12
HD = 64
BF = jnp.bfloat16
F32 = jnp.float32


def dot(spec, a, b):
    return jnp.einsum(spec, a, b, preferred_element_type=F32)


def unit_norm(values):
    centred = values - jnp.mean(values, axis=-1, keepdims=True)
    inverse = lax.rsqrt(jnp.mean(centred * centred, axis=-1, keepdims=True) + 1e-06)
    return centred * inverse, inverse


def norm_back(grad_rows, unit_rows, inverse, gain):
    scaled = grad_rows * gain
    centred = scaled - jnp.mean(scaled, axis=-1, keepdims=True)
    correction = unit_rows * jnp.mean(scaled * unit_rows, axis=-1, keepdims=True)
    return (
        inverse * (centred - correction),
        jnp.sum(grad_rows * unit_rows, axis=(0, 1)),
        jnp.sum(grad_rows, axis=(0, 1)),
    )


def gelu_tanh(values):
    return jax.nn.gelu(values, approximate=True)


def to_images(array):
    return lax.all_to_all(array, "seq", split_axis=0, concat_axis=1, tiled=True)


def to_blocks(array):
    return lax.all_to_all(array, "seq", split_axis=1, concat_axis=0, tiled=True)


def to_experts(rows):
    rows = lax.all_to_all(rows, "dp", split_axis=1, concat_axis=0, tiled=True)
    return lax.all_gather(rows, "seq", axis=0, tiled=True)


def from_experts(rows):
    rows = lax.psum_scatter(rows, "seq", scatter_dimension=0, tiled=True).astype(BF)
    return lax.all_to_all(rows, "dp", split_axis=0, concat_axis=1, tiled=True)


def plain_plan(
    tokens, lengths, w_qkv, w_out, router, gain_one, shift_one, gain_two, shift_two,
    w_up, w_down, cotangent,
):
    groups = lax.axis_size("seq")
    model_width, slots_all = w_qkv.shape[1] // 3, router.shape[1]
    packed = jnp.concatenate(
        [w_qkv, w_out, router]
        + [vec[:, None] for vec in (gain_one, shift_one, gain_two, shift_two)],
        axis=1,
    )
    packed = lax.all_gather(packed, ("dp", "seq"), axis=0, tiled=True)
    split = 4 * model_width
    w_qkv, w_out = packed[:, : 3 * model_width], packed[:, 3 * model_width : split]
    router = packed[:, split : split + slots_all]
    gain_one, shift_one, gain_two, shift_two = (
        packed[:, split + slots_all + k].astype(F32) for k in range(4)
    )
    x = to_images(tokens).astype(F32)
    cot = to_images(cotangent)
    images, length_all = x.shape[:2]
    lengths_own = lax.dynamic_slice_in_dim(lengths, lax.axis_index("seq") * images, images)
    valid = jnp.arange(length_all, dtype=jnp.int32)[None, :] < lengths_own[:, None]

    unit_one, inverse_one = unit_norm(x)
    normed_one = (unit_one * gain_one + shift_one).astype(BF)
    qkv = dot("btd,de->bte", normed_one, w_qkv).astype(BF).reshape(images, length_all, 3, H, HD)
    queries, keys_all, values_all = qkv[:, :, 0], qkv[:, :, 1], qkv[:, :, 2]
    scores = dot("bqhd,bkhd->bhqk", queries, keys_all) * HD ** (-0.5)
    probs = jax.nn.softmax(jnp.where(valid[:, None, None, :], scores, -1000000000.0), axis=-1)
    probs_low = probs.astype(BF)
    attended = dot("bhqk,bkhd->bqhd", probs_low, values_all).astype(BF)
    attended = attended.reshape(images, length_all, model_width)
    middle = x + dot("btd,de->bte", attended, w_out)
    unit_two, inverse_two = unit_norm(middle)
    normed_two = (unit_two * gain_two + shift_two).astype(BF)
    logits = dot("btd,de->bte", normed_two, router)
    top = jnp.floor(jnp.max(jnp.where(valid[:, :, None], logits, -1000000000.0), axis=1))
    dispatch = jnp.where(valid[:, :, None], jnp.exp(logits - top[:, None, :]), 0.0)
    dispatch_low = dispatch.astype(BF)
    denominator = jnp.sum(dispatch, axis=1)
    slot_vals = dot("bte,btd->bed", dispatch_low, normed_two) / denominator[:, :, None]
    slot_rows = to_experts(slot_vals.astype(BF))
    hidden = dot("red,edf->ref", slot_rows, w_up)
    active = gelu_tanh(hidden).astype(BF)
    expert_out = from_experts(dot("ref,efd->red", active, w_down))
    combine = jax.nn.softmax(logits, axis=-1)
    combine_low = combine.astype(BF)
    block_out = (middle + dot("bte,bed->btd", combine_low, expert_out)).astype(BF)

    d_combine = dot("btd,bed->bte", cot, expert_out)
    d_expert = dot("bte,btd->bed", combine_low, cot).astype(BF)
    d_rows = to_experts(d_expert)
    d_active = dot("red,efd->ref", d_rows, w_down)
    grad_down = dot("ref,red->efd", active, d_rows)
    d_hidden = jax.vjp(gelu_tanh, hidden)[1](d_active)[0].astype(BF)
    grad_up = dot("red,ref->edf", slot_rows, d_hidden)
    d_slots = from_experts(dot("ref,edf->red", d_hidden, w_up))
    d_slots_wide = d_slots.astype(F32)
    inner = jnp.sum(slot_vals * d_slots_wide, axis=-1)
    projected = dot("btd,bed->bte", normed_two, d_slots)
    d_logits = (projected - inner[:, None, :]) / denominator[:, None, :] * dispatch
    d_logits = d_logits + combine * (
        d_combine - jnp.sum(combine * d_combine, axis=-1, keepdims=True)
    )
    d_logits = d_logits.astype(BF)
    scaled = d_slots_wide / denominator[:, :, None]
    scaled_high = scaled.astype(BF)
    scaled_rest = (scaled - scaled_high.astype(F32)).astype(BF)
    d_normed_two = (
        dot("bte,bed->btd", dispatch_low, scaled_high)
        + dot("bte,bed->btd", dispatch_low, scaled_rest)
        + dot("bte,de->btd", d_logits, router)
    )
    grad_router = dot("btd,bte->de", normed_two, d_logits)
    d_norm, grad_gain_two, grad_shift_two = norm_back(d_normed_two, unit_two, inverse_two, gain_two)
    d_middle = cot.astype(F32) + d_norm
    d_branch = d_middle.astype(BF)
    grad_out_w = dot("btd,bte->de", attended, d_branch)
    d_attended = dot("bte,de->btd", d_branch, w_out).astype(BF)
    d_attended = d_attended.reshape(images, length_all, H, HD)
    d_values = dot("bhqk,bqhd->bkhd", probs_low, d_attended)
    d_probs = dot("bqhd,bkhd->bhqk", d_attended, values_all)
    d_scores = probs * (d_probs - jnp.sum(probs * d_probs, axis=-1, keepdims=True))
    d_scores = d_scores.astype(BF)
    d_queries = dot("bhqk,bkhd->bqhd", d_scores, keys_all) * HD ** (-0.5)
    d_keys = dot("bhqk,bqhd->bkhd", d_scores, queries) * HD ** (-0.5)
    d_qkv = jnp.stack([d_queries, d_keys, d_values], axis=2).astype(BF)
    d_qkv = d_qkv.reshape(images, length_all, 3 * model_width)
    grad_qkv = dot("btd,bte->de", normed_one, d_qkv)
    d_normed_one = dot("bte,de->btd", d_qkv, w_qkv)
    d_norm, grad_gain_one, grad_shift_one = norm_back(d_normed_one, unit_one, inverse_one, gain_one)
    grad_input = to_blocks(d_middle + d_norm)

    vectors = (grad_gain_one, grad_shift_one, grad_gain_two, grad_shift_two)
    packed = jnp.concatenate(
        [grad_qkv, grad_out_w, grad_router] + [vec[:, None] for vec in vectors], axis=1
    )
    packed = lax.psum_scatter(packed, ("dp", "seq"), scatter_dimension=0, tiled=True)
    return (
        to_blocks(block_out),
        grad_input,
        packed[:, : 3 * model_width],
        packed[:, 3 * model_width : split],
        packed[:, split : split + slots_all],
        packed[:, split + slots_all],
        packed[:, split + slots_all + 1],
        packed[:, split + slots_all + 2],
        packed[:, split + slots_all + 3],
        grad_up,
        grad_down,
    )


def solution(mesh):
    rows, vector = P(("dp", "seq"), None), P(("dp", "seq"))
    tokens = P("dp", "seq", None)
    up, down = P("dp", None, "seq"), P("dp", "seq", None)
    return jax.shard_map(
        plain_plan,
        mesh=mesh,
        in_specs=(tokens, P("dp"), rows, rows, rows)
        + (vector,) * 4
        + (up, down, tokens),
        out_specs=(tokens, tokens, rows, rows, rows) + (vector,) * 4 + (up, down),
        check_vma=False,
    )
```

time: 831 us -> 539 us (0.65); the launches traced: 818 us -> 537 us
  blocking collectives: 236 us -> 27.8 us
  waiting for transfers between devices: 237 us -> 320 us
  local copies, waits for them, and re-layouts: 102 us -> 53.6 us
  other arithmetic: 65.2 us -> 22.2 us
  starting transfers between devices: 67.4 us -> 33.1 us
  matrix products: 94 us -> 65.4 us
    unnamed x6 -> x5, waiting for transfers between devices: 1.44 us -> 148 us
    all_gather x7 -> x2, blocking collectives: 156 us -> 27.8 us  [to_experts(): return lax.all_gather(rows, 'seq', axis=0, tiled=True)]
    unnamed x2 -> x0, blocking collectives: 79.8 us -> none
    psum x2 -> x0, waiting for transfers between devices: 62.4 us -> none  [the longest x1 34.7 us: forward_batch(): expert_rows = lax.psum(partial_value.astype(jnp.bfloat16), 'seq')]
    all_to_all x16 -> x8, starting transfers between devices: 66.9 us -> 32.8 us  [the longest x2 10.5 us: to_images(): return lax.all_to_all(array, 'seq', split_axis=0, concat_axis=1, tiled=True)]
    reshape x14 -> x0, local copies, waits for them, and re-layouts: 32.2 us -> none  [the longest x4 12.1 us: forward_batch(): mixed_qkv = mixed_qkv.reshape(images, block_len, 3, groups, per_head)]
    dot_general x54 -> x28, matrix products: 94 us -> 65.4 us  [dot(): return jnp.einsum(spec, a, b, preferred_element_type=F32)]
    reduce_scatter x2, waiting for transfers between devices: 54.2 us -> 30.2 us  [from_experts(): lax.psum_scatter(rows, 'seq', scatter_dimension=0, tiled=True).astype(BF)]
  transfers between devices with their start and end apart: 22 -> 12, of which waited for: 15 -> 10; matrix products, arithmetic and copies ran while one was open for 23% -> 6% of each run, Pallas kernels for 0% -> 0%
where the time goes in v1:
time: 539 us; the launch traced here: 537 us
  waiting for transfers between devices  320 us (59%)
  matrix products  65.4 us (12%)
  local copies, waits for them, and re-layouts  53.6 us (10%)
  starting transfers between devices  33.1 us (6%)
  blocking collectives  27.8 us (5%)
  other arithmetic  22.2 us (4%)
  between operations  14.7 us (3%)
    unnamed x5, waiting for transfers between devices  148 us
    all_to_all x2, waiting for transfers between devices, to_blocks(): return lax.all_to_all(array, 'seq', split_axis=1, concat_axis=0, tiled=True)  73.4 us
    dot_general x28, matrix products, dot(): return jnp.einsum(spec, a, b, preferred_element_type=F32)  65.4 us
    all_to_all x2, waiting for transfers between devices, to_images(): return lax.all_to_all(array, 'seq', split_axis=0, concat_axis=1, tiled=True)  46.1 us
    reduce_scatter x2, waiting for transfers between devices, from_experts(): lax.psum_scatter(rows, 'seq', scatter_dimension=0, tiled=True).astype(BF)  30.2 us
    all_gather x2, blocking collectives, to_experts(): return lax.all_gather(rows, 'seq', axis=0, tiled=True)  27.8 us
    all_gather x1, waiting for transfers between devices, plain_plan(): packed = lax.all_gather(packed, ('dp', 'seq'), axis=0, tiled=True)  19.7 us
    concatenate x1, local copies, waits for them, and re-layouts, plain_plan(): jnp.concatenate([grad_qkv, grad_out_w, grad_router] + [vec[:, None] for v...  11.5 us
  transfers between devices with their start and end apart: 12, of which 10 were waited for; matrix products, arithmetic and copies ran while one was open for 6% of the time, Pallas kernels for 0%

profile of v1, /device:TPU:0, one launch (start us, length us, event | category | flops | bytes accessed | tf_op | source)
XLA Modules:
  0.0 537.2 jit_solution(11595601760084780760)
XLA Ops:
  11.1 1.6 concatenate.6
  12.8 6.3 %all-to-all-start = ((bf16[8,64,768]{2,1,0:T(8,128)(2,1)}), bf16[8,64,768]{2,1,0:T(8,128)(2,1)S(1)}, u32[]{:S(2)}, u32[]{:S(2)}) async-start(bf16[8,64,768]{2,1,0:T(8,128)(2,1)} %param.12), calls=%async_computation | async-start | bytes 1572864 | tf_op jit(solution)/shard_map/all_to_all | solution.py:38
  19.2 23.3 %all-to-all-done = bf16[8,64,768]{2,1,0:T(8,128)(2,1)S(1)} async-done(((bf16[8,64,768]{2,1,0:T(8,128)(2,1)}), bf16[8,64,768]{2,1,0:T(8,128)(2,1)S(1)}, u32[]{:S(2)}, u32[]{:S(2)}) %all-to-all-start) | async-done | bytes 786464 | tf_op jit(solution)/shard_map/all_to_all | solution.py:38
  42.4 4.2 all-to-all-start.4
  49.7 22.8 %all-to-all-done.4 = bf16[8,64,768]{2,1,0:T(8,128)(2,1)} async-done(((bf16[8,64,768]{2,1,0:T(8,128)(2,1)}), bf16[8,64,768]{2,1,0:T(8,128)(2,1)}, u32[]{:S(2)}, u32[]{:S(2)}) %all-to-all-start.4) | async-done | bytes 786464 | tf_op jit(solution)/shard_map/all_to_all | solution.py:38
  72.5 2.1 copy.193
  74.5 19.7 %all-gather.2.cloned.1.call-done = bf16[768,3084]{1,0:T(8,128)(2,1)} async-done(((bf16[24,3084]{1,0:T(8,128)(2,1)}), bf16[768,3084]{1,0:T(8,128)(2,1)}) %all-gather.2.cloned.1.call-update) | async-done | bytes 4737040 | tf_op jit(solution)/shard_map/all_gather | solution.py:66
  94.3 1.9 convert_reduce_fusion.1
  97.1 5.4 %convolution_convert_fusion = bf16[2,256,2304]{2,1,0:T(8,128)(2,1)} fusion(bf16[2,256,768]{2,1,0:T(8,128)(2,1)S(1)} %add_convert_fusion.3, bf16[768,3084]{1,0:T(8,128)(2,1)} %all-gather.2.cloned.1.call-done), kind=kOutput, calls=%fused_computation.10 | convolution fusion | flops 1813118976 | bytes 6684672 | tf_op jit(solution)/shard_map/btd,de->bte/dot_general | solution.py:13
  102.6 4.3 copy.181
  106.8 2.4 fusion.49
  109.2 2.7 fusion.98
  112.0 2.6 fusion.16
  115.4 2.2 fusion.99
  122.7 3.9 all-to-all-start.1
  126.7 2.0 convolution_convert_fusion.2
  131.5 3.9 all-to-all-start.5
  136.9 14.2 %all_gather.10 = bf16[64,1,768]{2,0,1:T(8,128)(2,1)} all-gather(bf16[16,1,768]{2,0,1:T(8,128)(2,1)} %all_to_all.102), channel_id=1, replica_groups=mesh['dp'=8,'seq'=4] {'seq'}, dimensions={0}, use_global_device_ids=true | all-gather | bytes 122880 | tf_op jit(solution)/shard_map/all_gather | solution.py:47
  152.4 13.6 %all_gather.11 = bf16[64,1,768]{2,0,1:T(8,128)(2,1)S(1)} all-gather(bf16[16,1,768]{2,0,1:T(8,128)(2,1)} %all_to_all.118), channel_id=1, replica_groups=mesh['dp'=8,'seq'=4] {'seq'}, dimensions={0}, use_global_device_ids=true | all-gather | bytes 122880 | tf_op jit(solution)/shard_map/all_gather | solution.py:47
  170.4 2.4 fusion.34
  172.8 17.2 %reduce-scatter.5.cloned.1.call-done = f32[16,1,768]{2,0,1:T(8,128)} async-done(((f32[64,1,768]{2,0,1:T(8,128)}), f32[16,1,768]{2,0,1:T(8,128)}) %reduce-scatter.5.cloned.1.call-update) | async-done | bytes 49168 | tf_op jit(solution)/shard_map/reduce_scatter | solution.py:51
  192.7 3.7 all-to-all-start.6
  197.7 13.0 %reduce-scatter.3.cloned.1.call-done = f32[16,1,768]{2,0,1:T(8,128)} async-done(((f32[64,1,768]{2,0,1:T(8,128)}), f32[16,1,768]{2,0,1:T(8,128)}) %reduce-scatter.3.cloned.1.call-update) | async-done | bytes 49168 | tf_op jit(solution)/shard_map/reduce_scatter | solution.py:51
  212.7 3.6 all-to-all-start.2
  222.1 4.6 multiply_reduce_fusion.1
  226.7 2.0 multiply_add_fusion.1
  229.9 3.0 convolution_convert_fusion.1
  234.3 4.9 fusion.13
  239.2 6.7 %multiply_reduce_fusion = (f32[2,12,256]{2,1,0:T(8,128)S(1)}, f32[2,12,256,256]{2,3,1,0:T(8,128)}) fusion(f32[2,12,256,256]{2,3,1,0:T(8,128)} %copy-done.12, f32[2,12,256]{2,1,0:T(8,128)S(1)} %copy-done.48, bf16[2,256,12,64]{1,3,2,0:T(8,128)(2,1)S(1)} %bitcast.260, bf16[2,256,3,12,64]{1,4,3,2,0:T(8,128)(2,1)S(1)} %bitcast.241), kind=kOutput, calls=%fused_computation.4 | convolution fusion | flops 206039040 | bytes 14213120 | tf_op jit(solution)/shard_map/bqhd,bkhd->bhqk/dot_general | solution.py:13
  245.9 4.3 multiply_convert_fusion
  250.2 2.0 multiply_bitcast_fusion
  253.8 2.2 convolution_bitcast_fusion.3
  257.2 1.6 maximum_convert_fusion
  259.9 4.9 convolution_bitcast_fusion
  264.9 4.4 multiply_reduce_fusion.2
  270.2 11.5 %concatenate.7 = f32[768,3084]{1,0:T(8,128)} concatenate(f32[768,2304]{1,0:T(8,128)} %convolution_bitcast_fusion, f32[768,768]{1,0:T(8,128)} %convolution_bitcast_fusion.3, f32[768,8]{1,0:T(8,128)S(1)} %copy-done.19, f32[768,1]{1,0:T(8,128)S(1)} %broadcast_in_dim.97, f32[768,1]{1,0:T(8,128)S(1)} %broadcast_in_dim.98, f32[768,1]{1,0:T(8,128)S(1)} %broadcast_in_dim.99, ...), dimensions={1} | concatenate | bytes 18948096 | tf_op jit(solution)/shard_map/concatenate | solution.py:150
  282.9 1.7 copy.191
  284.6 3.5 all-to-all-start.3
  288.2 2.4 multiply_add_fusion
  290.6 2.4 copy.204
  293.0 24.0 %all-to-all-done.3 = bf16[2,256,768]{2,0,1:T(2,128)(2,1)S(1)} async-done(((bf16[2,256,768]{2,0,1:T(2,128)(2,1)}), bf16[2,256,768]{2,0,1:T(2,128)(2,1)S(1)}, u32[]{:S(2)}, u32[]{:S(2)}) %all-to-all-start.3) | async-done | bytes 786464 | tf_op jit(solution)/shard_map/all_to_all | solution.py:42
  317.0 3.6 all-to-all-start.7
  320.6 1.9 convolution_bitcast_fusion.2
  322.5 1.9 convolution_bitcast_fusion.1
  325.4 49.4 %all-to-all-done.7 = f32[2,256,768]{2,0,1:T(2,128)S(1)} async-done(((f32[2,256,768]{2,0,1:T(2,128)}), f32[2,256,768]{2,0,1:T(2,128)S(1)}, u32[]{:S(2)}, u32[]{:S(2)}) %all-to-all-start.7) | async-done | bytes 1572896 | tf_op jit(solution)/shard_map/all_to_all | solution.py:42
  376.1 148.3 %all-reduce.3.cloned.1.call-done = f32[768,3084]{1,0:T(8,128)} async-done(((f32[768,3084]{1,0:T(8,128)}), f32[768,3084]{1,0:T(8,128)}) %all-reduce.3.cloned.1.call-update) | async-done | bytes 9474064
  525.8 1.6 constant_dynamic-slice_fusion
  527.4 1.6 dynamic-slice.2
  (229 shorter events, 49.3 us)
Async XLA Ops:
  7.2 158.8 %copy-start = (bf16[1,768,768]{2,1,0:T(8,128)(2,1)S(1)}, bf16[1,768,768]{2,1,0:T(8,128)(2,1)}, u32[]{:S(2)}) copy-start(bf16[1,768,768]{2,1,0:T(8,128)(2,1)} %param.21) | copy-start | bytes 3538948
  7.2 11.9 %copy-start.67 = (s32[8]{0:T(128)S(1)}, s32[8]{0:T(128)}, u32[]{:S(2)}) copy-start(s32[8]{0:T(128)} %param.13) | copy-start | bytes 100
  7.2 87.0 %all-gather.2.cloned.1.call-start = ((), (), s32[]{:S(2)}) async-start(), calls=%async_computation.10 | async-start | bytes 5068800 | tf_op jit(solution)/shard_map/all_gather | solution.py:66
  12.8 29.7 %all-to-all-start = ((bf16[8,64,768]{2,1,0:T(8,128)(2,1)}), bf16[8,64,768]{2,1,0:T(8,128)(2,1)S(1)}, u32[]{:S(2)}, u32[]{:S(2)}) async-start(bf16[8,64,768]{2,1,0:T(8,128)(2,1)} %param.12), calls=%async_computation | async-start | bytes 1572864 | tf_op jit(solution)/shard_map/all_to_all | solution.py:38
  42.4 30.1 %all-to-all-start.4 = ((bf16[8,64,768]{2,1,0:T(8,128)(2,1)}), bf16[8,64,768]{2,1,0:T(8,128)(2,1)}, u32[]{:S(2)}, u32[]{:S(2)}) async-start(bf16[8,64,768]{2,1,0:T(8,128)(2,1)} %param.23), calls=%async_computation.5 | async-start | bytes 1572864 | tf_op jit(solution)/shard_map/all_to_all | solution.py:38
  47.6 48.7 %copy-start.2 = (f32[2,4,64,768]{3,2,1,0:T(8,128)}, f32[2,4,64,768]{3,2,1,0:T(8,128)S(1)}, u32[]{:S(2)}) copy-start(f32[2,4,64,768]{3,2,1,0:T(8,128)S(1)} %copy.173) | copy-start | bytes 4718596
  49.6 47.5 %copy-start.51 = (f32[2,256]{1,0:T(2,128)}, f32[2,256]{1,0:T(2,128)S(1)}, u32[]{:S(2)}) copy-start(f32[2,256]{1,0:T(2,128)S(1)} %rsqrt.21) | copy-start | bytes 6148
  49.7 47.4 %copy-start.54 = (f32[2,256]{1,0:T(2,128)}, f32[2,256]{1,0:T(2,128)S(1)}, u32[]{:S(2)}) copy-start(f32[2,256]{1,0:T(2,128)S(1)} %div.65) | copy-start | bytes 6148
  96.2 21.7 %copy-start.37 = (f32[768]{0:T(1024)}, f32[768]{0:T(1024)S(1)}, u32[]{:S(2)}) copy-start(f32[768]{0:T(1024)S(1)} %get-tuple-element.70) | copy-start | bytes 9220
  122.7 8.8 %all-to-all-start.1 = ((bf16[2,8,768]{2,0,1:T(2,128)(2,1)}), bf16[2,8,768]{2,0,1:T(2,128)(2,1)}, u32[]{:S(2)}, u32[]{:S(2)}) async-start(bf16[2,8,768]{2,0,1:T(2,128)(2,1)} %copy.188), calls=%async_computation.1 | async-start | bytes 49152 | tf_op jit(solution)/shard_map/all_to_all | solution.py:46
  131.5 19.6 %all-to-all-start.5 = ((bf16[2,8,768]{2,0,1:T(2,128)(2,1)}), bf16[2,8,768]{2,0,1:T(2,128)(2,1)}, u32[]{:S(2)}, u32[]{:S(2)}) async-start(bf16[2,8,768]{2,0,1:T(2,128)(2,1)} %copy.194), calls=%async_computation.6 | async-start | bytes 49152 | tf_op jit(solution)/shard_map/all_to_all | solution.py:46
  135.4 54.6 %reduce-scatter.5.cloned.1.call-start = ((), (), s32[]{:S(2)}) async-start(), calls=%async_computation.12 | async-start | bytes 245760 | tf_op jit(solution)/shard_map/reduce_scatter | solution.py:51
  152.4 15.5 %copy-start.20 = (bf16[1,768,768]{2,1,0:T(8,128)(2,1)S(1)}, bf16[1,768,768]{2,1,0:T(8,128)(2,1)}, u32[]{:S(2)}) copy-start(bf16[1,768,768]{2,1,0:T(8,128)(2,1)} %param.22) | copy-start | bytes 3538948
  170.3 26.0 %copy-start.33 = (f32[2,4,64]{2,0,1:T(2,128)S(1)}, f32[2,4,64]{2,0,1:T(2,128)}, u32[]{:S(2)}) copy-start(f32[2,4,64]{2,0,1:T(2,128)} %copy-done.32) | copy-start | bytes 6148
  170.3 26.0 %copy-start.35 = (f32[768]{0:T(1024)S(1)}, f32[768]{0:T(1024)}, u32[]{:S(2)}) copy-start(f32[768]{0:T(1024)} %copy-done.34) | copy-start | bytes 9220
  170.3 26.0 %copy-start.44 = (f32[768]{0:T(1024)S(1)}, f32[768]{0:T(1024)}, u32[]{:S(2)}) copy-start(f32[768]{0:T(1024)} %copy-done.43) | copy-start | bytes 9220
  170.3 26.0 %copy-start.46 = (f32[2,4,64]{2,0,1:T(2,128)S(1)}, f32[2,4,64]{2,0,1:T(2,128)}, u32[]{:S(2)}) copy-start(f32[2,4,64]{2,0,1:T(2,128)} %copy-done.45) | copy-start | bytes 6148
  170.4 40.3 %reduce-scatter.3.cloned.1.call-start = ((), (), s32[]{:S(2)}) async-start(), calls=%async_computation.11 | async-start | bytes 245760 | tf_op jit(solution)/shard_map/reduce_scatter | solution.py:51
  192.7 20.1 %all-to-all-start.6 = ((bf16[8,2,768]{2,1,0:T(2,128)(2,1)}), bf16[8,2,768]{2,1,0:T(2,128)(2,1)S(1)}, u32[]{:S(2)}, u32[]{:S(2)}) async-start(bf16[8,2,768]{2,1,0:T(2,128)(2,1)} %reshape.250), calls=%async_computation.8 | async-start | bytes 49152 | tf_op jit(solution)/shard_map/all_to_all | solution.py:52
  196.4 20.4 %copy-start.31 = (bf16[2,256,8]{1,2,0:T(8,128)(2,1)S(1)}, bf16[2,256,8]{1,2,0:T(8,128)(2,1)}, u32[]{:S(2)}) copy-start(bf16[2,256,8]{1,2,0:T(8,128)(2,1)} %copy-done.30) | copy-start | bytes 24580
  196.4 20.4 %copy-start.60 = (f32[2,8]{1,0:T(2,128)S(1)}, f32[2,8]{1,0:T(2,128)}, u32[]{:S(2)}) copy-start(f32[2,8]{1,0:T(2,128)} %copy-done.59) | copy-start | bytes 196
  212.7 8.4 %all-to-all-start.2 = ((bf16[8,2,768]{2,1,0:T(2,128)(2,1)}), bf16[8,2,768]{2,1,0:T(2,128)(2,1)S(1)}, u32[]{:S(2)}, u32[]{:S(2)}) async-start(bf16[8,2,768]{2,1,0:T(2,128)(2,1)} %reshape.248), calls=%async_computation.3 | async-start | bytes 49152 | tf_op jit(solution)/shard_map/all_to_all | solution.py:52
  216.4 308.0 %all-reduce.3.cloned.1.call-start = ((), (), s32[]{:S(2)}) async-start(), calls=%async_computation.13 | async-start | bytes 19660800
  216.8 4.7 copy-start.11
  216.8 4.6 copy-start.62
  216.8 4.6 copy-start.64
  221.3 5.4 copy-start.26
  234.3 4.9 copy-start.8
  234.3 11.6 %slice-start = ((s8[6291456]{0:T(1024)(128)(4,1)}), s8[4194304]{0:T(1024)(128)(4,1)S(1)}, s32[]{:S(2)}) async-start(s8[6291456]{0:T(1024)(128)(4,1)} %bitcast.249), calls=%async_computation.14 | async-start | bytes 8388608
  239.2 6.7 %slice-start.1 = ((s8[6291456]{0:T(1024)(128)(4,1)}), s8[2097152]{0:T(1024)(128)(4,1)S(1)}, s32[]{:S(2)}) async-start(s8[6291456]{0:T(1024)(128)(4,1)} %bitcast.249), calls=%async_computation.15 | async-start | bytes 4194304
  258.8 6.0 %slice-start.2 = ((s8[4915200]{0:T(1024)(128)(4,1)}), s8[4194304]{0:T(1024)(128)(4,1)S(1)}, s32[]{:S(2)}) async-start(s8[4915200]{0:T(1024)(128)(4,1)} %bitcast.256), calls=%async_computation.16 | async-start | bytes 8388608
  259.9 4.9 copy-start.4
  259.9 4.9 slice-start.3
  259.9 4.9 copy-start.52
  259.9 4.9 copy-start.55
  264.8 4.7 copy-start.58
  264.9 4.9 copy-start.57
  282.9 5.3 copy-start.66
  282.9 5.3 copy-start.65
  282.9 5.3 copy-start.5
  282.9 5.3 copy-start.36
  282.9 5.3 copy-start.53
  282.9 5.3 copy-start.56
  284.6 32.3 %all-to-all-start.3 = ((bf16[2,256,768]{2,0,1:T(2,128)(2,1)}), bf16[2,256,768]{2,0,1:T(2,128)(2,1)S(1)}, u32[]{:S(2)}, u32[]{:S(2)}) async-start(bf16[2,256,768]{2,0,1:T(2,128)(2,1)} %copy.191), calls=%async_computation.4 | async-start | bytes 1572864 | tf_op jit(solution)/shard_map/all_to_all | solution.py:42
  293.0 27.6 %copy-start.21 = (bf16[64,1,768]{2,0,1:T(8,128)(2,1)S(1)}, bf16[64,1,768]{2,0,1:T(8,128)(2,1)}, u32[]{:S(2)}) copy-start(bf16[64,1,768]{2,0,1:T(8,128)(2,1)} %all_gather.10) | copy-start | bytes 294916
  293.0 27.6 %copy-start.23 = (bf16[64,768]{1,0:T(8,128)(2,1)S(1)}, bf16[64,768]{1,0:T(8,128)(2,1)}, u32[]{:S(2)}) copy-start(bf16[64,768]{1,0:T(8,128)(2,1)} %copy-done.22) | copy-start | bytes 294916
  317.0 57.8 %all-to-all-start.7 = ((f32[2,256,768]{2,0,1:T(2,128)}), f32[2,256,768]{2,0,1:T(2,128)S(1)}, u32[]{:S(2)}, u32[]{:S(2)}) async-start(f32[2,256,768]{2,0,1:T(2,128)} %copy.204), calls=%async_computation.9 | async-start | bytes 3145728 | tf_op jit(solution)/shard_map/all_to_all | solution.py:42
  374.8 155.9 %copy-start.1 = (bf16[1,768,768]{2,1,0:T(8,128)(2,1)S(1)}, bf16[1,768,768]{2,1,0:T(8,128)(2,1)}, u32[]{:S(2)}) copy-start(bf16[1,768,768]{2,1,0:T(8,128)(2,1)} %param.21) | copy-start | bytes 3538948
  (36 other events, 70.3 us)
Sparse Core Ops, SparseCore 0:
  12.9 81.3 all-gather.1
  170.5 19.5 reduce-scatter.4
  193.0 17.6 reduce-scatter.2
  281.9 242.4 all-reduce.2

commit v2 on v1

--- a/solution.py
+++ b/solution.py
@@ -1,6 +1,8 @@
 import jax
 import jax.numpy as jnp
 from jax import lax
+from jax.experimental import pallas as pl
+from jax.experimental.pallas import tpu as pltpu
 from jax.sharding import PartitionSpec as P
 
 H = 12
@@ -166,12 +168,469 @@
     )
 
 
+MESH = pl.DeviceIdType.MESH
+VM = pltpu.VMEM
+
+
+def nt(a, b):
+    return lax.dot_general(a, b, (((1,), (1,)), ((), ())), preferred_element_type=F32)
+
+
+def tn(a, b):
+    return lax.dot_general(a, b, (((0,), (0,)), ((), ())), preferred_element_type=F32)
+
+
+def mm(a, b):
+    return jnp.dot(a, b, preferred_element_type=F32)
+
+
+def ds(start, size):
+    return pl.ds(pl.multiple_of(start, size), size)
+
+
+def remote(src, dst, send, recv, device):
+    return pltpu.make_async_remote_copy(
+        src_ref=src, dst_ref=dst, send_sem=send, recv_sem=recv, device_id=device,
+        device_id_type=MESH,
+    )
+
+
+def place():
+    d, z = lax.axis_index("dp"), lax.axis_index("seq")
+    core, x, y = lax.rem(d, 2), lax.rem(d // 2, 2), d // 4
+    return d, z, d + 2 - 4 * x, d + 4 - 8 * y, d + 1 - 2 * core
+
+
+def other(d, kind):
+    core, x, y = lax.rem(d, 2), lax.rem(d // 2, 2), d // 4
+    return {"x": d + 2 - 4 * x, "y": d + 4 - 8 * y, "core": d + 1 - 2 * core}[kind]
+
+
+def greet(devices):
+    barrier = pltpu.get_barrier_semaphore()
+    for device in devices:
+        pl.semaphore_signal(barrier, inc=1, device_id=device, device_id_type=MESH)
+    pl.semaphore_wait(barrier, len(devices))
+
+
+def gather_steps(packed, stage, full, zsend, zrecv, send, recv):
+    d, z, dx, dy, dc = place()
+    rows = 4 * packed.shape[0] // 2
+    half = rows // 2
+    over_x, over_y, over_c = (dx, z), (dy, z), (dc, z)
+
+    def block(owner, part):
+        if part is None:
+            return full.at[ds(owner * rows, rows)]
+        return full.at[ds(owner * rows + part * half, half)]
+
+    first = [
+        remote(packed, stage.at[z], zsend.at[k - 1], zrecv.at[k - 1], (d, lax.rem(z + k, 4)))
+        for k in range(1, 4)
+    ]
+
+    def copy(n, owner, part, device):
+        ref = block(owner, part)
+        return remote(ref, ref, send.at[n], recv.at[n], device)
+
+    ddx, ddy = other(dx, "y"), other(dy, "x")
+    plan = [
+        copy(0, d, 0, over_x),
+        copy(1, d, 1, over_y),
+        copy(2, d, 1, over_x),
+        copy(3, d, 0, over_y),
+        copy(4, d, None, over_c),
+        copy(5, dx, 0, over_y),
+        copy(6, dy, 1, over_x),
+        copy(7, dx, 0, over_c),
+        copy(8, dy, 1, over_c),
+        copy(9, dx, 1, over_c),
+        copy(10, dy, 0, over_c),
+        copy(11, ddx, 0, over_c),
+        copy(12, ddx, 1, over_c),
+    ]
+    s = dc
+    sx, sy = other(s, "x"), other(s, "y")
+    sd = other(sx, "y")
+    landing = [
+        (dx, 0), (dy, 1), (dx, 1), (dy, 0), (s, None), (ddx, 0), (ddx, 1),
+        (sx, 0), (sy, 1), (sx, 1), (sy, 0), (sd, 0), (sd, 1),
+    ]
+
+    def arrived(n):
+        ref = block(*landing[n])
+        remote(ref, ref, send.at[n], recv.at[n], over_x).wait_recv()
+
+    def start():
+        for one in first:
+            one.start()
+
+    def assemble():
+        own = pltpu.make_async_copy(packed, stage.at[z], zrecv.at[3])
+        own.start()
+        own.wait()
+        for one in first:
+            one.wait_recv()
+        quarter = packed.shape[0] // 2
+        wide = packed.shape[1]
+        for side in range(2):
+            value = jnp.concatenate(
+                [
+                    stage[k].astype(F32)[side * quarter : (side + 1) * quarter]
+                    for k in range(4)
+                ],
+                axis=0,
+            )
+            full[ds(d * rows, rows), side * wide : (side + 1) * wide] = value.astype(BF)
+        for n in range(5):
+            plan[n].start()
+
+    def forward_one():
+        arrived(0)
+        plan[5].start()
+        plan[7].start()
+        arrived(1)
+        plan[6].start()
+        plan[8].start()
+
+    def forward_two():
+        arrived(2)
+        plan[9].start()
+        arrived(3)
+        plan[10].start()
+        arrived(5)
+        plan[11].start()
+        arrived(6)
+        plan[12].start()
+
+    def finish():
+        for n in (4, 7, 8, 9, 10, 11, 12):
+            arrived(n)
+        for one in first + plan:
+            one.wait_send()
+
+    return start, assemble, forward_one, forward_two, finish
+
+
+def image_steps(blocks, whole, send, recv, images, local_sem):
+    d, z = lax.axis_index("dp"), lax.axis_index("seq")
+    size = blocks.shape[1]
+    length = 4 * size
+
+    def make(i, k):
+        there = lax.rem(z + k, 4)
+        src = blocks.at[there * images + i]
+        dst = whole.at[ds(i * length + z * size, size)]
+        if k == 0:
+            return pltpu.make_async_copy(src, dst, local_sem.at[i])
+        return remote(
+            src, dst, send.at[i * 3 + k - 1], recv.at[i * 3 + k - 1], (d, there)
+        )
+
+    table = [[make(i, k) for k in range(4)] for i in range(images)]
+
+    def start(i):
+        for one in table[i]:
+            one.start()
+
+    def arrived(i):
+        table[i][0].wait()
+        for one in table[i][1:]:
+            one.wait_recv()
+
+    def finish():
+        for i in range(images):
+            for one in table[i][1:]:
+                one.wait_send()
+
+    return start, arrived, finish
+
+
+def unit_rows(x):
+    centred = x - jnp.mean(x, axis=-1, keepdims=True)
+    inverse = lax.rsqrt(jnp.mean(centred * centred, axis=-1, keepdims=True) + 1e-06)
+    return centred * inverse, inverse
+
+
+def head_masks():
+    lane = lax.broadcasted_iota(jnp.int32, (1, 2 * HD), 1)
+    left = jnp.where(lane < HD, 1.0, 0.0)
+    return left.astype(BF), (1.0 - left).astype(BF)
+
+
+def split_heads(pair):
+    left, right = head_masks()
+    return jnp.concatenate([pair * left, pair * right], axis=0)
+
+
+def forward_kernel(
+    lengths, packed, tokens, cotangent,
+    full, small, xs, cots, qkv, probs, attended, middle, n_one, n_two,
+    disp, comb, slots, denom,
+    stage, bias, zsend, zrecv, wsend, wrecv, tsend, trecv, csend, crecv, local,
+):
+    d, z, dx, dy, dc = place()
+    width = tokens.shape[2]
+    images = tokens.shape[0] // 4
+    length = 4 * tokens.shape[1]
+    pairs = width // (2 * HD)
+    zs = [(d, lax.rem(z + k, 4)) for k in range(1, 4)]
+    greet(zs + [(dx, z), (dy, z), (dc, z)])
+    w_start, w_assemble, w_one, w_two, w_finish = gather_steps(
+        packed, stage, full, zsend, zrecv, wsend, wrecv
+    )
+    t_start, t_arrived, t_finish = image_steps(tokens, xs, tsend, trecv, images, local)
+    c_start, c_arrived, c_finish = image_steps(cotangent, cots, csend, crecv, images, local)
+    w_start()
+    for i in range(images):
+        t_start(i)
+    w_assemble()
+    w_one()
+    w_two()
+    for i in range(images):
+        t_arrived(i)
+    for i in range(images):
+        c_start(i)
+    w_finish()
+    small[...] = full[:, 4 * width : 4 * width + 128].astype(F32).T[:16]
+    gains = [small[8 + k : 9 + k, :] for k in range(4)]
+
+    rows = 64
+
+    def norm_one(k, carry):
+        at = ds(k * rows, rows)
+        unit, _ = unit_rows(xs[at, :].astype(F32))
+        n_one[at, :] = (unit * gains[0] + gains[1]).astype(BF)
+        return carry
+
+    lax.fori_loop(0, images * length // rows, norm_one, 0)
+
+    def project(k, carry):
+        at = ds(k * 256, 256)
+        qkv[:, at] = mm(n_one[...], full[:, at]).astype(BF)
+        return carry
+
+    lax.fori_loop(0, 3 * width // 256, project, 0)
+
+    key = lax.broadcasted_iota(jnp.int32, (1, length), 1)
+    for i in range(images):
+        bias[i] = jnp.where(key < lengths[z * images + i], 0.0, -1000000000.0)
+
+    def attend(t, carry):
+        i, p = t // pairs, lax.rem(t, pairs)
+        at = ds(i * length, length)
+        q = qkv[at, ds(p * 128, 128)] * jnp.asarray(HD ** (-0.5), BF)
+        keys = split_heads(qkv[at, ds(width + p * 128, 128)])
+        values = split_heads(qkv[at, ds(2 * width + p * 128, 128)])
+        scores = nt(q, keys)
+        for h in range(2):
+            part = scores[:, h * length : (h + 1) * length] + bias[i]
+            top = jnp.max(part, axis=-1, keepdims=True)
+            e = jnp.exp(part - top)
+            total = jnp.sum(e, axis=-1, keepdims=True)
+            probs[t, :, h * length : (h + 1) * length] = (e * (1.0 / total)).astype(BF)
+        attended[at, ds(p * 128, 128)] = mm(probs[t], values).astype(BF)
+        return carry
+
+    lax.fori_loop(0, images * pairs, attend, 0)
+
+    def project_out(k, carry):
+        at = ds(k * 256, 256)
+        weight = full[:, ds(3 * width + k * 256, 256)]
+        middle[:, at] = xs[:, at].astype(F32) + mm(attended[...], weight)
+        return carry
+
+    lax.fori_loop(0, width // 256, project_out, 0)
+
+    def norm_two(k, carry):
+        at = ds(k * rows, rows)
+        unit, _ = unit_rows(middle[at, :])
+        n_two[at, :] = (unit * gains[2] + gains[3]).astype(BF)
+        return carry
+
+    lax.fori_loop(0, images * length // rows, norm_two, 0)
+    router = small[0:8, :].astype(BF)
+    for i in range(images):
+        at = slice(i * length, (i + 1) * length)
+        logits = nt(router, n_two[at, :])
+        inside = key < lengths[z * images + i]
+        top = jnp.floor(
+            jnp.max(jnp.where(inside, logits, -1000000000.0), axis=-1, keepdims=True)
+        )
+        dispatch = jnp.where(inside, jnp.exp(logits - top), 0.0)
+        peak = jnp.max(logits, axis=0, keepdims=True)
+        e = jnp.exp(logits - peak)
+        disp[:, at] = dispatch
+        comb[:, at] = e / jnp.sum(e, axis=0, keepdims=True)
+        total = jnp.sum(dispatch, axis=-1, keepdims=True)
+        denom[i] = jnp.broadcast_to(total, denom.shape[1:])
+        slots[i] = mm(dispatch.astype(BF), n_two[at, :]) / total
+    for i in range(images):
+        c_arrived(i)
+    t_finish()
+    c_finish()
+
+
+def run_forward(lengths, packed, tokens, cotangent):
+    width = tokens.shape[2]
+    images, length = tokens.shape[0] // 4, 4 * tokens.shape[1]
+    count = images * length
+    pairs = width // (2 * HD)
+
+    def shape(*dims, kind=BF):
+        return jax.ShapeDtypeStruct(dims, kind)
+
+    outs = (
+        shape(width, 2 * packed.shape[1]),
+        shape(16, width, kind=F32),
+        shape(count, width),
+        shape(count, width),
+        shape(count, 3 * width),
+        shape(images * pairs, length, 2 * length),
+        shape(count, width),
+        shape(count, width, kind=F32),
+        shape(count, width),
+        shape(count, width),
+        shape(8, count, kind=F32),
+        shape(8, count, kind=F32),
+        shape(images, 8, width, kind=F32),
+        shape(images, 8, 128, kind=F32),
+    )
+    dma = pltpu.SemaphoreType.DMA
+    return pl.pallas_call(
+        forward_kernel,
+        out_shape=outs,
+        in_specs=[pl.BlockSpec(memory_space=pltpu.SMEM)]
+        + [pl.BlockSpec(memory_space=VM)]
+        + [pl.BlockSpec(memory_space=pl.ANY)] * 2,
+        out_specs=[pl.BlockSpec(memory_space=VM)] * len(outs),
+        scratch_shapes=[
+            VM((4,) + packed.shape, BF),
+            VM((images, 1, length), F32),
+            dma((3,)), dma((4,)), dma((13,)), dma((13,)),
+            dma((3 * images,)), dma((3 * images,)), dma((3 * images,)), dma((3 * images,)),
+            dma((images,)),
+        ],
+        compiler_params=pltpu.CompilerParams(
+            collective_id=0, has_side_effects=True, vmem_limit_bytes=60 * 2**20
+        ),
+        name="forward",
+    )(lengths, packed, tokens, cotangent)
+
+
+def kernel_plan(
+    tokens, lengths, w_qkv, w_out, router, gain_one, shift_one, gain_two, shift_two,
+    w_up, w_down, cotangent,
+):
+    model_width, slots_all = w_qkv.shape[1] // 3, router.shape[1]
+    vectors = jnp.stack([gain_one, shift_one, gain_two, shift_two], axis=1)
+    filler = jnp.zeros((w_qkv.shape[0], 256 - slots_all - 4), BF)
+    packed = jnp.concatenate([w_qkv, w_out, router, vectors, filler], axis=1)
+    half = packed.shape[1] // 2
+    packed = jnp.concatenate([packed[:, :half], packed[:, half:]], axis=0)
+    (full, small, xs, cots, qkv, probs, attended, middle, n_one, n_two, disp, comb, slots, denom) = (
+        run_forward(lengths, packed, tokens, cotangent)
+    )
+    images, length_all = 2, 256
+    split = 4 * model_width
+    w_qkv, w_out = full[:, : 3 * model_width], full[:, 3 * model_width : split]
+    router = full[:, split : split + slots_all]
+    gain_one, shift_one, gain_two, shift_two = (small[8 + k] for k in range(4))
+    cot = cots.reshape(images, length_all, model_width)
+    qkv = qkv.reshape(images, length_all, 3, H, HD)
+    queries, keys_all, values_all = qkv[:, :, 0], qkv[:, :, 1], qkv[:, :, 2]
+    probs_low = probs.reshape(images, H // 2, length_all, 2, length_all).transpose(0, 1, 3, 2, 4)
+    probs_low = probs_low.reshape(images, H, length_all, length_all)
+    probs = probs_low.astype(F32)
+    attended = attended.reshape(images, length_all, model_width)
+    middle = middle.reshape(images, length_all, model_width)
+    normed_one = n_one.reshape(images, length_all, model_width)
+    normed_two = n_two.reshape(images, length_all, model_width)
+    unit_one, inverse_one = unit_norm(xs.reshape(images, length_all, model_width).astype(F32))
+    unit_two, inverse_two = unit_norm(middle)
+    dispatch = disp.T.reshape(images, length_all, slots_all)
+    combine = comb.T.reshape(images, length_all, slots_all)
+    dispatch_low = dispatch.astype(BF)
+    denominator = denom[:, :, 0]
+    slot_vals = slots
+    slot_rows = to_experts(slot_vals.astype(BF))
+    hidden = dot("red,edf->ref", slot_rows, w_up)
+    active = gelu_tanh(hidden).astype(BF)
+    expert_out = from_experts(dot("ref,efd->red", active, w_down))
+    combine_low = combine.astype(BF)
+    block_out = (middle + dot("bte,bed->btd", combine_low, expert_out)).astype(BF)
+
+    d_combine = dot("btd,bed->bte", cot, expert_out)
+    d_expert = dot("bte,btd->bed", combine_low, cot).astype(BF)
+    d_rows = to_experts(d_expert)
+    d_active = dot("red,efd->ref", d_rows, w_down)
+    grad_down = dot("ref,red->efd", active, d_rows)
+    d_hidden = jax.vjp(gelu_tanh, hidden)[1](d_active)[0].astype(BF)
+    grad_up = dot("red,ref->edf", slot_rows, d_hidden)
+    d_slots = from_experts(dot("ref,edf->red", d_hidden, w_up))
+    d_slots_wide = d_slots.astype(F32)
+    inner = jnp.sum(slot_vals * d_slots_wide, axis=-1)
+    projected = dot("btd,bed->bte", normed_two, d_slots)
+    d_logits = (projected - inner[:, None, :]) / denominator[:, None, :] * dispatch
+    d_logits = d_logits + combine * (
+        d_combine - jnp.sum(combine * d_combine, axis=-1, keepdims=True)
+    )
+    d_logits = d_logits.astype(BF)
+    scaled = d_slots_wide / denominator[:, :, None]
+    scaled_high = scaled.astype(BF)
+    scaled_rest = (scaled - scaled_high.astype(F32)).astype(BF)
+    d_normed_two = (
+        dot("bte,bed->btd", dispatch_low, scaled_high)
+        + dot("bte,bed->btd", dispatch_low, scaled_rest)
+        + dot("bte,de->btd", d_logits, router)
+    )
+    grad_router = dot("btd,bte->de", normed_two, d_logits)
+    d_norm, grad_gain_two, grad_shift_two = norm_back(d_normed_two, unit_two, inverse_two, gain_two)
+    d_middle = cot.astype(F32) + d_norm
+    d_branch = d_middle.astype(BF)
+    grad_out_w = dot("btd,bte->de", attended, d_branch)
+    d_attended = dot("bte,de->btd", d_branch, w_out).astype(BF)
+    d_attended = d_attended.reshape(images, length_all, H, HD)
+    d_values = dot("bhqk,bqhd->bkhd", probs_low, d_attended)
+    d_probs = dot("bqhd,bkhd->bhqk", d_attended, values_all)
+    d_scores = probs * (d_probs - jnp.sum(probs * d_probs, axis=-1, keepdims=True))
+    d_scores = d_scores.astype(BF)
+    d_queries = dot("bhqk,bkhd->bqhd", d_scores, keys_all) * HD ** (-0.5)
+    d_keys = dot("bhqk,bqhd->bkhd", d_scores, queries) * HD ** (-0.5)
+    d_qkv = jnp.stack([d_queries, d_keys, d_values], axis=2).astype(BF)
+    d_qkv = d_qkv.reshape(images, length_all, 3 * model_width)
+    grad_qkv = dot("btd,bte->de", normed_one, d_qkv)
+    d_normed_one = dot("bte,de->btd", d_qkv, w_qkv)
+    d_norm, grad_gain_one, grad_shift_one = norm_back(d_normed_one, unit_one, inverse_one, gain_one)
+    grad_input = to_blocks(d_middle + d_norm)
+
+    vectors = (grad_gain_one, grad_shift_one, grad_gain_two, grad_shift_two)
+    packed = jnp.concatenate(
+        [grad_qkv, grad_out_w, grad_router] + [vec[:, None] for vec in vectors], axis=1
+    )
+    packed = lax.psum_scatter(packed, ("dp", "seq"), scatter_dimension=0, tiled=True)
+    return (
+        to_blocks(block_out),
+        grad_input,
+        packed[:, : 3 * model_width],
+        packed[:, 3 * model_width : split],
+        packed[:, split : split + slots_all],
+        packed[:, split + slots_all],
+        packed[:, split + slots_all + 1],
+        packed[:, split + slots_all + 2],
+        packed[:, split + slots_all + 3],
+        grad_up,
+        grad_down,
+    )
+
+
 def solution(mesh):
+    plan = kernel_plan if dict(mesh.shape) == {"dp": 8, "seq": 4} else plain_plan
     rows, vector = P(("dp", "seq"), None), P(("dp", "seq"))
     tokens = P("dp", "seq", None)
     up, down = P("dp", None, "seq"), P("dp", "seq", None)
     return jax.shard_map(
-        plain_plan,
+        plan,
         mesh=mesh,
         in_specs=(tokens, P("dp"), rows, rows, rows)
         + (vector,) * 4

time: 539 us -> 509 us (0.944)
  waiting for transfers between devices: 320 us -> 239 us
  Pallas kernels: 0 us -> 62.9 us
  matrix products: 65.4 us -> 42 us
  local copies, waits for them, and re-layouts: 53.6 us -> 73.9 us
  starting transfers between devices: 33.1 us -> 23.3 us
  blocking collectives: 27.8 us -> 36.9 us
  other arithmetic: 22.2 us -> 14.8 us
    pallas_call x0 -> x1, Pallas kernels: none -> 62.9 us  [run_forward(): pl.pallas_call(forward_kernel, out_shape=outs, in_specs=[pl.BlockSpec(mem...]
    all_to_all x2 -> x0, waiting for transfers between devices: 46.1 us -> none  [to_images(): return lax.all_to_all(array, 'seq', split_axis=0, concat_axis=1, tiled=True)]
    dot_general x28 -> x22, matrix products: 65.4 us -> 42 us  [dot(): return jnp.einsum(spec, a, b, preferred_element_type=F32)]
    all_gather x1 -> x0, waiting for transfers between devices: 19.7 us -> none  [plain_plan(): packed = lax.all_gather(packed, ('dp', 'seq'), axis=0, tiled=True)]
    reduce_scatter x2, waiting for transfers between devices: 30.2 us -> 16 us  [from_experts(): lax.psum_scatter(rows, 'seq', scatter_dimension=0, tiled=True).astype(BF)]
    reshape x0 -> x2, local copies, waits for them, and re-layouts: none -> 11.6 us  [the longest x1 6.04 us: kernel_plan(): qkv = qkv.reshape(images, length_all, 3, H, HD)]
    all_to_all x2 -> x0, starting transfers between devices: 10.5 us -> none  [to_images(): return lax.all_to_all(array, 'seq', split_axis=0, concat_axis=1, tiled=True)]
    all_gather x2, blocking collectives: 27.8 us -> 36.9 us  [to_experts(): return lax.all_gather(rows, 'seq', axis=0, tiled=True)]
  transfers between devices with their start and end apart: 12 -> 9, of which waited for: 10 -> 5; matrix products, arithmetic and copies ran while one was open for 6% -> 11% of each run, Pallas kernels for 0% -> 0%
where the time goes in v2:
time: 509 us; the launch traced here: 507 us
  waiting for transfers between devices  239 us (47%)
  local copies, waits for them, and re-layouts  73.9 us (15%)
  Pallas kernels  62.9 us (12%)
  matrix products  42 us (8%)
  blocking collectives  36.9 us (7%)
  starting transfers between devices  23.3 us (5%)
  other arithmetic  14.8 us (3%)
  between operations  14.4 us (3%)
    unnamed x4, waiting for transfers between devices  148 us
    all_to_all x2, waiting for transfers between devices, to_blocks(): return lax.all_to_all(array, 'seq', split_axis=1, concat_axis=0, tiled=True)  73.8 us
    pallas_call x1, Pallas kernels, run_forward(): pl.pallas_call(forward_kernel, out_shape=outs, in_specs=[pl.BlockSpec(mem...  62.9 us
    dot_general x22, matrix products, dot(): return jnp.einsum(spec, a, b, preferred_element_type=F32)  42 us
    all_gather x2, blocking collectives, to_experts(): return lax.all_gather(rows, 'seq', axis=0, tiled=True)  36.9 us
    reduce_scatter x2, waiting for transfers between devices, from_experts(): lax.psum_scatter(rows, 'seq', scatter_dimension=0, tiled=True).astype(BF)  16 us
    concatenate x1, local copies, waits for them, and re-layouts, kernel_plan(): jnp.concatenate([grad_qkv, grad_out_w, grad_router] + [vec[:, None] for v...  11.5 us
  transfers between devices with their start and end apart: 9, of which 5 were waited for; matrix products, arithmetic and copies ran while one was open for 11% of the time, Pallas kernels for 0%

profile of v2, /device:TPU:0, one launch (start us, length us, event | category | flops | bytes accessed | tf_op | source)
XLA Modules:
  0.0 506.8 jit_solution(5989024569588364197)
XLA Ops:
  13.6 62.9 %forward.1 = (bf16[768,3328]{1,0:T(8,128)(2,1)}, f32[16,768]{1,0:T(8,128)}, bf16[512,768]{1,0:T(8,128)(2,1)}, bf16[512,768]{1,0:T(8,128)(2,1)}, bf16[512,2304]{1...) custom-call(s32[8]{0:T(128)} %lengths.1, ...), custom_call_target="tpu_custom_call" | custom-call | tf_op jit(solution)/shard_map/forward/pallas_call | solution.py:500
  78.1 3.9 all-to-all-start
  82.0 1.6 reduce_sum.135
  85.0 4.3 copy.129
  89.2 6.0 %reshape.189 = bf16[2,256,3,12,64]{1,0,4,3,2:T(2,128)(2,1)} reshape(bf16[512,2304]{0,1:T(8,128)(2,1)} %copy.129) | data formatting | bytes 4718592 | tf_op jit(solution)/shard_map/reshape | solution.py:540
  95.3 4.2 fusion.83
  101.5 4.1 all-to-all-start.3
  105.6 1.4 all_to_all.81
  107.0 23.2 %all_gather.6 = bf16[64,1,768]{2,0,1:T(8,128)(2,1)} all-gather(bf16[16,1,768]{2,0,1:T(8,128)(2,1)} %all_to_all.81), channel_id=1, replica_groups=mesh['dp'=8,'seq'=4] {'seq'}, dimensions={0}, use_global_device_ids=true | all-gather | bytes 122880 | tf_op jit(solution)/shard_map/all_gather | solution.py:49
  130.2 1.4 all_to_all.93
  131.6 13.7 %all_gather.7 = bf16[64,1,768]{2,0,1:T(8,128)(2,1)S(1)} all-gather(bf16[16,1,768]{2,0,1:T(8,128)(2,1)} %all_to_all.93), channel_id=1, replica_groups=mesh['dp'=8,'seq'=4] {'seq'}, dimensions={0}, use_global_device_ids=true | all-gather | bytes 122880 | tf_op jit(solution)/shard_map/all_gather | solution.py:49
  145.3 1.3 fusion.16
  148.4 1.2 fusion.19
  150.3 2.4 fusion.22
  153.6 16.0 %reduce-scatter.5.cloned.1.call-done = f32[16,1,768]{2,0,1:T(8,128)} async-done(((f32[64,1,768]{2,0,1:T(8,128)}), f32[16,1,768]{2,0,1:T(8,128)}) %reduce-scatter.5.cloned.1.call-update) | async-done | bytes 49168 | tf_op jit(solution)/shard_map/reduce_scatter | solution.py:53
  172.2 3.6 all-to-all-start.4
  176.0 5.5 %reshape.190 = bf16[2,6,256,2,256]{4,3,2,1,0:T(2,128)(2,1)} reshape(bf16[12,256,512]{2,1,0:T(8,128)(2,1)} %get-tuple-element.36) | data formatting | bytes 6291456 | tf_op jit(solution)/shard_map/reshape | solution.py:542
  181.6 8.6 %copy.131 = bf16[2,6,2,256,256]{3,4,2,1,0:T(8,128)(2,1)} copy(bf16[2,6,2,256,256]{4,2,3,1,0:T(2,128)(2,1)} %bitcast.202) | data formatting | bytes 6291456 | tf_op jit(solution)/shard_map/transpose | solution.py:542
  192.2 4.2 all-to-all-start.1
  196.9 1.6 fusion.75
  198.5 1.6 fusion.63
  201.7 1.5 fusion.32
  203.2 2.3 convolution_bitcast_fusion.5
  205.5 4.6 multiply_reduce_fusion
  210.1 2.0 multiply_add_fusion.1
  212.1 1.1 copy-done.4
  213.2 3.0 convolution_convert_fusion
  216.2 1.4 copy.132
  217.6 3.1 convolution_bitcast_fusion.4
  225.2 1.2 copy-done.5
  226.6 2.2 convolution_bitcast_fusion.3
  228.8 4.9 convolution_bitcast_fusion
  233.7 4.5 multiply_reduce_fusion.1
  239.7 11.5 %concatenate.11 = f32[768,3084]{1,0:T(8,128)} concatenate(f32[768,2304]{1,0:T(8,128)} %convolution_bitcast_fusion, f32[768,768]{1,0:T(8,128)} %convolution_bitcast_fusion.3, f32[768,8]{1,0:T(8,128)} %convolution_bitcast_fusion.5, f32[768,1]{1,0:T(8,128)S(1)} %broadcast_in_dim.15, f32[768,1]{1,0:T(8,128)S(1)} %broadcast_in_dim.32, f32[768,1]{1,0:T(8,128)S(1)} %broadcast_in_dim.33, ...), dimensions={1} | concatenate | bytes 18948096 | tf_op jit(solution)/shard_map/concatenate | solution.py:608
  252.5 1.7 copy.123
  254.2 3.5 all-to-all-start.2
  257.7 2.0 multiply_add_fusion
  259.7 2.4 copy.140
  262.1 24.4 %all-to-all-done.2 = bf16[2,256,768]{2,0,1:T(2,128)(2,1)S(1)} async-done(((bf16[2,256,768]{2,0,1:T(2,128)(2,1)}), bf16[2,256,768]{2,0,1:T(2,128)(2,1)S(1)}, u32[]{:S(2)}, u32[]{:S(2)}) %all-to-all-start.2) | async-done | bytes 786464 | tf_op jit(solution)/shard_map/all_to_all | solution.py:44
  287.4 3.6 all-to-all-start.5
  291.0 1.9 convolution_bitcast_fusion.2
  292.9 1.9 convolution_bitcast_fusion.1
  295.8 49.4 %all-to-all-done.5 = f32[2,256,768]{2,0,1:T(2,128)S(1)} async-done(((f32[2,256,768]{2,0,1:T(2,128)}), f32[2,256,768]{2,0,1:T(2,128)S(1)}, u32[]{:S(2)}, u32[]{:S(2)}) %all-to-all-start.5) | async-done | bytes 1572896 | tf_op jit(solution)/shard_map/all_to_all | solution.py:44
  345.2 1.3 copy.141
  346.5 147.5 %all-reduce.3.cloned.1.call-done = f32[768,3084]{1,0:T(8,128)} async-done(((f32[768,3084]{1,0:T(8,128)}), f32[768,3084]{1,0:T(8,128)}) %all-reduce.3.cloned.1.call-update) | async-done | bytes 9474064
  495.4 1.6 constant_dynamic-slice_fusion
  497.0 1.6 dynamic-slice.2
  498.7 1.6 dynamic-slice_reduce_fusion
  (166 shorter events, 32.2 us)
Async XLA Ops:
  7.2 138.1 %copy-start = (bf16[1,768,768]{2,1,0:T(8,128)(2,1)S(1)}, bf16[1,768,768]{2,1,0:T(8,128)(2,1)}, u32[]{:S(2)}) copy-start(bf16[1,768,768]{2,1,0:T(8,128)(2,1)} %param.21) | copy-start | bytes 3538948
  76.6 7.6 %copy-start.7 = (bf16[512,768]{1,0:T(8,128)(2,1)S(1)}, bf16[512,768]{1,0:T(8,128)(2,1)}, u32[]{:S(2)}) copy-start(bf16[512,768]{1,0:T(8,128)(2,1)} %get-tuple-element.34) | copy-start | bytes 2359300
  78.1 23.4 %all-to-all-start = ((bf16[2,8,768]{2,0,1:T(2,128)(2,1)}), bf16[2,8,768]{2,0,1:T(2,128)(2,1)}, u32[]{:S(2)}, u32[]{:S(2)}) async-start(bf16[2,8,768]{2,0,1:T(2,128)(2,1)} %copy.120), calls=%async_computation | async-start | bytes 49152 | tf_op jit(solution)/shard_map/all_to_all | solution.py:48
  95.3 4.2 copy-start.8
  95.3 4.2 copy-start.25
  95.3 4.4 copy-start.2
  95.3 4.4 copy-start.30
  95.3 4.4 copy-start.32
  101.5 28.7 %all-to-all-start.3 = ((bf16[2,8,768]{2,0,1:T(2,128)(2,1)}), bf16[2,8,768]{2,0,1:T(2,128)(2,1)}, u32[]{:S(2)}, u32[]{:S(2)}) async-start(bf16[2,8,768]{2,0,1:T(2,128)(2,1)} %copy.125), calls=%async_computation.4 | async-start | bytes 49152 | tf_op jit(solution)/shard_map/all_to_all | solution.py:48
  105.6 64.1 %reduce-scatter.5.cloned.1.call-start = ((), (), s32[]{:S(2)}) async-start(), calls=%async_computation.9 | async-start | bytes 245760 | tf_op jit(solution)/shard_map/reduce_scatter | solution.py:53
  131.6 15.6 %copy-start.17 = (bf16[1,768,768]{2,1,0:T(8,128)(2,1)S(1)}, bf16[1,768,768]{2,1,0:T(8,128)(2,1)}, u32[]{:S(2)}) copy-start(bf16[1,768,768]{2,1,0:T(8,128)(2,1)} %param.22) | copy-start | bytes 3538948
  145.3 2.5 copy-start.23
  149.5 4.1 copy-start.42
  149.5 26.3 %copy-start.43 = (f32[2,8,128]{2,1,0:T(8,128)S(1)}, f32[2,8,128]{2,1,0:T(8,128)}, u32[]{:S(2)}) copy-start(f32[2,8,128]{2,1,0:T(8,128)} %get-tuple-element.30) | copy-start | bytes 24580
  149.6 26.4 %copy-start.31 = (f32[512]{0:T(512)S(1)}, f32[512]{0:T(512)}, u32[]{:S(2)}) copy-start(f32[512]{0:T(512)} %broadcast_multiply_fusion.5) | copy-start | bytes 6148
  149.6 26.4 %copy-start.33 = (f32[512]{0:T(512)S(1)}, f32[512]{0:T(512)}, u32[]{:S(2)}) copy-start(f32[512]{0:T(512)} %broadcast_multiply_fusion.4) | copy-start | bytes 6148
  149.6 40.6 %reduce-scatter.3.cloned.1.call-start = ((), (), s32[]{:S(2)}) async-start(), calls=%async_computation.8 | async-start | bytes 245760 | tf_op jit(solution)/shard_map/reduce_scatter | solution.py:53
  153.6 80.1 %copy-start.36 = (f32[768]{0:T(1024)}, f32[768]{0:T(1024)S(1)}, u32[]{:S(2)}) copy-start(f32[768]{0:T(1024)S(1)} %get-tuple-element.95) | copy-start | bytes 9220
  172.2 20.0 %all-to-all-start.4 = ((bf16[8,2,768]{2,1,0:T(2,128)(2,1)}), bf16[8,2,768]{2,1,0:T(2,128)(2,1)S(1)}, u32[]{:S(2)}, u32[]{:S(2)}) async-start(bf16[8,2,768]{2,1,0:T(2,128)(2,1)} %reshape.213), calls=%async_computation.6 | async-start | bytes 49152 | tf_op jit(solution)/shard_map/all_to_all | solution.py:54
  176.0 57.7 %copy-start.38 = (f32[2,256]{1,0:T(2,128)}, f32[2,256]{1,0:T(2,128)S(1)}, u32[]{:S(2)}) copy-start(f32[2,256]{1,0:T(2,128)S(1)} %div.59) | copy-start | bytes 6148
  176.0 57.7 %copy-start.40 = (f32[2,256]{1,0:T(2,128)}, f32[2,256]{1,0:T(2,128)S(1)}, u32[]{:S(2)}) copy-start(f32[2,256]{1,0:T(2,128)S(1)} %rsqrt.25) | copy-start | bytes 6148
  181.6 15.3 %copy-start.29 = (f32[8,512]{1,0:T(8,128)S(1)}, f32[8,512]{1,0:T(8,128)}, u32[]{:S(2)}) copy-start(f32[8,512]{1,0:T(8,128)} %get-tuple-element.29) | copy-start | bytes 49156
  192.2 9.0 %all-to-all-start.1 = ((bf16[8,2,768]{2,1,0:T(2,128)(2,1)}), bf16[8,2,768]{2,1,0:T(2,128)(2,1)S(1)}, u32[]{:S(2)}, u32[]{:S(2)}) async-start(bf16[8,2,768]{2,1,0:T(2,128)(2,1)} %reshape.211), calls=%async_computation.2 | async-start | bytes 49152 | tf_op jit(solution)/shard_map/all_to_all | solution.py:54
  196.4 297.5 %all-reduce.3.cloned.1.call-start = ((), (), s32[]{:S(2)}) async-start(), calls=%async_computation.10 | async-start | bytes 19660800
  196.9 3.2 copy-start.28
  196.9 4.6 copy-start.9
  201.4 8.7 %copy-start.26 = (bf16[8,2,1,768]{3,1,0,2:T(2,128)(2,1)}, bf16[8,2,1,768]{3,1,0,2:T(2,128)(2,1)S(1)}, u32[]{:S(2)}) copy-start(bf16[8,2,1,768]{3,1,0,2:T(2,128)(2,1)S(1)} %all_to_all.83) | copy-start | bytes 73732
  217.6 3.1 copy-start.3
  217.6 3.1 copy-start.14
  226.6 2.2 copy-start.19
  226.6 7.1 %slice-start = ((s8[5111808]{0:T(1024)(128)(4,1)}), s8[4194304]{0:T(1024)(128)(4,1)S(1)}, s32[]{:S(2)}) async-start(s8[5111808]{0:T(1024)(128)(4,1)} %bitcast.226), calls=%async_computation.11 | async-start | bytes 8388608
  228.8 4.9 slice-start.1
  233.7 4.9 copy-start.35
  233.7 5.1 copy-start.34
  252.4 5.3 %copy-start.45 = (f32[2,256]{1,0:T(2,128)S(1)}, f32[2,256]{1,0:T(2,128)}, u32[]{:S(2)}) copy-start(f32[2,256]{1,0:T(2,128)} %get-tuple-element.91) | copy-start | bytes 6148
  252.4 5.3 %copy-start.44 = (f32[2,256]{1,0:T(2,128)S(1)}, f32[2,256]{1,0:T(2,128)}, u32[]{:S(2)}) copy-start(f32[2,256]{1,0:T(2,128)} %get-tuple-element.92) | copy-start | bytes 6148
  252.4 5.3 %copy-start.6 = (f32[2,256,768]{2,1,0:T(8,128)S(1)}, f32[2,256,768]{2,1,0:T(8,128)}, u32[]{:S(2)}) copy-start(f32[2,256,768]{2,1,0:T(8,128)} %copy-done.4) | copy-start | bytes 4718596
  252.4 5.3 %copy-start.37 = (f32[768]{0:T(1024)S(1)}, f32[768]{0:T(1024)}, u32[]{:S(2)}) copy-start(f32[768]{0:T(1024)} %copy-done.36) | copy-start | bytes 9220
  252.4 5.3 %copy-start.39 = (f32[2,256]{1,0:T(2,128)S(1)}, f32[2,256]{1,0:T(2,128)}, u32[]{:S(2)}) copy-start(f32[2,256]{1,0:T(2,128)} %copy-done.38) | copy-start | bytes 6148
  252.5 5.3 %copy-start.41 = (f32[2,256]{1,0:T(2,128)S(1)}, f32[2,256]{1,0:T(2,128)}, u32[]{:S(2)}) copy-start(f32[2,256]{1,0:T(2,128)} %copy-done.40) | copy-start | bytes 6148
  254.2 32.3 %all-to-all-start.2 = ((bf16[2,256,768]{2,0,1:T(2,128)(2,1)}), bf16[2,256,768]{2,0,1:T(2,128)(2,1)S(1)}, u32[]{:S(2)}, u32[]{:S(2)}) async-start(bf16[2,256,768]{2,0,1:T(2,128)(2,1)} %copy.123), calls=%async_computation.3 | async-start | bytes 1572864 | tf_op jit(solution)/shard_map/all_to_all | solution.py:44
  262.1 28.9 %copy-start.18 = (bf16[64,1,768]{2,0,1:T(8,128)(2,1)S(1)}, bf16[64,1,768]{2,0,1:T(8,128)(2,1)}, u32[]{:S(2)}) copy-start(bf16[64,1,768]{2,0,1:T(8,128)(2,1)} %all_gather.6) | copy-start | bytes 294916
  262.1 28.9 %copy-start.22 = (bf16[64,768]{1,0:T(8,128)(2,1)S(1)}, bf16[64,768]{1,0:T(8,128)(2,1)}, u32[]{:S(2)}) copy-start(bf16[64,768]{1,0:T(8,128)(2,1)} %copy-done.21) | copy-start | bytes 294916
  287.4 57.8 %all-to-all-start.5 = ((f32[2,256,768]{2,0,1:T(2,128)}), f32[2,256,768]{2,0,1:T(2,128)S(1)}, u32[]{:S(2)}, u32[]{:S(2)}) async-start(f32[2,256,768]{2,0,1:T(2,128)} %copy.140), calls=%async_computation.7 | async-start | bytes 3145728 | tf_op jit(solution)/shard_map/all_to_all | solution.py:44
  290.9 1.9 copy-start.16
  290.9 1.9 copy-start.24
  292.9 1.9 copy-start.13
  345.2 155.1 %copy-start.1 = (bf16[1,768,768]{2,1,0:T(8,128)(2,1)S(1)}, bf16[1,768,768]{2,1,0:T(8,128)(2,1)}, u32[]{:S(2)}) copy-start(bf16[1,768,768]{2,1,0:T(8,128)(2,1)} %param.21) | copy-start | bytes 3538948
  (9 other events, 9.3 us)
Sparse Core Ops, SparseCore 0:
  149.7 19.8 reduce-scatter.4
  172.6 17.5 reduce-scatter.2
  251.4 242.5 all-reduce.2

commit v3 on v1

--- a/solution.py
+++ b/solution.py
@@ -1,6 +1,8 @@
 import jax
 import jax.numpy as jnp
 from jax import lax
+from jax.experimental import pallas as pl
+from jax.experimental.pallas import tpu as pltpu
 from jax.sharding import PartitionSpec as P
 
 H = 12
@@ -166,12 +168,829 @@
     )
 
 
+MESH = pl.DeviceIdType.MESH
+VM = pltpu.VMEM
+SMALL = 256
+ROWS = 64
+
+
+def nt(a, b):
+    return lax.dot_general(a, b, (((1,), (1,)), ((), ())), preferred_element_type=F32)
+
+
+def tn(a, b):
+    return lax.dot_general(a, b, (((0,), (0,)), ((), ())), preferred_element_type=F32)
+
+
+def mm(a, b):
+    return jnp.dot(a, b, preferred_element_type=F32)
+
+
+def ds(start, size):
+    return pl.ds(pl.multiple_of(start, size), size)
+
+
+def remote(src, dst, send, recv, device):
+    return pltpu.make_async_remote_copy(
+        src_ref=src, dst_ref=dst, send_sem=send, recv_sem=recv, device_id=device,
+        device_id_type=MESH,
+    )
+
+
+def other(d, kind):
+    core, x, y = lax.rem(d, 2), lax.rem(d // 2, 2), d // 4
+    return {"x": d + 2 - 4 * x, "y": d + 4 - 8 * y, "core": d + 1 - 2 * core}[kind]
+
+
+def gather_steps(packed, stage, full, zsend, zrecv, send, recv):
+    d, z = lax.axis_index("dp"), lax.axis_index("seq")
+    dx, dy, dc = other(d, "x"), other(d, "y"), other(d, "core")
+    half = packed.shape[0]
+    rows = 2 * half
+    over_x, over_y, over_c = (dx, z), (dy, z), (dc, z)
+
+    def block(owner, part):
+        if part is None:
+            return full.at[ds(owner * rows, rows)]
+        return full.at[ds(owner * rows + part * half, half)]
+
+    first = [
+        remote(packed, stage.at[z], zsend.at[k - 1], zrecv.at[k - 1], (d, lax.rem(z + k, 4)))
+        for k in range(1, 4)
+    ]
+
+    def copy(n, owner, part, device):
+        ref = block(owner, part)
+        return remote(ref, ref, send.at[n], recv.at[n], device)
+
+    dd = other(dx, "y")
+    plan = [
+        copy(0, d, 0, over_x), copy(1, d, 1, over_y), copy(2, d, 1, over_x),
+        copy(3, d, 0, over_y), copy(4, d, None, over_c), copy(5, dx, 0, over_y),
+        copy(6, dy, 1, over_x), copy(7, dx, 0, over_c), copy(8, dy, 1, over_c),
+        copy(9, dx, 1, over_c), copy(10, dy, 0, over_c), copy(11, dd, 0, over_c),
+        copy(12, dd, 1, over_c),
+    ]
+    cx, cy = other(dc, "x"), other(dc, "y")
+    cd = other(cx, "y")
+    landing = [
+        (dx, 0), (dy, 1), (dx, 1), (dy, 0), (dc, None), (dd, 0), (dd, 1),
+        (cx, 0), (cy, 1), (cx, 1), (cy, 0), (cd, 0), (cd, 1),
+    ]
+
+    def arrived(n):
+        ref = block(*landing[n])
+        remote(ref, ref, send.at[n], recv.at[n], over_x).wait_recv()
+
+    def start():
+        for one in first:
+            one.start()
+
+    def assemble():
+        own = pltpu.make_async_copy(packed, stage.at[z], zrecv.at[3])
+        own.start()
+        own.wait()
+        for one in first:
+            one.wait_recv()
+        quarter, wide = packed.shape[0] // 2, packed.shape[1]
+        for side in range(2):
+            value = jnp.concatenate(
+                [
+                    stage[k].astype(F32)[side * quarter : (side + 1) * quarter]
+                    for k in range(4)
+                ],
+                axis=0,
+            )
+            full[ds(d * rows, rows), side * wide : (side + 1) * wide] = value.astype(BF)
+        for n in range(5):
+            plan[n].start()
+
+    def forward_one():
+        arrived(0)
+        plan[5].start()
+        plan[7].start()
+        arrived(1)
+        plan[6].start()
+        plan[8].start()
+
+    def forward_two():
+        arrived(2)
+        plan[9].start()
+        arrived(3)
+        plan[10].start()
+        arrived(5)
+        plan[11].start()
+        arrived(6)
+        plan[12].start()
+
+    def finish():
+        for n in (4, 7, 8, 9, 10, 11, 12):
+            arrived(n)
+        for one in first + plan:
+            one.wait_send()
+
+    return start, assemble, forward_one, forward_two, finish
+
+
+def image_steps(blocks, whole, send, recv, local_sem, images, home):
+    d, z = lax.axis_index("dp"), lax.axis_index("seq")
+    size = blocks.shape[1]
+    length = 4 * size
+
+    def make(i, k):
+        there = lax.rem(z + k, 4)
+        if home:
+            src = whole.at[ds(i * length + there * size, size)]
+            dst = blocks.at[z * images + i]
+        else:
+            src = blocks.at[there * images + i]
+            dst = whole.at[ds(i * length + z * size, size)]
+        if k == 0:
+            return pltpu.make_async_copy(src, dst, local_sem.at[i])
+        return remote(src, dst, send.at[i * 3 + k - 1], recv.at[i * 3 + k - 1], (d, there))
+
+    table = [[make(i, k) for k in range(4)] for i in range(images)]
+
+    def start(i):
+        for one in table[i]:
+            one.start()
+
+    def arrived(i):
+        table[i][0].wait()
+        for one in table[i][1:]:
+            one.wait_recv()
+
+    def sent():
+        for i in range(images):
+            for one in table[i][1:]:
+                one.wait_send()
+
+    return start, arrived, sent
+
+
+def swap_steps(src, dst, send, recv, to_expert):
+    d, z = lax.axis_index("dp"), lax.axis_index("seq")
+    count = dst.shape[0]
+    me = d * 4 + z
+
+    def start():
+        def one(k, carry):
+            j = lax.rem(me + k, count)
+            e = j // 4
+            row = src.at[e] if to_expert else src.at[j]
+            remote(row, dst.at[me], send, recv, (e, lax.rem(j, 4))).start()
+            return carry
+
+        lax.fori_loop(1, count, one, 0)
+        pltpu.make_async_copy(src.at[d] if to_expert else src.at[me], dst.at[me], recv).start()
+
+    def arrived():
+        pltpu.make_async_copy(dst, dst, recv).wait()
+
+    def sent():
+        part = dst.at[pl.ds(0, count - 1)]
+        remote(part, part, send, recv, (other(d, "x"), z)).wait_send()
+
+    return start, arrived, sent
+
+
+def reduce_steps(grads, pairs, inter, out_stage, in_stage, sems, chunk, lo, hi, emit):
+    d, z = lax.axis_index("dp"), lax.axis_index("seq")
+    dx, dy, dc = other(d, "x"), other(d, "y"), other(d, "core")
+    core = lax.rem(d, 2)
+    over_x, over_y, over_c = (dx, z), (dy, z), (dc, z)
+    rows = pairs.shape[1]
+    half, quarter = rows // 2, rows // 4
+    cols = slice(lo, hi)
+    send1, recv1, send2, recv2, send3, recv3 = sems
+    chips = pairs.shape[0]
+
+    step1 = []
+    for m in range(chips):
+        block = grads.at[ds((2 * m + 1 - core) * rows, rows), cols]
+        n = chunk * chips + m
+        step1.append(remote(block, pairs.at[m, :, cols], send1.at[n], recv1.at[n], over_c))
+    here, mx, my, md = d // 2, dx // 2, dy // 2, other(dx, "y") // 2
+
+    def part(m, h):
+        return pairs.at[m, h * half : (h + 1) * half, cols]
+
+    def hop(k, m, h, device):
+        n = chunk * 6 + k
+        return remote(part(m, h), inter.at[k, :, cols], send2.at[n], recv2.at[n], device)
+
+    step2 = [
+        hop(0, md, 0, over_y), hop(1, md, 1, over_x), hop(2, my, 0, over_y),
+        hop(3, mx, 1, over_x), hop(4, mx, 0, over_x), hop(5, my, 1, over_y),
+    ]
+    narrow = slice(lo // 2, hi // 2)
+    step3 = []
+    for k in range(1, 4):
+        n = chunk * 3 + k - 1
+        there = lax.rem(z + k, 4)
+        step3.append(
+            remote(
+                out_stage.at[there, :, narrow], in_stage.at[k - 1, :, narrow],
+                send3.at[n], recv3.at[n], (d, there),
+            )
+        )
+
+    def one():
+        for c in step1:
+            c.start()
+
+    def two():
+        for m in range(chips):
+            step1[m].wait_recv()
+            own = grads[ds((2 * m + core) * rows, rows), cols].astype(F32)
+            pairs[m, :, cols] = (own + pairs[m, :, cols].astype(F32)).astype(BF)
+        for k in range(4):
+            step2[k].start()
+
+    def three():
+        for k, m, h in ((0, mx, 0), (1, my, 1)):
+            step2[k].wait_recv()
+            at = slice(h * half, (h + 1) * half)
+            total = pairs[m, at, cols].astype(F32) + inter[k, :, cols].astype(F32)
+            pairs[m, at, cols] = total.astype(BF)
+            step2[4 + k].start()
+
+    def four():
+        for k in (2, 3, 4, 5):
+            step2[k].wait_recv()
+        own = pairs[here, :, cols].astype(F32)
+        top = own[:half] + inter[2, :, cols].astype(F32) + inter[4, :, cols].astype(F32)
+        low = own[half:] + inter[3, :, cols].astype(F32) + inter[5, :, cols].astype(F32)
+        total = jnp.concatenate([top, low], axis=0)
+        middle = (hi - lo) // 2
+        for t in range(4):
+            shard = total[t * quarter : (t + 1) * quarter]
+            both = jnp.concatenate([shard[:, :middle], shard[:, middle:]], axis=0)
+            out_stage[t, :, narrow] = both.astype(BF)
+        for c in step3:
+            c.start()
+
+    def five():
+        total = out_stage[z, :, narrow].astype(F32)
+        for k in range(3):
+            step3[k].wait_recv()
+            total = total + in_stage[k, :, narrow].astype(F32)
+        emit(jnp.concatenate([total[:quarter], total[quarter:]], axis=1))
+
+    def sent():
+        for c in step1 + step2 + step3:
+            c.wait_send()
+
+    return one, two, three, four, five, sent
+
+
+def unit_rows(x):
+    centred = x - jnp.mean(x, axis=-1, keepdims=True)
+    inverse = lax.rsqrt(jnp.mean(centred * centred, axis=-1, keepdims=True) + 1e-06)
+    return centred * inverse, inverse
+
+
+def fold_rows(x):
+    total = x[:8]
+    for k in range(1, x.shape[0] // 8):
+        total = total + x[8 * k : 8 * (k + 1)]
+    return total
+
+
+def norm_rows_back(grad, unit, inverse, gain):
+    scaled = grad * gain
+    centred = scaled - jnp.mean(scaled, axis=-1, keepdims=True)
+    correction = unit * jnp.mean(scaled * unit, axis=-1, keepdims=True)
+    return inverse * (centred - correction)
+
+
+def split_heads(pair):
+    lane = lax.broadcasted_iota(jnp.int32, (1, 2 * HD), 1)
+    left = jnp.where(lane < HD, 1.0, 0.0)
+    return jnp.concatenate([pair * left.astype(BF), pair * (1.0 - left).astype(BF)], axis=0)
+
+
+def join_heads(pair):
+    lane = lax.broadcasted_iota(jnp.int32, (1, 2 * HD), 1)
+    rows = pair.shape[0] // 2
+    return jnp.where(lane < HD, pair[:rows], pair[rows:])
+
+
+def gelu_parts(v):
+    inner = jnp.tanh(0.7978845608 * (v + 0.044715 * v * v * v))
+    slope = 0.5 * (1.0 + inner) + 0.5 * v * (1.0 - inner * inner) * 0.7978845608 * (
+        1.0 + 3.0 * 0.044715 * v * v
+    )
+    return 0.5 * v * (1.0 + inner), slope
+
+
+def block_kernel(
+    lengths, w_qkv, w_out, smalls, tokens, cotangent, w_up, w_down,
+    block_out, grad_input, grad_qkv, grad_out_w, grad_small, grad_up, grad_down,
+    packed, stage, full, small, xs, cots, qkv, probs, attended, middle, n_one, n_two,
+    disp, comb, dcomb, slots, bias, up, down, out_rows, pair_in, pair_out, row_sums,
+    recv_a, recv_b, recv_c, recv_d, send_b, send_d, turned_one, turned_att,
+    d_norm, d_diff, d_branch, d_attended, d_qkv, g_rows, g_blocks, cot_home,
+    grads, pairs_buf, inter, out_stage, in_stage,
+    zsend, zrecv, wsend, wrecv, tsend, trecv, csend, crecv, bsend, brecv, gsend, grecv,
+    local, loads, swap_send, swap_recv, send1, recv1, send2, recv2, send3, recv3,
+):
+    d, z = lax.axis_index("dp"), lax.axis_index("seq")
+    width = tokens.shape[2]
+    images = tokens.shape[0] // 4
+    length = 4 * tokens.shape[1]
+    count = images * length
+    groups = width // 256
+    experts = disp.shape[0]
+    devices = recv_a.shape[0]
+    me = d * 4 + z
+
+    barrier = pltpu.get_barrier_semaphore()
+
+    def greet(k, carry):
+        j = lax.rem(me + k, devices)
+        pl.semaphore_signal(
+            barrier, inc=1, device_id=(j // 4, lax.rem(j, 4)), device_id_type=MESH
+        )
+        return carry
+
+    lax.fori_loop(1, devices, greet, 0)
+    load_up = pltpu.make_async_copy(w_up.at[0], up, loads.at[0])
+    load_down = pltpu.make_async_copy(w_down.at[0], down, loads.at[1])
+    load_home = pltpu.make_async_copy(cotangent, cot_home, loads.at[2])
+    for load in (load_up, load_down, load_home):
+        load.start()
+    own = w_qkv[...]
+    pieces = [w_out[...]]
+    for g in range(groups):
+        for k in range(3):
+            pieces.append(own[:, k * width + g * 256 : k * width + (g + 1) * 256])
+    pieces.append(smalls[...])
+    line = jnp.concatenate([piece.astype(F32) for piece in pieces], axis=1)
+    wide = packed.shape[1]
+    packed[...] = jnp.concatenate([line[:, :wide], line[:, wide:]], axis=0).astype(BF)
+    pl.semaphore_wait(barrier, devices - 1)
+
+    w_start, w_assemble, w_one, w_two, w_finish = gather_steps(
+        packed, stage, full, zsend, zrecv, wsend, wrecv
+    )
+    t_start, t_arrived, t_sent = image_steps(tokens, xs, tsend, trecv, local, images, False)
+    c_start, c_arrived, c_sent = image_steps(cotangent, cots, csend, crecv, local, images, False)
+    w_start()
+    for i in range(images):
+        t_start(i)
+    w_assemble()
+    w_one()
+    w_two()
+    for i in range(images):
+        t_arrived(i)
+    for i in range(images):
+        c_start(i)
+    w_finish()
+    small[...] = full[:, 4 * width : 4 * width + 128].astype(F32).T[:16]
+    gains = [small[8 + k : 9 + k, :] for k in range(4)]
+
+    def norm_one(k, carry):
+        at = ds(k * ROWS, ROWS)
+        unit, _ = unit_rows(xs[at, :].astype(F32))
+        n_one[at, :] = (unit * gains[0] + gains[1]).astype(BF)
+        return carry
+
+    lax.fori_loop(0, count // ROWS, norm_one, 0)
+
+    def project(k, carry):
+        qkv[:, ds(k * 256, 256)] = mm(n_one[...], full[:, ds(width + k * 256, 256)]).astype(BF)
+        return carry
+
+    lax.fori_loop(0, 3 * groups, project, 0)
+
+    key = lax.broadcasted_iota(jnp.int32, (1, length), 1)
+    for i in range(images):
+        bias[i] = jnp.where(key < lengths[z * images + i], 0.0, -1000000000.0)
+    scale = jnp.asarray(HD ** (-0.5), BF)
+
+    def heads(t):
+        i, p = lax.rem(t, images), t // images
+        base = (p // 2) * 768 + lax.rem(p, 2) * 128
+        return i, p, ds(i * length, length), base
+
+    def attend(t, carry):
+        i, p, at, base = heads(t)
+        keys = split_heads(qkv[at, ds(base + 256, 128)])
+        values = split_heads(qkv[at, ds(base + 512, 128)])
+        scores = nt(qkv[at, ds(base, 128)] * scale, keys)
+        for h in range(2):
+            part = scores[:, h * length : (h + 1) * length] + bias[i]
+            e = jnp.exp(part - jnp.max(part, axis=-1, keepdims=True))
+            total = jnp.sum(e, axis=-1, keepdims=True)
+            probs[t, :, h * length : (h + 1) * length] = (e * (1.0 / total)).astype(BF)
+        attended[at, ds(p * 128, 128)] = mm(probs[t], values).astype(BF)
+        return carry
+
+    lax.fori_loop(0, images * 2 * groups, attend, 0)
+
+    def project_out(k, carry):
+        at = ds(k * 256, 256)
+        middle[:, at] = xs[:, at].astype(F32) + mm(attended[...], full[:, at])
+        return carry
+
+    lax.fori_loop(0, groups, project_out, 0)
+
+    def norm_two(k, carry):
+        at = ds(k * ROWS, ROWS)
+        unit, _ = unit_rows(middle[at, :])
+        n_two[at, :] = (unit * gains[2] + gains[3]).astype(BF)
+        return carry
+
+    lax.fori_loop(0, count // ROWS, norm_two, 0)
+    router = small[0:8, :].astype(BF)
+    spans = [slice(i * length, (i + 1) * length) for i in range(images)]
+    denominators = []
+    for i, at in enumerate(spans):
+        logits = nt(router, n_two[at, :])
+        inside = key < lengths[z * images + i]
+        top = jnp.floor(
+            jnp.max(jnp.where(inside, logits, -1000000000.0), axis=-1, keepdims=True)
+        )
+        dispatch = jnp.where(inside, jnp.exp(logits - top), 0.0)
+        e = jnp.exp(logits - jnp.max(logits, axis=0, keepdims=True))
+        disp[:, at] = dispatch
+        comb[:, at] = e / jnp.sum(e, axis=0, keepdims=True)
+        denominators.append(jnp.sum(dispatch, axis=-1, keepdims=True))
+        slots[i] = mm(dispatch.astype(BF), n_two[at, :]) / denominators[i]
+
+    swap_a = swap_steps(pair_in.at[0], recv_a, swap_send.at[0], swap_recv.at[0], True)
+    swap_b = swap_steps(send_b, recv_b, swap_send.at[1], swap_recv.at[1], False)
+    swap_c = swap_steps(pair_in.at[1], recv_c, swap_send.at[2], swap_recv.at[2], True)
+    swap_d = swap_steps(send_d, recv_d, swap_send.at[3], swap_recv.at[3], False)
+
+    def to_pairs(which, values):
+        for e in range(experts):
+            pair_in[which, e] = jnp.concatenate(
+                [value[e : e + 1] for value in values], axis=0
+            ).astype(BF)
+
+    def from_pairs(ref):
+        for j in range(devices):
+            row_sums[images * j : images * (j + 1), :] = ref[j].astype(F32)
+        return row_sums[...].astype(BF)
+
+    def spread(ref, value):
+        row_sums[...] = value
+        for j in range(devices):
+            ref[j] = row_sums[images * j : images * (j + 1), :].astype(BF)
+
+    def collect(ref):
+        for e in range(experts):
+            total = ref[4 * e].astype(F32)
+            for k in range(1, 4):
+                total = total + ref[4 * e + k].astype(F32)
+            for i in range(images):
+                pair_out[i, e : e + 1, :] = total[i : i + 1]
+        return [pair_out[i].astype(BF) for i in range(images)]
+
+    to_pairs(0, [slots[i] for i in range(images)])
+    swap_a[0]()
+    for i in range(images):
+        c_arrived(i)
+    turned_one[...] = n_one[...].T
+    load_up.wait()
+    load_down.wait()
+    swap_a[1]()
+    rows_low = from_pairs(recv_a)
+    hidden = mm(rows_low, up[...])
+    active, slope = gelu_parts(hidden)
+    active = active.astype(BF)
+    spread(send_b, mm(active, down[...]))
+    swap_b[0]()
+    turned_att[...] = attended[...].T
+    swap_b[1]()
+    outs = collect(recv_b)
+    combs = [comb[:, at].astype(BF) for at in spans]
+    sends = []
+    for i, at in enumerate(spans):
+        sends.append(mm(combs[i], cots[at, :]))
+        dcomb[:, at] = nt(outs[i], cots[at, :])
+    to_pairs(1, sends)
+    swap_c[0]()
+    b_start, b_arrived, b_sent = image_steps(
+        block_out, out_rows, bsend, brecv, local, images, True
+    )
+    for i, at in enumerate(spans):
+        for k in range(groups):
+            cut = slice(k * 256, (k + 1) * 256)
+            moe = tn(combs[i], outs[i][:, cut])
+            out_rows[at, cut] = (middle[at, cut] + moe).astype(BF)
+    swap_c[1]()
+    d_rows = from_pairs(recv_c)
+    d_active = nt(d_rows, down[...])
+    d_hidden = (d_active * slope).astype(BF)
+    spread(send_d, nt(d_hidden, up[...]))
+    swap_d[0]()
+    grad_down[0] = tn(active, d_rows)
+    grad_up[0] = tn(rows_low, d_hidden)
+    swap_d[1]()
+    for i in range(images):
+        b_start(i)
+    d_slots = collect(recv_d)
+
+    router_grad = jnp.zeros((experts, width), F32)
+    for i, at in enumerate(spans):
+        wide_slots = d_slots[i].astype(F32)
+        inner = jnp.sum(slots[i] * wide_slots, axis=-1, keepdims=True)
+        projected = nt(d_slots[i], n_two[at, :])
+        weight, change = comb[:, at], dcomb[:, at]
+        d_logits = (projected - inner) / denominators[i] * disp[:, at]
+        d_logits = d_logits + weight * (
+            change - jnp.sum(weight * change, axis=0, keepdims=True)
+        )
+        router_grad = router_grad + mm(d_logits.astype(BF), n_two[at, :])
+        scaled = wide_slots / denominators[i]
+        high = scaled.astype(BF).astype(F32)
+        left = jnp.concatenate(
+            [disp[:, at], disp[:, at], d_logits, jnp.zeros_like(d_logits)], axis=0
+        ).astype(BF)
+        right = jnp.concatenate(
+            [high, scaled - high, small[0:8, :], jnp.zeros_like(scaled)], axis=0
+        ).astype(BF)
+        for k in range(groups):
+            cut = slice(k * 256, (k + 1) * 256)
+            d_norm[at, cut] = tn(left, right[:, cut])
+
+    nothing = jnp.zeros((8, width), F32)
+
+    def back_two(k, carry):
+        at = ds(k * ROWS, ROWS)
+        grad = d_norm[at, :]
+        unit, inverse = unit_rows(middle[at, :])
+        change = norm_rows_back(grad, unit, inverse, gains[2])
+        d_diff[at, :] = change
+        d_branch[at, :] = (change + cots[at, :].astype(F32)).astype(BF)
+        return carry[0] + fold_rows(grad * unit), carry[1] + fold_rows(grad)
+
+    gain_two, shift_two = lax.fori_loop(0, count // ROWS, back_two, (nothing, nothing))
+
+    def emit_out(value):
+        grad_out_w[...] = value
+
+    def emit_group(g):
+        def emit(value):
+            for k in range(3):
+                grad_qkv[:, k * width + g * 256 : k * width + (g + 1) * 256] = value[
+                    :, k * 256 : (k + 1) * 256
+                ]
+            if value.shape[1] > 768:
+                grad_small[...] = value[:, 768:896]
+
+        return emit
+
+    sems = (send1, recv1, send2, recv2, send3, recv3)
+    chunks = []
+    for c in range(groups + 1):
+        hi = grads.shape[1] if c == groups else (c + 1) * 768
+        emit = emit_out if c == 0 else emit_group(c - 1)
+        chunks.append(
+            reduce_steps(
+                grads, pairs_buf, inter, out_stage, in_stage, sems, c, c * 768, hi, emit
+            )
+        )
+
+    def grad_out(k, carry):
+        at = ds(k * 256, 256)
+        grads[:, at] = mm(turned_att[...], d_branch[:, at]).astype(BF)
+        return carry
+
+    lax.fori_loop(0, groups, grad_out, 0)
+    chunks[0][0]()
+
+    def back_out(k, carry):
+        at = ds(k * 256, 256)
+        d_attended[:, at] = nt(d_branch[...], full[at, 0:width]).astype(BF)
+        return carry
+
+    lax.fori_loop(0, groups, back_out, 0)
+
+    def attend_back(t, carry):
+        i, p, at, base = heads(t)
+        q = qkv[at, ds(base, 128)] * scale
+        keys = split_heads(qkv[at, ds(base + 256, 128)])
+        values = split_heads(qkv[at, ds(base + 512, 128)])
+        grad = d_attended[at, ds(p * 128, 128)]
+        d_values = join_heads(tn(probs[t], grad))
+        d_probs = nt(grad, values)
+        cuts = []
+        for h in range(2):
+            cut = slice(h * length, (h + 1) * length)
+            weight = probs[t, :, cut].astype(F32)
+            change = weight * d_probs[:, cut]
+            total = jnp.sum(change, axis=-1, keepdims=True)
+            cuts.append((change - weight * total).astype(BF))
+        d_scores = jnp.concatenate(cuts, axis=1)
+        d_qkv[at, ds(base, 128)] = (mm(d_scores, keys) * HD ** (-0.5)).astype(BF)
+        d_qkv[at, ds(base + 256, 128)] = join_heads(tn(d_scores, q)).astype(BF)
+        d_qkv[at, ds(base + 512, 128)] = d_values.astype(BF)
+        return carry
+
+    def group_grads(g):
+        def one(k, carry):
+            at = ds(g * 768 + k * 256, 256)
+            to = ds(width + g * 768 + k * 256, 256)
+            grads[:, to] = mm(turned_one[...], d_qkv[:, at]).astype(BF)
+            return carry
+
+        lax.fori_loop(0, 3, one, 0)
+
+    per_group = 2 * images
+    lax.fori_loop(0, per_group, attend_back, 0)
+    chunks[0][1]()
+    group_grads(0)
+    chunks[1][0]()
+    lax.fori_loop(per_group, 2 * per_group, attend_back, 0)
+    chunks[0][2]()
+    chunks[1][1]()
+    group_grads(1)
+    chunks[2][0]()
+    lax.fori_loop(2 * per_group, 3 * per_group, attend_back, 0)
+    chunks[0][3]()
+    chunks[1][2]()
+    chunks[2][1]()
+
+    def back_qkv(k, carry):
+        at = ds(k * 256, 256)
+        d_norm[:, at] = nt(d_qkv[...], full[at, width : 4 * width])
+        return carry
+
+    lax.fori_loop(0, groups, back_qkv, 0)
+
+    def back_one(k, carry):
+        at = ds(k * ROWS, ROWS)
+        grad = d_norm[at, :]
+        unit, inverse = unit_rows(xs[at, :].astype(F32))
+        change = norm_rows_back(grad, unit, inverse, gains[0])
+        g_rows[at, :] = (change + d_diff[at, :]).astype(BF)
+        return carry[0] + fold_rows(grad * unit), carry[1] + fold_rows(grad)
+
+    gain_one, shift_one = lax.fori_loop(0, count // ROWS, back_one, (nothing, nothing))
+    g_start, g_arrived, g_sent = image_steps(g_blocks, g_rows, gsend, grecv, local, images, True)
+    for i in range(images):
+        b_arrived(i)
+        g_start(i)
+    sums = [
+        jnp.sum(value, axis=0, keepdims=True)
+        for value in (gain_one, shift_one, gain_two, shift_two)
+    ]
+    tall = jnp.concatenate(
+        [router_grad] + sums + [jnp.zeros((128 - experts - 4, width), F32)], axis=0
+    )
+    grads[:, 4 * width : 4 * width + 128] = tall.T.astype(BF)
+    grads[:, 4 * width + 128 :] = jnp.zeros((width, SMALL - 128), BF)
+    group_grads(2)
+    chunks[3][0]()
+    chunks[1][3]()
+    chunks[2][2]()
+    chunks[3][1]()
+    chunks[0][4]()
+    chunks[2][3]()
+    chunks[1][4]()
+    chunks[3][2]()
+    chunks[3][3]()
+    chunks[2][4]()
+    for i in range(images):
+        g_arrived(i)
+        for s in range(4):
+            j = s * images + i
+            grad_input[j] = g_blocks[j].astype(F32) + 0.0
+    load_home.wait()
+    for j in range(4 * images):
+        grad_input[j] = grad_input[j] + cot_home[j].astype(F32)
+    chunks[3][4]()
+    t_sent()
+    c_sent()
+    b_sent()
+    g_sent()
+    for swap in (swap_a, swap_b, swap_c, swap_d):
+        swap[2]()
+    for chunk in chunks:
+        chunk[5]()
+
+
+def kernel_plan(
+    tokens, lengths, w_qkv, w_out, router, gain_one, shift_one, gain_two, shift_two,
+    w_up, w_down, cotangent,
+):
+    own_rows, width = w_out.shape
+    images, size = tokens.shape[0] // 4, tokens.shape[1]
+    length, experts = 4 * size, router.shape[1]
+    count = images * length
+    groups = width // 256
+    pairs = 2 * groups
+    devices = 4 * experts
+    columns = 4 * width + SMALL
+    fan = w_up.shape[2]
+    vectors = jnp.stack([gain_one, shift_one, gain_two, shift_two], axis=1)
+    filler = jnp.zeros((own_rows, SMALL - experts - 4), BF)
+    smalls = jnp.concatenate([router, vectors, filler], axis=1)
+
+    def shape(*dims, kind=F32):
+        return jax.ShapeDtypeStruct(dims, kind)
+
+    outs = (
+        shape(*tokens.shape, kind=BF),
+        shape(*tokens.shape),
+        shape(own_rows, 3 * width),
+        shape(own_rows, width),
+        shape(own_rows, 128),
+        shape(*w_up.shape),
+        shape(*w_down.shape),
+    )
+    dma = pltpu.SemaphoreType.DMA
+    vmem, anywhere = pl.BlockSpec(memory_space=VM), pl.BlockSpec(memory_space=pl.ANY)
+    quarter = 4 * own_rows
+    pair = (images, width)
+    scratch = [
+        VM((2 * own_rows, columns // 2), BF),
+        VM((4, 2 * own_rows, columns // 2), BF),
+        VM((width, columns), BF),
+        VM((16, width), F32),
+        VM((count, width), BF),
+        VM((count, width), BF),
+        VM((count, 3 * width), BF),
+        VM((images * pairs, length, 2 * length), BF),
+        VM((count, width), BF),
+        VM((count, width), F32),
+        VM((count, width), BF),
+        VM((count, width), BF),
+        VM((experts, count), F32),
+        VM((experts, count), F32),
+        VM((experts, count), F32),
+        VM((images, experts, width), F32),
+        VM((images, 1, length), F32),
+        VM((width, fan), BF),
+        VM((fan, width), BF),
+        VM((count, width), BF),
+        VM((2, experts) + pair, BF),
+        VM((images, experts, width), F32),
+        VM((devices * images, width), F32),
+        VM((devices,) + pair, BF),
+        VM((devices,) + pair, BF),
+        VM((devices,) + pair, BF),
+        VM((devices,) + pair, BF),
+        VM((devices,) + pair, BF),
+        VM((devices,) + pair, BF),
+        VM((width, count), BF),
+        VM((width, count), BF),
+        VM((count, width), F32),
+        VM((count, width), F32),
+        VM((count, width), BF),
+        VM((count, width), BF),
+        VM((count, 3 * width), BF),
+        VM((count, width), BF),
+        VM(tokens.shape, BF),
+        VM(tokens.shape, BF),
+        VM((width, columns), BF),
+        VM((4, quarter, columns), BF),
+        VM((6, quarter // 2, columns), BF),
+        VM((4, 2 * own_rows, columns // 2), BF),
+        VM((3, 2 * own_rows, columns // 2), BF),
+    ]
+    scratch += [dma((3,)), dma((4,)), dma((13,)), dma((13,))]
+    scratch += [dma((3 * images,))] * 8
+    scratch += [dma((images,)), dma((3,)), dma((4,)), dma((4,))]
+    chunks = groups + 1
+    scratch += [dma((4 * chunks,))] * 2 + [dma((6 * chunks,))] * 2 + [dma((3 * chunks,))] * 2
+    block_out, grad_input, grad_qkv, grad_out_w, grad_small, grad_up, grad_down = pl.pallas_call(
+        block_kernel,
+        out_shape=outs,
+        in_specs=[pl.BlockSpec(memory_space=pltpu.SMEM)] + [vmem] * 3 + [anywhere] * 4,
+        out_specs=[anywhere] + [vmem] * 6,
+        scratch_shapes=scratch,
+        compiler_params=pltpu.CompilerParams(
+            collective_id=0, has_side_effects=True, vmem_limit_bytes=63 * 2**20
+        ),
+        name="block",
+    )(lengths, w_qkv, w_out, smalls, tokens, cotangent, w_up, w_down)
+    return (
+        block_out,
+        grad_input,
+        grad_qkv,
+        grad_out_w,
+        grad_small[:, :experts],
+        grad_small[:, experts],
+        grad_small[:, experts + 1],
+        grad_small[:, experts + 2],
+        grad_small[:, experts + 3],
+        grad_up,
+        grad_down,
+    )
+
+
 def solution(mesh):
+    plan = kernel_plan if dict(mesh.shape) == {"dp": 8, "seq": 4} else plain_plan
     rows, vector = P(("dp", "seq"), None), P(("dp", "seq"))
     tokens = P("dp", "seq", None)
     up, down = P("dp", None, "seq"), P("dp", "seq", None)
     return jax.shard_map(
-        plain_plan,
+        plan,
         mesh=mesh,
         in_specs=(tokens, P("dp"), rows, rows, rows)
         + (vector,) * 4

time: 539 us -> 169 us (0.31)
  waiting for transfers between devices: 320 us -> 0 us
  Pallas kernels: 0 us -> 152 us
  matrix products: 65.4 us -> 0 us
  local copies, waits for them, and re-layouts: 53.6 us -> 16 us
  starting transfers between devices: 33.1 us -> 0 us
  blocking collectives: 27.8 us -> 0 us
  other arithmetic: 22.2 us -> 0 us
  between operations: 14.7 us -> 0.67 us
    pallas_call x0 -> x1, Pallas kernels: none -> 152 us  [kernel_plan(): pl.pallas_call(block_kernel, out_shape=outs, in_specs=[pl.BlockSpec(memor...]
    unnamed x5 -> x0, waiting for transfers between devices: 148 us -> none
    all_to_all x8 -> x0, waiting for transfers between devices: 122 us -> none  [the longest x2 73.4 us: to_blocks(): return lax.all_to_all(array, 'seq', split_axis=1, concat_axis=0, tiled=True)]
    dot_general x28 -> x0, matrix products: 65.4 us -> none  [dot(): return jnp.einsum(spec, a, b, preferred_element_type=F32)]
    all_to_all x8 -> x0, starting transfers between devices: 32.8 us -> none  [the longest x2 10.5 us: to_images(): return lax.all_to_all(array, 'seq', split_axis=0, concat_axis=1, tiled=True)]
    reduce_scatter x2 -> x0, waiting for transfers between devices: 30.2 us -> none  [from_experts(): lax.psum_scatter(rows, 'seq', scatter_dimension=0, tiled=True).astype(BF)]
    all_gather x2 -> x0, blocking collectives: 27.8 us -> none  [to_experts(): return lax.all_gather(rows, 'seq', axis=0, tiled=True)]
    all_gather x1 -> x0, waiting for transfers between devices: 19.7 us -> none  [plain_plan(): packed = lax.all_gather(packed, ('dp', 'seq'), axis=0, tiled=True)]
  transfers between devices with their start and end apart: 12 -> 0, of which waited for: 10 -> 0; matrix products, arithmetic and copies ran while one was open for 6% -> 0% of each run, Pallas kernels for 0% -> 0%
where the time goes in v3:
time: 169 us
  Pallas kernels  152 us (90%)
  local copies, waits for them, and re-layouts  16 us (9%)
    pallas_call x1, Pallas kernels, kernel_plan(): pl.pallas_call(block_kernel, out_shape=outs, in_specs=[pl.BlockSpec(memor...  152 us
    unnamed x18, local copies, waits for them, and re-layouts  10.7 us

profile of v3, /device:TPU:0, one launch (start us, length us, event | category | flops | bytes accessed | tf_op | source)
XLA Modules:
  0.0 169.0 jit_solution(4211525506427190797)
XLA Ops:
  0.6 0.8 copy.29
  1.4 0.7 copy.30
  2.2 0.7 copy.31
  2.9 0.7 copy.32
  3.6 0.7 copy.33
  4.4 0.7 concatenate.3.smalls
  5.1 152.2 %block.1 = (bf16[8,64,768]{2,1,0:T(8,128)(2,1)}, f32[8,64,768]{2,1,0:T(8,128)}, f32[24,2304]{1,0:T(8,128)}, f32[24,768]{1,0:T(8,128)}, f32[24,128]{1,0:T(8,128)}...) custom-call(s32[8]{0:T(128)} %lengths.1, bf16[24,2304]{1,0:T(8,128)(2,1)} %w_qkv.1, bf16[24,768]{1,0:T(8,128)(2,1)} %w_out.1, ...), custom_call_target="tpu_custom_call" | custom-call | tf_op jit(solution)/shard_map/block/pallas_call | solution.py:961
  157.3 0.0 copy-start.2
  157.4 1.6 slice_reduce_fusion
  159.0 1.4 copy.34
  160.3 0.0 copy-start.3
  160.3 0.0 copy-start.4
  160.3 0.0 copy-start.1
  160.3 2.2 %copy.41 = bf16[8,64,768]{2,1,0:T(8,128)(2,1)} copy(bf16[8,64,768]{2,1,0:T(8,128)(2,1)} %get-tuple-element.62) | data formatting | bytes 1572864
  162.6 0.0 copy-done.2
  162.6 1.1 copy.42
  163.7 0.0 copy-done.3
  163.7 0.7 copy.43
  164.4 0.0 copy-done.4
  164.4 0.6 copy.44
  165.0 0.0 copy-done.1
  165.0 0.0 copy-start
  165.0 1.4 copy.45
  166.4 1.1 copy-done
  167.5 1.4 copy.46
  (1 shorter events, 0.0 us)
Async XLA Ops:
  157.3 5.2 %copy-start.2 = (f32[8,64,768]{2,1,0:T(8,128)S(1)}, f32[8,64,768]{2,1,0:T(8,128)}, u32[]{:S(2)}) copy-start(f32[8,64,768]{2,1,0:T(8,128)} %get-tuple-element.63) | copy-start | bytes 4718596
  160.3 3.4 %copy-start.3 = (f32[24,2304]{1,0:T(8,128)S(1)}, f32[24,2304]{1,0:T(8,128)}, u32[]{:S(2)}) copy-start(f32[24,2304]{1,0:T(8,128)} %get-tuple-element.64) | copy-start | bytes 663556
  160.3 4.1 %copy-start.4 = (f32[24,768]{1,0:T(8,128)S(1)}, f32[24,768]{1,0:T(8,128)}, u32[]{:S(2)}) copy-start(f32[24,768]{1,0:T(8,128)} %get-tuple-element.65) | copy-start | bytes 221188
  160.3 4.7 %copy-start.1 = (f32[1,768,768]{2,1,0:T(8,128)S(1)}, f32[1,768,768]{2,1,0:T(8,128)}, u32[]{:S(2)}) copy-start(f32[1,768,768]{2,1,0:T(8,128)} %get-tuple-element.71) | copy-start | bytes 7077892
  165.0 2.5 %copy-start = (f32[1,768,768]{2,1,0:T(8,128)S(1)}, f32[1,768,768]{2,1,0:T(8,128)}, u32[]{:S(2)}) copy-start(f32[1,768,768]{2,1,0:T(8,128)} %get-tuple-element.72) | copy-start | bytes 7077892

commit v4 on v3

--- a/solution.py
+++ b/solution.py
@@ -170,7 +170,7 @@
 
 MESH = pl.DeviceIdType.MESH
 VM = pltpu.VMEM
-SMALL = 256
+SMALL = 128
 ROWS = 64
 
 
@@ -186,8 +186,8 @@
     return jnp.dot(a, b, preferred_element_type=F32)
 
 
-def ds(start, size):
-    return pl.ds(pl.multiple_of(start, size), size)
+def ds(start, size, unit=None):
+    return pl.ds(pl.multiple_of(start, unit or size), size)
 
 
 def remote(src, dst, send, recv, device):
@@ -202,25 +202,26 @@
     return {"x": d + 2 - 4 * x, "y": d + 4 - 8 * y, "core": d + 1 - 2 * core}[kind]
 
 
-def gather_steps(packed, stage, full, zsend, zrecv, send, recv):
+def gather_steps(stage, full, lo, hi, zsend, zrecv, send, recv, first_sem):
     d, z = lax.axis_index("dp"), lax.axis_index("seq")
     dx, dy, dc = other(d, "x"), other(d, "y"), other(d, "core")
-    half = packed.shape[0]
+    half = stage.shape[1]
     rows = 2 * half
     over_x, over_y, over_c = (dx, z), (dy, z), (dc, z)
 
     def block(owner, part):
         if part is None:
-            return full.at[ds(owner * rows, rows)]
-        return full.at[ds(owner * rows + part * half, half)]
-
-    first = [
-        remote(packed, stage.at[z], zsend.at[k - 1], zrecv.at[k - 1], (d, lax.rem(z + k, 4)))
-        for k in range(1, 4)
-    ]
+            return full.at[ds(owner * rows, rows), lo:hi]
+        return full.at[ds(owner * rows + part * half, half), lo:hi]
+
+    mine = stage.at[z]
+    first = []
+    for k in range(1, 4):
+        n = first_sem * 3 + k - 1
+        first.append(remote(mine, mine, zsend.at[n], zrecv.at[n], (d, lax.rem(z + k, 4))))
 
     def copy(n, owner, part, device):
-        ref = block(owner, part)
+        ref, n = block(owner, part), n + 13 * first_sem
         return remote(ref, ref, send.at[n], recv.at[n], device)
 
     dd = other(dx, "y")
@@ -239,7 +240,7 @@
     ]
 
     def arrived(n):
-        ref = block(*landing[n])
+        ref, n = block(*landing[n]), n + 13 * first_sem
         remote(ref, ref, send.at[n], recv.at[n], over_x).wait_recv()
 
     def start():
@@ -247,12 +248,9 @@
             one.start()
 
     def assemble():
-        own = pltpu.make_async_copy(packed, stage.at[z], zrecv.at[3])
-        own.start()
-        own.wait()
         for one in first:
             one.wait_recv()
-        quarter, wide = packed.shape[0] // 2, packed.shape[1]
+        quarter, wide = half // 2, stage.shape[2]
         for side in range(2):
             value = jnp.concatenate(
                 [
@@ -261,7 +259,8 @@
                 ],
                 axis=0,
             )
-            full[ds(d * rows, rows), side * wide : (side + 1) * wide] = value.astype(BF)
+            base = lo + side * wide
+            full[ds(d * rows, rows), base : base + wide] = value.astype(BF)
         for n in range(5):
             plan[n].start()
 
@@ -286,10 +285,12 @@
     def finish():
         for n in (4, 7, 8, 9, 10, 11, 12):
             arrived(n)
+
+    def sent():
         for one in first + plan:
             one.wait_send()
 
-    return start, assemble, forward_one, forward_two, finish
+    return start, assemble, forward_one, forward_two, finish, sent
 
 
 def image_steps(blocks, whole, send, recv, local_sem, images, home):
@@ -354,7 +355,7 @@
     return start, arrived, sent
 
 
-def reduce_steps(grads, pairs, inter, out_stage, in_stage, sems, chunk, lo, hi, emit):
+def reduce_steps(grads, pairs, inter, out_stage, in_stage, sems, chunk, lo, hi, narrow):
     d, z = lax.axis_index("dp"), lax.axis_index("seq")
     dx, dy, dc = other(d, "x"), other(d, "y"), other(d, "core")
     core = lax.rem(d, 2)
@@ -383,10 +384,12 @@
         hop(0, md, 0, over_y), hop(1, md, 1, over_x), hop(2, my, 0, over_y),
         hop(3, mx, 1, over_x), hop(4, mx, 0, over_x), hop(5, my, 1, over_y),
     ]
-    narrow = slice(lo // 2, hi // 2)
+    local_copy = pltpu.make_async_copy(
+        out_stage.at[z, :, narrow], in_stage.at[3, :, narrow], recv3.at[chunk * 4 + 3]
+    )
     step3 = []
     for k in range(1, 4):
-        n = chunk * 3 + k - 1
+        n = chunk * 4 + k - 1
         there = lax.rem(z + k, 4)
         step3.append(
             remote(
@@ -422,20 +425,22 @@
         top = own[:half] + inter[2, :, cols].astype(F32) + inter[4, :, cols].astype(F32)
         low = own[half:] + inter[3, :, cols].astype(F32) + inter[5, :, cols].astype(F32)
         total = jnp.concatenate([top, low], axis=0)
-        middle = (hi - lo) // 2
+        middle = narrow.stop - narrow.start
+        if 2 * middle > hi - lo:
+            filler = jnp.zeros((rows, 2 * middle - (hi - lo)), F32)
+            total = jnp.concatenate([total, filler], axis=1)
         for t in range(4):
             shard = total[t * quarter : (t + 1) * quarter]
             both = jnp.concatenate([shard[:, :middle], shard[:, middle:]], axis=0)
             out_stage[t, :, narrow] = both.astype(BF)
         for c in step3:
             c.start()
+        local_copy.start()
 
     def five():
-        total = out_stage[z, :, narrow].astype(F32)
-        for k in range(3):
-            step3[k].wait_recv()
-            total = total + in_stage[k, :, narrow].astype(F32)
-        emit(jnp.concatenate([total[:quarter], total[quarter:]], axis=1))
+        for c in step3:
+            c.wait_recv()
+        local_copy.wait()
 
     def sent():
         for c in step1 + step2 + step3:
@@ -485,15 +490,17 @@
 
 
 def block_kernel(
-    lengths, w_qkv, w_out, smalls, tokens, cotangent, w_up, w_down,
-    block_out, grad_input, grad_qkv, grad_out_w, grad_small, grad_up, grad_down,
-    packed, stage, full, small, xs, cots, qkv, probs, attended, middle, n_one, n_two,
+    lengths, w_qkv, w_out, router_own, gain_a, shift_a, gain_b, shift_b, tokens, cotangent,
+    w_up, w_down,
+    block_out, g_blocks, in_stage, rows_low, active, d_rows, d_hidden,
+    stage_a, stage_b, full, corner, small, xs, cots, qkv, probs, attended, middle, n_one, n_two,
     disp, comb, dcomb, slots, bias, up, down, out_rows, pair_in, pair_out, row_sums,
     recv_a, recv_b, recv_c, recv_d, send_b, send_d, turned_one, turned_att,
-    d_norm, d_diff, d_branch, d_attended, d_qkv, g_rows, g_blocks, cot_home,
-    grads, pairs_buf, inter, out_stage, in_stage,
+    d_norm, d_diff, d_branch, d_attended, d_qkv, g_rows,
+    grads, pairs_buf, inter, out_stage,
     zsend, zrecv, wsend, wrecv, tsend, trecv, csend, crecv, bsend, brecv, gsend, grecv,
-    local, loads, swap_send, swap_recv, send1, recv1, send2, recv2, send3, recv3,
+    t_local, c_local, b_local, g_local, loads, swap_send, swap_recv,
+    send1, recv1, send2, recv2, send3, recv3,
 ):
     d, z = lax.axis_index("dp"), lax.axis_index("seq")
     width = tokens.shape[2]
@@ -503,52 +510,57 @@
     groups = width // 256
     experts = disp.shape[0]
     devices = recv_a.shape[0]
-    me = d * 4 + z
+    base_qkv, base_out = SMALL, SMALL + 3 * width
 
     barrier = pltpu.get_barrier_semaphore()
-
-    def greet(k, carry):
-        j = lax.rem(me + k, devices)
-        pl.semaphore_signal(
-            barrier, inc=1, device_id=(j // 4, lax.rem(j, 4)), device_id_type=MESH
-        )
-        return carry
-
-    lax.fori_loop(1, devices, greet, 0)
+    partners = [(d, lax.rem(z + k, 4)) for k in range(1, 4)]
+    partners += [(other(d, kind), z) for kind in ("x", "y", "core")]
+    for partner in partners:
+        pl.semaphore_signal(barrier, inc=1, device_id=partner, device_id_type=MESH)
     load_up = pltpu.make_async_copy(w_up.at[0], up, loads.at[0])
     load_down = pltpu.make_async_copy(w_down.at[0], down, loads.at[1])
-    load_home = pltpu.make_async_copy(cotangent, cot_home, loads.at[2])
-    for load in (load_up, load_down, load_home):
-        load.start()
-    own = w_qkv[...]
-    pieces = [w_out[...]]
+    load_up.start()
+    load_down.start()
+    own_rows = w_out.shape[0]
+    corner[...] = jnp.zeros_like(corner)
+    corner[0:experts, 0:own_rows] = router_own[...].astype(F32)
+    for k, vector in enumerate((gain_a, shift_a, gain_b, shift_b)):
+        corner[experts + k : experts + k + 1, 0:own_rows] = vector[...].astype(F32)
+    own = w_qkv[...].astype(F32)
+    pieces = [corner[...].T[:own_rows]]
     for g in range(groups):
         for k in range(3):
             pieces.append(own[:, k * width + g * 256 : k * width + (g + 1) * 256])
-    pieces.append(smalls[...])
-    line = jnp.concatenate([piece.astype(F32) for piece in pieces], axis=1)
-    wide = packed.shape[1]
-    packed[...] = jnp.concatenate([line[:, :wide], line[:, wide:]], axis=0).astype(BF)
-    pl.semaphore_wait(barrier, devices - 1)
-
-    w_start, w_assemble, w_one, w_two, w_finish = gather_steps(
-        packed, stage, full, zsend, zrecv, wsend, wrecv
-    )
-    t_start, t_arrived, t_sent = image_steps(tokens, xs, tsend, trecv, local, images, False)
-    c_start, c_arrived, c_sent = image_steps(cotangent, cots, csend, crecv, local, images, False)
-    w_start()
+    pieces += [w_out[...].astype(F32), jnp.zeros((own_rows, 128), F32)]
+    line = jnp.concatenate(pieces, axis=1)
+    cut = 2 * stage_a.shape[2]
+    for ref, part in ((stage_a, line[:, :cut]), (stage_b, line[:, cut:])):
+        wide = ref.shape[2]
+        ref[z] = jnp.concatenate([part[:, :wide], part[:, wide:]], axis=0).astype(BF)
+    pl.semaphore_wait(barrier, len(partners))
+
+    weight_sems = (zsend, zrecv, wsend, wrecv)
+    wa_start, wa_assemble, wa_one, wa_two, wa_finish, wa_sent = gather_steps(
+        stage_a, full, 0, cut, *weight_sems, 0
+    )
+    wb_start, wb_assemble, wb_one, wb_two, wb_finish, wb_sent = gather_steps(
+        stage_b, full, cut, base_out + width, *weight_sems, 1
+    )
+    t_start, t_arrived, t_sent = image_steps(tokens, xs, tsend, trecv, t_local, images, False)
+    c_start, c_arrived, c_sent = image_steps(cotangent, cots, csend, crecv, c_local, images, False)
+    wa_start()
+    wb_start()
+    wa_assemble()
+    wb_assemble()
     for i in range(images):
         t_start(i)
-    w_assemble()
-    w_one()
-    w_two()
-    for i in range(images):
-        t_arrived(i)
-    for i in range(images):
-        c_start(i)
-    w_finish()
-    small[...] = full[:, 4 * width : 4 * width + 128].astype(F32).T[:16]
+    wa_one()
+    wa_two()
+    wb_one()
+    wa_finish()
+    small[...] = full[:, 0:128].astype(F32).T[:16]
     gains = [small[8 + k : 9 + k, :] for k in range(4)]
+    wb_two()
 
     def norm_one(k, carry):
         at = ds(k * ROWS, ROWS)
@@ -556,10 +568,18 @@
         n_one[at, :] = (unit * gains[0] + gains[1]).astype(BF)
         return carry
 
-    lax.fori_loop(0, count // ROWS, norm_one, 0)
+    per_image = length // ROWS
+    for i in range(images):
+        t_arrived(i)
+        if i == images - 1:
+            for k in range(images):
+                c_start(k)
+        lax.fori_loop(i * per_image, (i + 1) * per_image, norm_one, 0)
+    wb_finish()
 
     def project(k, carry):
-        qkv[:, ds(k * 256, 256)] = mm(n_one[...], full[:, ds(width + k * 256, 256)]).astype(BF)
+        weight = full[:, ds(base_qkv + k * 256, 256, 128)]
+        qkv[:, ds(k * 256, 256)] = mm(n_one[...], weight).astype(BF)
         return carry
 
     lax.fori_loop(0, 3 * groups, project, 0)
@@ -568,9 +588,10 @@
     for i in range(images):
         bias[i] = jnp.where(key < lengths[z * images + i], 0.0, -1000000000.0)
     scale = jnp.asarray(HD ** (-0.5), BF)
+    pairs = 2 * groups
 
     def heads(t):
-        i, p = lax.rem(t, images), t // images
+        i, p = t // pairs, pairs - 1 - lax.rem(t, pairs)
         base = (p // 2) * 768 + lax.rem(p, 2) * 128
         return i, p, ds(i * length, length), base
 
@@ -587,11 +608,12 @@
         attended[at, ds(p * 128, 128)] = mm(probs[t], values).astype(BF)
         return carry
 
-    lax.fori_loop(0, images * 2 * groups, attend, 0)
+    lax.fori_loop(0, images * pairs, attend, 0)
 
     def project_out(k, carry):
         at = ds(k * 256, 256)
-        middle[:, at] = xs[:, at].astype(F32) + mm(attended[...], full[:, at])
+        weight = full[:, ds(base_out + k * 256, 256, 128)]
+        middle[:, at] = xs[:, at].astype(F32) + mm(attended[...], weight)
         return carry
 
     lax.fori_loop(0, groups, project_out, 0)
@@ -657,11 +679,11 @@
     load_up.wait()
     load_down.wait()
     swap_a[1]()
-    rows_low = from_pairs(recv_a)
-    hidden = mm(rows_low, up[...])
-    active, slope = gelu_parts(hidden)
-    active = active.astype(BF)
-    spread(send_b, mm(active, down[...]))
+    rows_low[...] = from_pairs(recv_a)
+    hidden = mm(rows_low[...], up[...])
+    act, slope = gelu_parts(hidden)
+    active[...] = act.astype(BF)
+    spread(send_b, mm(active[...], down[...]))
     swap_b[0]()
     turned_att[...] = attended[...].T
     swap_b[1]()
@@ -674,24 +696,22 @@
     to_pairs(1, sends)
     swap_c[0]()
     b_start, b_arrived, b_sent = image_steps(
-        block_out, out_rows, bsend, brecv, local, images, True
+        block_out, out_rows, bsend, brecv, b_local, images, True
     )
     for i, at in enumerate(spans):
         for k in range(groups):
-            cut = slice(k * 256, (k + 1) * 256)
-            moe = tn(combs[i], outs[i][:, cut])
-            out_rows[at, cut] = (middle[at, cut] + moe).astype(BF)
+            cols = slice(k * 256, (k + 1) * 256)
+            moe = tn(combs[i], outs[i][:, cols])
+            out_rows[at, cols] = (middle[at, cols] + moe).astype(BF)
     swap_c[1]()
-    d_rows = from_pairs(recv_c)
-    d_active = nt(d_rows, down[...])
-    d_hidden = (d_active * slope).astype(BF)
-    spread(send_d, nt(d_hidden, up[...]))
+    d_rows[...] = from_pairs(recv_c)
+    d_active = nt(d_rows[...], down[...])
+    d_hidden[...] = (d_active * slope).astype(BF)
+    spread(send_d, nt(d_hidden[...], up[...]))
     swap_d[0]()
-    grad_down[0] = tn(active, d_rows)
-    grad_up[0] = tn(rows_low, d_hidden)
-    swap_d[1]()
     for i in range(images):
         b_start(i)
+    swap_d[1]()
     d_slots = collect(recv_d)
 
     router_grad = jnp.zeros((experts, width), F32)
@@ -714,8 +734,8 @@
             [high, scaled - high, small[0:8, :], jnp.zeros_like(scaled)], axis=0
         ).astype(BF)
         for k in range(groups):
-            cut = slice(k * 256, (k + 1) * 256)
-            d_norm[at, cut] = tn(left, right[:, cut])
+            cols = slice(k * 256, (k + 1) * 256)
+            d_norm[at, cols] = tn(left, right[:, cols])
 
     nothing = jnp.zeros((8, width), F32)
 
@@ -730,42 +750,27 @@
 
     gain_two, shift_two = lax.fori_loop(0, count // ROWS, back_two, (nothing, nothing))
 
-    def emit_out(value):
-        grad_out_w[...] = value
-
-    def emit_group(g):
-        def emit(value):
-            for k in range(3):
-                grad_qkv[:, k * width + g * 256 : k * width + (g + 1) * 256] = value[
-                    :, k * 256 : (k + 1) * 256
-                ]
-            if value.shape[1] > 768:
-                grad_small[...] = value[:, 768:896]
-
-        return emit
-
     sems = (send1, recv1, send2, recv2, send3, recv3)
-    chunks = []
-    for c in range(groups + 1):
-        hi = grads.shape[1] if c == groups else (c + 1) * 768
-        emit = emit_out if c == 0 else emit_group(c - 1)
-        chunks.append(
-            reduce_steps(
-                grads, pairs_buf, inter, out_stage, in_stage, sems, c, c * 768, hi, emit
-            )
+    chunks = [
+        reduce_steps(
+            grads, pairs_buf, inter, out_stage, in_stage, sems, c, lo, hi, narrow
         )
+        for c, (lo, hi, narrow) in enumerate(chunk_table(width))
+    ]
+    c_out, c_pos = chunks[groups], chunks[:groups]
 
     def grad_out(k, carry):
-        at = ds(k * 256, 256)
-        grads[:, at] = mm(turned_att[...], d_branch[:, at]).astype(BF)
+        cols = ds(k * 256, 256)
+        to = ds(base_out + k * 256, 256, 128)
+        grads[:, to] = mm(turned_att[...], d_branch[:, cols]).astype(BF)
         return carry
 
     lax.fori_loop(0, groups, grad_out, 0)
-    chunks[0][0]()
+    c_out[0]()
 
     def back_out(k, carry):
         at = ds(k * 256, 256)
-        d_attended[:, at] = nt(d_branch[...], full[at, 0:width]).astype(BF)
+        d_attended[:, at] = nt(d_branch[...], full[at, base_out : base_out + width]).astype(BF)
         return carry
 
     lax.fori_loop(0, groups, back_out, 0)
@@ -794,47 +799,56 @@
     def group_grads(g):
         def one(k, carry):
             at = ds(g * 768 + k * 256, 256)
-            to = ds(width + g * 768 + k * 256, 256)
+            to = ds(base_qkv + g * 768 + k * 256, 256, 128)
             grads[:, to] = mm(turned_one[...], d_qkv[:, at]).astype(BF)
             return carry
 
         lax.fori_loop(0, 3, one, 0)
 
-    per_group = 2 * images
-    lax.fori_loop(0, per_group, attend_back, 0)
-    chunks[0][1]()
-    group_grads(0)
-    chunks[1][0]()
-    lax.fori_loop(per_group, 2 * per_group, attend_back, 0)
-    chunks[0][2]()
-    chunks[1][1]()
+    def input_grads(i, carry):
+        at = spans[i]
+
+        def back_qkv(k, carry):
+            cols = ds(k * 256, 256)
+            d_norm[at, cols] = nt(d_qkv[at, :], full[cols, base_qkv : base_qkv + 3 * width])
+            return carry
+
+        def back_one(k, carry):
+            at = ds(k * ROWS, ROWS)
+            grad = d_norm[at, :]
+            unit, inverse = unit_rows(xs[at, :].astype(F32))
+            change = norm_rows_back(grad, unit, inverse, gains[0])
+            g_rows[at, :] = (change + d_diff[at, :]).astype(BF)
+            return carry[0] + fold_rows(grad * unit), carry[1] + fold_rows(grad)
+
+        lax.fori_loop(0, groups, back_qkv, 0)
+        carry = lax.fori_loop(i * per_image, (i + 1) * per_image, back_one, carry)
+        g_start(i)
+        return carry
+
+    g_start, g_arrived, g_sent = image_steps(
+        g_blocks, g_rows, gsend, grecv, g_local, images, True
+    )
+    sums_one = (nothing, nothing)
+    for i in range(images - 1):
+        lax.fori_loop(i * pairs, (i + 1) * pairs, attend_back, 0)
+        if i == 0:
+            c_out[1]()
+        sums_one = input_grads(i, sums_one)
+    begin = (images - 1) * pairs
+    lax.fori_loop(begin, begin + 2, attend_back, 0)
+    c_out[2]()
+    group_grads(2)
+    c_pos[2][0]()
+    lax.fori_loop(begin + 2, begin + 4, attend_back, 0)
+    c_out[3]()
+    c_pos[2][1]()
     group_grads(1)
-    chunks[2][0]()
-    lax.fori_loop(2 * per_group, 3 * per_group, attend_back, 0)
-    chunks[0][3]()
-    chunks[1][2]()
-    chunks[2][1]()
-
-    def back_qkv(k, carry):
-        at = ds(k * 256, 256)
-        d_norm[:, at] = nt(d_qkv[...], full[at, width : 4 * width])
-        return carry
-
-    lax.fori_loop(0, groups, back_qkv, 0)
-
-    def back_one(k, carry):
-        at = ds(k * ROWS, ROWS)
-        grad = d_norm[at, :]
-        unit, inverse = unit_rows(xs[at, :].astype(F32))
-        change = norm_rows_back(grad, unit, inverse, gains[0])
-        g_rows[at, :] = (change + d_diff[at, :]).astype(BF)
-        return carry[0] + fold_rows(grad * unit), carry[1] + fold_rows(grad)
-
-    gain_one, shift_one = lax.fori_loop(0, count // ROWS, back_one, (nothing, nothing))
-    g_start, g_arrived, g_sent = image_steps(g_blocks, g_rows, gsend, grecv, local, images, True)
-    for i in range(images):
-        b_arrived(i)
-        g_start(i)
+    c_pos[1][0]()
+    lax.fori_loop(begin + 4, begin + 6, attend_back, 0)
+    c_pos[2][2]()
+    c_pos[1][1]()
+    gain_one, shift_one = input_grads(images - 1, sums_one)
     sums = [
         jnp.sum(value, axis=0, keepdims=True)
         for value in (gain_one, shift_one, gain_two, shift_two)
@@ -842,36 +856,72 @@
     tall = jnp.concatenate(
         [router_grad] + sums + [jnp.zeros((128 - experts - 4, width), F32)], axis=0
     )
-    grads[:, 4 * width : 4 * width + 128] = tall.T.astype(BF)
-    grads[:, 4 * width + 128 :] = jnp.zeros((width, SMALL - 128), BF)
-    group_grads(2)
-    chunks[3][0]()
-    chunks[1][3]()
-    chunks[2][2]()
-    chunks[3][1]()
-    chunks[0][4]()
-    chunks[2][3]()
-    chunks[1][4]()
-    chunks[3][2]()
-    chunks[3][3]()
-    chunks[2][4]()
+    grads[:, 0:SMALL] = tall.T.astype(BF)
+    group_grads(0)
+    c_pos[0][0]()
+    c_pos[1][2]()
+    c_pos[2][3]()
+    c_pos[0][1]()
+    c_pos[1][3]()
+    c_pos[0][2]()
+    c_pos[0][3]()
+    for i in range(images):
+        b_arrived(i)
+    c_out[4]()
+    c_pos[2][4]()
+    c_pos[1][4]()
     for i in range(images):
         g_arrived(i)
-        for s in range(4):
-            j = s * images + i
-            grad_input[j] = g_blocks[j].astype(F32) + 0.0
-    load_home.wait()
-    for j in range(4 * images):
-        grad_input[j] = grad_input[j] + cot_home[j].astype(F32)
-    chunks[3][4]()
-    t_sent()
-    c_sent()
-    b_sent()
-    g_sent()
+    c_pos[0][4]()
+    for done in (wa_sent, wb_sent, t_sent, c_sent, b_sent, g_sent):
+        done()
     for swap in (swap_a, swap_b, swap_c, swap_d):
         swap[2]()
     for chunk in chunks:
         chunk[5]()
+
+
+def chunk_table(width):
+    groups = width // 256
+    table = [(0, SMALL + 768, slice(0, 512))]
+    for g in range(1, groups):
+        table.append((SMALL + g * 768, SMALL + (g + 1) * 768, slice(128 + g * 384, 512 + g * 384)))
+    end = 128 + groups * 384
+    table.append((SMALL + 3 * width, SMALL + 4 * width, slice(end, end + width // 2)))
+    return table
+
+
+def finish_kernel(
+    out_in, diff, cotangent, parts, rows_low, active, d_rows, d_hidden,
+    block_out, grad_input, grad_qkv, grad_out_w, grad_small, grad_up, grad_down,
+):
+    block_out[...] = out_in[...]
+    grad_input[...] = diff[...].astype(F32) + cotangent[...].astype(F32)
+    grad_up[0] = tn(rows_low[...], d_hidden[...])
+    grad_down[0] = tn(active[...], d_rows[...])
+
+    @pl.when(pl.program_id(0) == 0)
+    def _():
+        width = grad_out_w.shape[1]
+        quarter = grad_out_w.shape[0]
+        total = parts[0].astype(F32)
+        for k in range(1, 4):
+            total = total + parts[k].astype(F32)
+        for c, (lo, hi, narrow) in enumerate(chunk_table(width)):
+            both = jnp.concatenate([total[:quarter, narrow], total[quarter:, narrow]], axis=1)
+            if c == width // 256:
+                grad_out_w[...] = both
+                continue
+            if c == 0:
+                square = jnp.concatenate(
+                    [both[:, :SMALL], jnp.zeros((128 - quarter, SMALL), F32)], axis=0
+                )
+                grad_small[...] = square.T[:16]
+                both = both[:, SMALL:]
+            for k in range(3):
+                grad_qkv[:, k * width + c * 256 : k * width + (c + 1) * 256] = both[
+                    :, k * 256 : (k + 1) * 256
+                ]
 
 
 def kernel_plan(
@@ -879,38 +929,39 @@
     w_up, w_down, cotangent,
 ):
     own_rows, width = w_out.shape
-    images, size = tokens.shape[0] // 4, tokens.shape[1]
-    length, experts = 4 * size, router.shape[1]
+    blocks, size = tokens.shape[:2]
+    images, length, experts = blocks // 4, 4 * size, router.shape[1]
     count = images * length
     groups = width // 256
     pairs = 2 * groups
     devices = 4 * experts
     columns = 4 * width + SMALL
     fan = w_up.shape[2]
-    vectors = jnp.stack([gain_one, shift_one, gain_two, shift_two], axis=1)
-    filler = jnp.zeros((own_rows, SMALL - experts - 4), BF)
-    smalls = jnp.concatenate([router, vectors, filler], axis=1)
+    wide_a, wide_b = width, width + 128
+    quarter = 4 * own_rows
+    pair = (images, width)
+    rows = devices * images
 
     def shape(*dims, kind=F32):
         return jax.ShapeDtypeStruct(dims, kind)
 
+    dma = pltpu.SemaphoreType.DMA
+    vmem, anywhere = pl.BlockSpec(memory_space=VM), pl.BlockSpec(memory_space=pl.ANY)
+    stage_wide = 512 + (groups - 1) * 384 + width // 2
     outs = (
         shape(*tokens.shape, kind=BF),
-        shape(*tokens.shape),
-        shape(own_rows, 3 * width),
-        shape(own_rows, width),
-        shape(own_rows, 128),
-        shape(*w_up.shape),
-        shape(*w_down.shape),
-    )
-    dma = pltpu.SemaphoreType.DMA
-    vmem, anywhere = pl.BlockSpec(memory_space=VM), pl.BlockSpec(memory_space=pl.ANY)
-    quarter = 4 * own_rows
-    pair = (images, width)
+        shape(*tokens.shape, kind=BF),
+        shape(4, 2 * own_rows, stage_wide, kind=BF),
+        shape(rows, width, kind=BF),
+        shape(rows, fan, kind=BF),
+        shape(rows, width, kind=BF),
+        shape(rows, fan, kind=BF),
+    )
     scratch = [
-        VM((2 * own_rows, columns // 2), BF),
-        VM((4, 2 * own_rows, columns // 2), BF),
-        VM((width, columns), BF),
+        VM((4, 2 * own_rows, wide_a), BF),
+        VM((4, 2 * own_rows, wide_b), BF),
+        VM((width, wide_a * 2 + wide_b * 2), BF),
+        VM((128, 128), F32),
         VM((16, width), F32),
         VM((count, width), BF),
         VM((count, width), BF),
@@ -930,13 +981,10 @@
         VM((count, width), BF),
         VM((2, experts) + pair, BF),
         VM((images, experts, width), F32),
-        VM((devices * images, width), F32),
-        VM((devices,) + pair, BF),
-        VM((devices,) + pair, BF),
-        VM((devices,) + pair, BF),
-        VM((devices,) + pair, BF),
-        VM((devices,) + pair, BF),
-        VM((devices,) + pair, BF),
+        VM((rows, width), F32),
+    ]
+    scratch += [VM((devices,) + pair, BF)] * 6
+    scratch += [
         VM((width, count), BF),
         VM((width, count), BF),
         VM((count, width), F32),
@@ -945,40 +993,80 @@
         VM((count, width), BF),
         VM((count, 3 * width), BF),
         VM((count, width), BF),
-        VM(tokens.shape, BF),
-        VM(tokens.shape, BF),
         VM((width, columns), BF),
         VM((4, quarter, columns), BF),
         VM((6, quarter // 2, columns), BF),
-        VM((4, 2 * own_rows, columns // 2), BF),
-        VM((3, 2 * own_rows, columns // 2), BF),
+        VM((4, 2 * own_rows, stage_wide), BF),
     ]
-    scratch += [dma((3,)), dma((4,)), dma((13,)), dma((13,))]
+    scratch += [dma((6,)), dma((6,)), dma((26,)), dma((26,))]
     scratch += [dma((3 * images,))] * 8
-    scratch += [dma((images,)), dma((3,)), dma((4,)), dma((4,))]
+    scratch += [dma((images,))] * 4
+    scratch += [dma((2,)), dma((4,)), dma((4,))]
     chunks = groups + 1
-    scratch += [dma((4 * chunks,))] * 2 + [dma((6 * chunks,))] * 2 + [dma((3 * chunks,))] * 2
-    block_out, grad_input, grad_qkv, grad_out_w, grad_small, grad_up, grad_down = pl.pallas_call(
+    scratch += [dma((4 * chunks,))] * 2 + [dma((6 * chunks,))] * 2 + [dma((4 * chunks,))] * 2
+    vectors = [vec[None, :] for vec in (gain_one, shift_one, gain_two, shift_two)]
+    out_in, diff, parts, rows_low, active, d_rows, d_hidden = pl.pallas_call(
         block_kernel,
         out_shape=outs,
-        in_specs=[pl.BlockSpec(memory_space=pltpu.SMEM)] + [vmem] * 3 + [anywhere] * 4,
-        out_specs=[anywhere] + [vmem] * 6,
+        in_specs=[pl.BlockSpec(memory_space=pltpu.SMEM)] + [vmem] * 7 + [anywhere] * 4,
+        out_specs=[anywhere] * 3 + [vmem] * 4,
         scratch_shapes=scratch,
         compiler_params=pltpu.CompilerParams(
             collective_id=0, has_side_effects=True, vmem_limit_bytes=63 * 2**20
         ),
         name="block",
-    )(lengths, w_qkv, w_out, smalls, tokens, cotangent, w_up, w_down)
+    )(lengths, w_qkv, w_out, router.T, *vectors, tokens, cotangent, w_up, w_down)
+
+    def by_columns(*dims):
+        return pl.BlockSpec(dims + (256,), lambda k: (0,) * len(dims) + (k,))
+
+    def whole(*dims):
+        return pl.BlockSpec(dims, lambda k: (0,) * len(dims))
+
+    block_out, grad_input, grad_qkv, grad_out_w, grad_small, grad_up, grad_down = pl.pallas_call(
+        finish_kernel,
+        grid=(groups,),
+        out_shape=(
+            shape(*tokens.shape, kind=BF),
+            shape(*tokens.shape),
+            shape(own_rows, 3 * width),
+            shape(own_rows, width),
+            shape(16, 128),
+            shape(*w_up.shape),
+            shape(*w_down.shape),
+        ),
+        in_specs=[
+            by_columns(blocks, size),
+            by_columns(blocks, size),
+            by_columns(blocks, size),
+            whole(4, 2 * own_rows, stage_wide),
+            whole(rows, width),
+            whole(rows, fan),
+            by_columns(rows),
+            by_columns(rows),
+        ],
+        out_specs=[
+            by_columns(blocks, size),
+            by_columns(blocks, size),
+            whole(own_rows, 3 * width),
+            whole(own_rows, width),
+            whole(16, 128),
+            by_columns(1, width),
+            by_columns(1, fan),
+        ],
+        compiler_params=pltpu.CompilerParams(vmem_limit_bytes=63 * 2**20),
+        name="finish",
+    )(out_in, diff, cotangent, parts, rows_low, active, d_rows, d_hidden)
     return (
         block_out,
         grad_input,
         grad_qkv,
         grad_out_w,
-        grad_small[:, :experts],
-        grad_small[:, experts],
-        grad_small[:, experts + 1],
-        grad_small[:, experts + 2],
-        grad_small[:, experts + 3],
+        grad_small[:experts, :own_rows].T,
+        grad_small[experts, :own_rows],
+        grad_small[experts + 1, :own_rows],
+        grad_small[experts + 2, :own_rows],
+        grad_small[experts + 3, :own_rows],
         grad_up,
         grad_down,
     )

time: 169 us -> 138 us (0.82)
  Pallas kernels: 152 us -> 133 us
  local copies, waits for them, and re-layouts: 16 us -> 2.62 us
    pallas_call x1, Pallas kernels: 152 us -> 128 us  [kernel_plan(): pl.pallas_call(block_kernel, out_shape=outs, in_specs=[pl.BlockSpec(memor...]
    unnamed x18 -> x0, local copies, waits for them, and re-layouts: 10.7 us -> none
    pallas_call x0 -> x1, Pallas kernels: none -> 5.87 us  [kernel_plan(): pl.pallas_call(finish_kernel, grid=(groups,), out_shape=(shape(*tokens.sh...]
    another operation x4 -> x0, local copies, waits for them, and re-layouts: 2.99 us -> none  [kernel_plan(): vectors = jnp.stack([gain_one, shift_one, gain_two, shift_two], axis=1)]
where the time goes in v4:
time: 138 us; the launch traced here: 137 us
  Pallas kernels  133 us (96%)
  local copies, waits for them, and re-layouts  2.62 us (2%)
    pallas_call x1, Pallas kernels, kernel_plan(): pl.pallas_call(block_kernel, out_shape=outs, in_specs=[pl.BlockSpec(memor...  128 us
    pallas_call x1, Pallas kernels, kernel_plan(): pl.pallas_call(finish_kernel, grid=(groups,), out_shape=(shape(*tokens.sh...  5.87 us

profile of v4, /device:TPU:0, one launch (start us, length us, event | category | flops | bytes accessed | tf_op | source)
XLA Modules:
  0.0 136.7 jit_solution(9746633721253378150)
XLA Ops:
  0.6 127.5 %block.1 = (bf16[8,64,768]{2,1,0:T(8,128)(2,1)}, bf16[8,64,768]{2,1,0:T(8,128)(2,1)}, bf16[4,48,1664]{2,1,0:T(8,128)(2,1)}, bf16[64,768]{1,0:T(8,128)(2,1)}, bf1...) custom-call(s32[8]{0:T(128)} %lengths.1, bf16[24,2304]{1,0:T(8,128)(2,1)} %w_qkv.1, ...), custom_call_target="tpu_custom_call" | custom-call | tf_op jit(solution)/shard_map/block/pallas_call | solution.py:1008
  128.2 5.9 %finish.1 = (bf16[8,64,768]{2,1,0:T(8,128)(2,1)}, f32[8,64,768]{2,1,0:T(8,128)}, f32[24,2304]{1,0:T(8,128)}, f32[24,768]{1,0:T(8,128)}, f32[16,128]{1,0:T(8,128)...) custom-call(bf16[8,64,768]{2,1,0:T(8,128)(2,1)} %get-tuple-element.25.out_in, ...), custom_call_target="tpu_custom_call" | custom-call | tf_op jit(solution)/shard_map/finish/pallas_call | solution.py:1026
  134.1 1.3 slice_bitcast_fusion.1
  135.4 1.3 slice_bitcast_fusion

commit v5 on v4

--- a/solution.py
+++ b/solution.py
@@ -202,95 +202,140 @@
     return {"x": d + 2 - 4 * x, "y": d + 4 - 8 * y, "core": d + 1 - 2 * core}[kind]
 
 
-def gather_steps(stage, full, lo, hi, zsend, zrecv, send, recv, first_sem):
-    d, z = lax.axis_index("dp"), lax.axis_index("seq")
-    dx, dy, dc = other(d, "x"), other(d, "y"), other(d, "core")
-    half = stage.shape[1]
-    rows = 2 * half
-    over_x, over_y, over_c = (dx, z), (dy, z), (dc, z)
-
-    def block(owner, part):
-        if part is None:
-            return full.at[ds(owner * rows, rows), lo:hi]
-        return full.at[ds(owner * rows + part * half, half), lo:hi]
-
-    mine = stage.at[z]
-    first = []
-    for k in range(1, 4):
-        n = first_sem * 3 + k - 1
-        first.append(remote(mine, mine, zsend.at[n], zrecv.at[n], (d, lax.rem(z + k, 4))))
-
-    def copy(n, owner, part, device):
-        ref, n = block(owner, part), n + 13 * first_sem
-        return remote(ref, ref, send.at[n], recv.at[n], device)
-
-    dd = other(dx, "y")
-    plan = [
-        copy(0, d, 0, over_x), copy(1, d, 1, over_y), copy(2, d, 1, over_x),
-        copy(3, d, 0, over_y), copy(4, d, None, over_c), copy(5, dx, 0, over_y),
-        copy(6, dy, 1, over_x), copy(7, dx, 0, over_c), copy(8, dy, 1, over_c),
-        copy(9, dx, 1, over_c), copy(10, dy, 0, over_c), copy(11, dd, 0, over_c),
-        copy(12, dd, 1, over_c),
-    ]
-    cx, cy = other(dc, "x"), other(dc, "y")
-    cd = other(cx, "y")
-    landing = [
-        (dx, 0), (dy, 1), (dx, 1), (dy, 0), (dc, None), (dd, 0), (dd, 1),
-        (cx, 0), (cy, 1), (cx, 1), (cy, 0), (cd, 0), (cd, 1),
-    ]
-
-    def arrived(n):
-        ref, n = block(*landing[n]), n + 13 * first_sem
-        remote(ref, ref, send.at[n], recv.at[n], over_x).wait_recv()
-
-    def start():
-        for one in first:
-            one.start()
-
-    def assemble():
-        for one in first:
-            one.wait_recv()
-        quarter, wide = half // 2, stage.shape[2]
+class Gather:
+    def __init__(self, shards, full, zup, zdown, zrecv, xsend, xrecv, ysend, yrecv, csend, crecv, dsend, drecv):
+        d, z = lax.axis_index("dp"), lax.axis_index("seq")
+        dx, dy, dc = other(d, "x"), other(d, "y"), other(d, "core")
+        self.shards, self.full, self.z = shards, full, z
+        self.owners = (d, dx, dy, other(dx, "y"))
+        self.over = {"x": (dx, z), "y": (dy, z), "core": (dc, z)}
+        self.up, self.down = (d, lax.rem(z + 1, 4)), (d, lax.rem(z + 3, 4))
+        self.sems = {
+            "up": (zup, zrecv), "down": (zdown, zrecv), "x": (xsend, xrecv),
+            "y": (ysend, yrecv), "core": (csend, crecv), "d": (dsend, drecv),
+        }
+
+    def copy(self, kind, owner, s, device, sem):
+        ref = self.shards.at[owner * 4 + s]
+        send, recv = self.sems[kind]
+        return remote(ref, ref, send.at[sem], recv.at[sem], device)
+
+    def pass_on(self, s, upward, downward):
+        d, z = self.owners[0], self.z
+        if upward:
+
+            @pl.when(z < 3)
+            def _():
+                self.copy("up", d, s, self.up, s).start()
+
+        if downward:
+
+            @pl.when(z > 0)
+            def _():
+                self.copy("down", d, s, self.down, s).start()
+
+        self.copy("x", d, s, self.over["x"], s).start()
+        self.copy("y", d, s, self.over["y"], s).start()
+        self.copy("core", d, s, self.over["core"], s).start()
+
+    def each(self, h, act):
+        if h == 0:
+            act(self.z)
+            return
+
+        @pl.when(self.z >= h)
+        def _():
+            act(self.z - h)
+
+        @pl.when(self.z + h <= 3)
+        def _():
+            act(self.z + h)
+
+    def line(self, h):
+        d, z = self.owners[0], self.z
+        if h == 0:
+            self.pass_on(z, True, True)
+            return
+
+        @pl.when(z >= h)
+        def _():
+            self.copy("up", d, z - h, self.up, z - h).wait_recv()
+            self.pass_on(z - h, True, False)
+
+        @pl.when(z + h <= 3)
+        def _():
+            self.copy("down", d, z + h, self.down, z + h).wait_recv()
+            self.pass_on(z + h, False, True)
+
+    def plane(self, h):
+        d, dx, dy, dd = self.owners
+
+        def act(s):
+            self.copy("x", dx, s, self.over["x"], s).wait_recv()
+
+            @pl.when(lax.rem(s, 2) == 0)
+            def _():
+                self.copy("d", dx, s, self.over["y"], s).start()
+
+            self.copy("core", dx, s, self.over["core"], 4 + s).start()
+            self.copy("y", dy, s, self.over["y"], s).wait_recv()
+
+            @pl.when(lax.rem(s, 2) == 1)
+            def _():
+                self.copy("d", dy, s, self.over["x"], s).start()
+
+            self.copy("core", dy, s, self.over["core"], 8 + s).start()
+
+        self.each(h, act)
+
+    def diagonal(self, h):
+        def act(s):
+            self.copy("d", self.owners[3], s, self.over["x"], s).wait_recv()
+            self.copy("core", self.owners[3], s, self.over["core"], 12 + s).start()
+
+        self.each(h, act)
+
+    def twin(self, k):
+        dc = other(self.owners[k], "core")
+        for s in range(4):
+            self.copy("core", dc, s, self.over["core"], 4 * k + s).wait_recv()
+        self.assemble(dc)
+
+    def assemble(self, owner):
+        half, wide = self.shards.shape[1:]
+        quarter = half // 2
         for side in range(2):
             value = jnp.concatenate(
                 [
-                    stage[k].astype(F32)[side * quarter : (side + 1) * quarter]
+                    self.shards[owner * 4 + k].astype(F32)[side * quarter : (side + 1) * quarter]
                     for k in range(4)
                 ],
                 axis=0,
             )
-            base = lo + side * wide
-            full[ds(d * rows, rows), base : base + wide] = value.astype(BF)
-        for n in range(5):
-            plan[n].start()
-
-    def forward_one():
-        arrived(0)
-        plan[5].start()
-        plan[7].start()
-        arrived(1)
-        plan[6].start()
-        plan[8].start()
-
-    def forward_two():
-        arrived(2)
-        plan[9].start()
-        arrived(3)
-        plan[10].start()
-        arrived(5)
-        plan[11].start()
-        arrived(6)
-        plan[12].start()
-
-    def finish():
-        for n in (4, 7, 8, 9, 10, 11, 12):
-            arrived(n)
-
-    def sent():
-        for one in first + plan:
-            one.wait_send()
-
-    return start, assemble, forward_one, forward_two, finish, sent
+            self.full[ds(owner * 2 * half, 2 * half), side * wide : (side + 1) * wide] = (
+                value.astype(BF)
+            )
+
+    def sent(self):
+        d, z = self.owners[0], self.z
+
+        def one(s, carry):
+            @pl.when((s <= z) & (z < 3))
+            def _():
+                self.copy("up", d, s, self.up, s).wait_send()
+
+            @pl.when((s >= z) & (z > 0))
+            def _():
+                self.copy("down", d, s, self.down, s).wait_send()
+
+            self.copy("x", d, s, self.over["x"], s).wait_send()
+            self.copy("y", d, s, self.over["y"], s).wait_send()
+            self.copy("d", d, s, self.over["x"], s).wait_send()
+            for k in range(4):
+                self.copy("core", self.owners[k], s, self.over["core"], 4 * k + s).wait_send()
+            return carry
+
+        lax.fori_loop(0, 4, one, 0)
 
 
 def image_steps(blocks, whole, send, recv, local_sem, images, home):
@@ -493,12 +538,12 @@
     lengths, w_qkv, w_out, router_own, gain_a, shift_a, gain_b, shift_b, tokens, cotangent,
     w_up, w_down,
     block_out, g_blocks, in_stage, rows_low, active, d_rows, d_hidden,
-    stage_a, stage_b, full, corner, small, xs, cots, qkv, probs, attended, middle, n_one, n_two,
+    shards, full, corner, small, xs, cots, qkv, probs, attended, middle, n_one, n_two,
     disp, comb, dcomb, slots, bias, up, down, out_rows, pair_in, pair_out, row_sums,
     recv_a, recv_b, recv_c, recv_d, send_b, send_d, turned_one, turned_att,
     d_norm, d_diff, d_branch, d_attended, d_qkv, g_rows,
     grads, pairs_buf, inter, out_stage,
-    zsend, zrecv, wsend, wrecv, tsend, trecv, csend, crecv, bsend, brecv, gsend, grecv,
+    zup, zdown, zrecv, xsend, xrecv, ysend, yrecv, wsend, wrecv, dsend, drecv, tsend, trecv, csend, crecv, bsend, brecv, gsend, grecv,
     t_local, c_local, b_local, g_local, loads, swap_send, swap_recv,
     send1, recv1, send2, recv2, send3, recv3,
 ):
@@ -533,34 +578,36 @@
             pieces.append(own[:, k * width + g * 256 : k * width + (g + 1) * 256])
     pieces += [w_out[...].astype(F32), jnp.zeros((own_rows, 128), F32)]
     line = jnp.concatenate(pieces, axis=1)
-    cut = 2 * stage_a.shape[2]
-    for ref, part in ((stage_a, line[:, :cut]), (stage_b, line[:, cut:])):
-        wide = ref.shape[2]
-        ref[z] = jnp.concatenate([part[:, :wide], part[:, wide:]], axis=0).astype(BF)
+    wide = shards.shape[2]
+    shards[d * 4 + z] = jnp.concatenate([line[:, :wide], line[:, wide:]], axis=0).astype(BF)
     pl.semaphore_wait(barrier, len(partners))
 
-    weight_sems = (zsend, zrecv, wsend, wrecv)
-    wa_start, wa_assemble, wa_one, wa_two, wa_finish, wa_sent = gather_steps(
-        stage_a, full, 0, cut, *weight_sems, 0
-    )
-    wb_start, wb_assemble, wb_one, wb_two, wb_finish, wb_sent = gather_steps(
-        stage_b, full, cut, base_out + width, *weight_sems, 1
+    gather = Gather(
+        shards, full, zup, zdown, zrecv, xsend, xrecv, ysend, yrecv, wsend, wrecv, dsend, drecv
     )
     t_start, t_arrived, t_sent = image_steps(tokens, xs, tsend, trecv, t_local, images, False)
     c_start, c_arrived, c_sent = image_steps(cotangent, cots, csend, crecv, c_local, images, False)
-    wa_start()
-    wb_start()
-    wa_assemble()
-    wb_assemble()
+    gather.line(0)
+    gather.line(1)
+    gather.plane(0)
+    gather.line(2)
+    gather.plane(1)
+    gather.diagonal(0)
+    gather.line(3)
     for i in range(images):
         t_start(i)
-    wa_one()
-    wa_two()
-    wb_one()
-    wa_finish()
+    gather.plane(2)
+    gather.diagonal(1)
+    gather.assemble(d)
+    gather.plane(3)
+    gather.diagonal(2)
+    gather.twin(0)
+    gather.diagonal(3)
+    for k in range(1, 4):
+        gather.assemble(gather.owners[k])
+        gather.twin(k)
     small[...] = full[:, 0:128].astype(F32).T[:16]
     gains = [small[8 + k : 9 + k, :] for k in range(4)]
-    wb_two()
 
     def norm_one(k, carry):
         at = ds(k * ROWS, ROWS)
@@ -575,7 +622,6 @@
             for k in range(images):
                 c_start(k)
         lax.fori_loop(i * per_image, (i + 1) * per_image, norm_one, 0)
-    wb_finish()
 
     def project(k, carry):
         weight = full[:, ds(base_qkv + k * 256, 256, 128)]
@@ -673,9 +719,13 @@
 
     to_pairs(0, [slots[i] for i in range(images)])
     swap_a[0]()
-    for i in range(images):
+    combs = [comb[:, at].astype(BF) for at in spans]
+    sends = []
+    for i, at in enumerate(spans):
         c_arrived(i)
-    turned_one[...] = n_one[...].T
+        sends.append(mm(combs[i], cots[at, :]))
+    to_pairs(1, sends)
+    swap_c[0]()
     load_up.wait()
     load_down.wait()
     swap_a[1]()
@@ -685,31 +735,25 @@
     active[...] = act.astype(BF)
     spread(send_b, mm(active[...], down[...]))
     swap_b[0]()
-    turned_att[...] = attended[...].T
-    swap_b[1]()
-    outs = collect(recv_b)
-    combs = [comb[:, at].astype(BF) for at in spans]
-    sends = []
-    for i, at in enumerate(spans):
-        sends.append(mm(combs[i], cots[at, :]))
-        dcomb[:, at] = nt(outs[i], cots[at, :])
-    to_pairs(1, sends)
-    swap_c[0]()
-    b_start, b_arrived, b_sent = image_steps(
-        block_out, out_rows, bsend, brecv, b_local, images, True
-    )
-    for i, at in enumerate(spans):
-        for k in range(groups):
-            cols = slice(k * 256, (k + 1) * 256)
-            moe = tn(combs[i], outs[i][:, cols])
-            out_rows[at, cols] = (middle[at, cols] + moe).astype(BF)
     swap_c[1]()
     d_rows[...] = from_pairs(recv_c)
     d_active = nt(d_rows[...], down[...])
     d_hidden[...] = (d_active * slope).astype(BF)
     spread(send_d, nt(d_hidden[...], up[...]))
     swap_d[0]()
-    for i in range(images):
+    turned_one[...] = n_one[...].T
+    turned_att[...] = attended[...].T
+    swap_b[1]()
+    outs = collect(recv_b)
+    b_start, b_arrived, b_sent = image_steps(
+        block_out, out_rows, bsend, brecv, b_local, images, True
+    )
+    for i, at in enumerate(spans):
+        for k in range(groups):
+            cols = slice(k * 256, (k + 1) * 256)
+            moe = tn(combs[i], outs[i][:, cols])
+            out_rows[at, cols] = (middle[at, cols] + moe).astype(BF)
+        dcomb[:, at] = nt(outs[i], cots[at, :])
         b_start(i)
     swap_d[1]()
     d_slots = collect(recv_d)
@@ -873,7 +917,7 @@
     for i in range(images):
         g_arrived(i)
     c_pos[0][4]()
-    for done in (wa_sent, wb_sent, t_sent, c_sent, b_sent, g_sent):
+    for done in (gather.sent, t_sent, c_sent, b_sent, g_sent):
         done()
     for swap in (swap_a, swap_b, swap_c, swap_d):
         swap[2]()
@@ -937,7 +981,6 @@
     devices = 4 * experts
     columns = 4 * width + SMALL
     fan = w_up.shape[2]
-    wide_a, wide_b = width, width + 128
     quarter = 4 * own_rows
     pair = (images, width)
     rows = devices * images
@@ -958,9 +1001,8 @@
         shape(rows, fan, kind=BF),
     )
     scratch = [
-        VM((4, 2 * own_rows, wide_a), BF),
-        VM((4, 2 * own_rows, wide_b), BF),
-        VM((width, wide_a * 2 + wide_b * 2), BF),
+        VM((devices, 2 * own_rows, columns // 2 + 64), BF),
+        VM((width, columns + 128), BF),
         VM((128, 128), F32),
         VM((16, width), F32),
         VM((count, width), BF),
@@ -998,7 +1040,7 @@
         VM((6, quarter // 2, columns), BF),
         VM((4, 2 * own_rows, stage_wide), BF),
     ]
-    scratch += [dma((6,)), dma((6,)), dma((26,)), dma((26,))]
+    scratch += [dma((4,))] * 7 + [dma((16,))] * 2 + [dma((4,))] * 2
     scratch += [dma((3 * images,))] * 8
     scratch += [dma((images,))] * 4
     scratch += [dma((2,)), dma((4,)), dma((4,))]

time: 138 us -> 129 us (0.935)
  Pallas kernels: 133 us -> 125 us
    pallas_call x1, Pallas kernels: 128 us -> 119 us  [kernel_plan(): pl.pallas_call(block_kernel, out_shape=outs, in_specs=[pl.BlockSpec(memor...]
where the time goes in v5:
time: 129 us; the launch traced here: 128 us
  Pallas kernels  125 us (97%)
  local copies, waits for them, and re-layouts  2.62 us (2%)
    pallas_call x1, Pallas kernels, kernel_plan(): pl.pallas_call(block_kernel, out_shape=outs, in_specs=[pl.BlockSpec(memor...  119 us
    pallas_call x1, Pallas kernels, kernel_plan(): pl.pallas_call(finish_kernel, grid=(groups,), out_shape=(shape(*tokens.sh...  5.87 us

profile of v5, /device:TPU:0, one launch (start us, length us, event | category | flops | bytes accessed | tf_op | source)
XLA Modules:
  0.0 128.3 jit_solution(10482446539096702604)
XLA Ops:
  0.6 119.2 %block.1 = (bf16[8,64,768]{2,1,0:T(8,128)(2,1)}, bf16[8,64,768]{2,1,0:T(8,128)(2,1)}, bf16[4,48,1664]{2,1,0:T(8,128)(2,1)}, bf16[64,768]{1,0:T(8,128)(2,1)}, bf1...) custom-call(s32[8]{0:T(128)} %lengths.1, bf16[24,2304]{1,0:T(8,128)(2,1)} %w_qkv.1, ...), custom_call_target="tpu_custom_call" | custom-call | tf_op jit(solution)/shard_map/block/pallas_call | solution.py:1050
  119.8 5.9 %finish.1 = (bf16[8,64,768]{2,1,0:T(8,128)(2,1)}, f32[8,64,768]{2,1,0:T(8,128)}, f32[24,2304]{1,0:T(8,128)}, f32[24,768]{1,0:T(8,128)}, f32[16,128]{1,0:T(8,128)...) custom-call(bf16[8,64,768]{2,1,0:T(8,128)(2,1)} %get-tuple-element.25.out_in, ...), custom_call_target="tpu_custom_call" | custom-call | tf_op jit(solution)/shard_map/finish/pallas_call | solution.py:1068
  125.7 1.3 %slice_bitcast_fusion.1 = (f32[24]{0:T(128)}, f32[24]{0:T(128)}, f32[24]{0:T(128)}, f32[24]{0:T(128)}) fusion(f32[16,128]{1,0:T(8,128)} %get-tuple-element.36), kind=kLoop, calls=%fused_computation.1 | loop fusion | bytes 768 | tf_op jit(solution)/shard_map/squeeze | solution.py:1111
  127.0 1.3 slice_bitcast_fusion

commit v6 on v5

--- a/solution.py
+++ b/solution.py
@@ -591,11 +591,11 @@
     gather.line(1)
     gather.plane(0)
     gather.line(2)
+    for i in range(images):
+        t_start(i)
     gather.plane(1)
     gather.diagonal(0)
     gather.line(3)
-    for i in range(images):
-        t_start(i)
     gather.plane(2)
     gather.diagonal(1)
     gather.assemble(d)

time: 129 us -> 124 us (0.961)
  Pallas kernels: 125 us -> 121 us
    pallas_call x1, Pallas kernels: 119 us -> 115 us  [kernel_plan(): pl.pallas_call(block_kernel, out_shape=outs, in_specs=[pl.BlockSpec(memor...]
where the time goes in v6:
time: 124 us
  Pallas kernels  121 us (98%)
  local copies, waits for them, and re-layouts  2.62 us (2%)
    pallas_call x1, Pallas kernels, kernel_plan(): pl.pallas_call(block_kernel, out_shape=outs, in_specs=[pl.BlockSpec(memor...  115 us
    pallas_call x1, Pallas kernels, kernel_plan(): pl.pallas_call(finish_kernel, grid=(groups,), out_shape=(shape(*tokens.sh...  5.87 us

profile of v6, /device:TPU:0, one launch (start us, length us, event | category | flops | bytes accessed | tf_op | source)
XLA Modules:
  0.0 124.0 jit_solution(1132209564418795145)
XLA Ops:
  0.6 114.8 %block.1 = (bf16[8,64,768]{2,1,0:T(8,128)(2,1)}, bf16[8,64,768]{2,1,0:T(8,128)(2,1)}, bf16[4,48,1664]{2,1,0:T(8,128)(2,1)}, bf16[64,768]{1,0:T(8,128)(2,1)}, bf1...) custom-call(s32[8]{0:T(128)} %lengths.1, bf16[24,2304]{1,0:T(8,128)(2,1)} %w_qkv.1, ...), custom_call_target="tpu_custom_call" | custom-call | tf_op jit(solution)/shard_map/block/pallas_call | solution.py:1050
  115.5 5.9 %finish.1 = (bf16[8,64,768]{2,1,0:T(8,128)(2,1)}, f32[8,64,768]{2,1,0:T(8,128)}, f32[24,2304]{1,0:T(8,128)}, f32[24,768]{1,0:T(8,128)}, f32[16,128]{1,0:T(8,128)...) custom-call(bf16[8,64,768]{2,1,0:T(8,128)(2,1)} %get-tuple-element.25.out_in, ...), custom_call_target="tpu_custom_call" | custom-call | tf_op jit(solution)/shard_map/finish/pallas_call | solution.py:1068
  121.4 1.3 %slice_bitcast_fusion.1 = (f32[24]{0:T(128)}, f32[24]{0:T(128)}, f32[24]{0:T(128)}, f32[24]{0:T(128)}) fusion(f32[16,128]{1,0:T(8,128)} %get-tuple-element.36), kind=kLoop, calls=%fused_computation.1 | loop fusion | bytes 768 | tf_op jit(solution)/shard_map/squeeze | solution.py:1111
  122.7 1.3 %slice_bitcast_fusion = f32[24,8]{0,1:T(8,128)} fusion(f32[16,128]{1,0:T(8,128)} %get-tuple-element.36), kind=kLoop, calls=%fused_computation | loop fusion | bytes 1536 | tf_op jit(solution)/shard_map/transpose | solution.py:1107

commit v7 on v5

--- a/solution.py
+++ b/solution.py
@@ -591,10 +591,11 @@
     gather.line(1)
     gather.plane(0)
     gather.line(2)
+    t_start(0)
     gather.plane(1)
     gather.diagonal(0)
     gather.line(3)
-    for i in range(images):
+    for i in range(1, images):
         t_start(i)
     gather.plane(2)
     gather.diagonal(1)
@@ -654,7 +655,7 @@
         attended[at, ds(p * 128, 128)] = mm(probs[t], values).astype(BF)
         return carry
 
-    lax.fori_loop(0, images * pairs, attend, 0)
+    lax.fori_loop(0, images * pairs, attend, 0, unroll=2)
 
     def project_out(k, carry):
         at = ds(k * 256, 256)
@@ -875,21 +876,21 @@
     )
     sums_one = (nothing, nothing)
     for i in range(images - 1):
-        lax.fori_loop(i * pairs, (i + 1) * pairs, attend_back, 0)
+        lax.fori_loop(i * pairs, (i + 1) * pairs, attend_back, 0, unroll=2)
         if i == 0:
             c_out[1]()
         sums_one = input_grads(i, sums_one)
     begin = (images - 1) * pairs
-    lax.fori_loop(begin, begin + 2, attend_back, 0)
+    lax.fori_loop(begin, begin + 2, attend_back, 0, unroll=2)
     c_out[2]()
     group_grads(2)
     c_pos[2][0]()
-    lax.fori_loop(begin + 2, begin + 4, attend_back, 0)
+    lax.fori_loop(begin + 2, begin + 4, attend_back, 0, unroll=2)
     c_out[3]()
     c_pos[2][1]()
     group_grads(1)
     c_pos[1][0]()
-    lax.fori_loop(begin + 4, begin + 6, attend_back, 0)
+    lax.fori_loop(begin + 4, begin + 6, attend_back, 0, unroll=2)
     c_pos[2][2]()
     c_pos[1][1]()
     gain_one, shift_one = input_grads(images - 1, sums_one)

time: 129 us -> 123 us (0.953)
  Pallas kernels: 125 us -> 119 us
    pallas_call x1, Pallas kernels: 119 us -> 114 us  [kernel_plan(): pl.pallas_call(block_kernel, out_shape=outs, in_specs=[pl.BlockSpec(memor...]
where the time goes in v7:
time: 123 us
  Pallas kernels  119 us (97%)
  local copies, waits for them, and re-layouts  2.62 us (2%)
    pallas_call x1, Pallas kernels, kernel_plan(): pl.pallas_call(block_kernel, out_shape=outs, in_specs=[pl.BlockSpec(memor...  114 us
    pallas_call x1, Pallas kernels, kernel_plan(): pl.pallas_call(finish_kernel, grid=(groups,), out_shape=(shape(*tokens.sh...  5.87 us

profile of v7, /device:TPU:0, one launch (start us, length us, event | category | flops | bytes accessed | tf_op | source)
XLA Modules:
  0.0 122.7 jit_solution(9341399033307981283)
XLA Ops:
  0.6 113.5 %block.1 = (bf16[8,64,768]{2,1,0:T(8,128)(2,1)}, bf16[8,64,768]{2,1,0:T(8,128)(2,1)}, bf16[4,48,1664]{2,1,0:T(8,128)(2,1)}, bf16[64,768]{1,0:T(8,128)(2,1)}, bf1...) custom-call(s32[8]{0:T(128)} %lengths.1, bf16[24,2304]{1,0:T(8,128)(2,1)} %w_qkv.1, ...), custom_call_target="tpu_custom_call" | custom-call | tf_op jit(solution)/shard_map/block/pallas_call | solution.py:1051
  114.2 5.9 %finish.1 = (bf16[8,64,768]{2,1,0:T(8,128)(2,1)}, f32[8,64,768]{2,1,0:T(8,128)}, f32[24,2304]{1,0:T(8,128)}, f32[24,768]{1,0:T(8,128)}, f32[16,128]{1,0:T(8,128)...) custom-call(bf16[8,64,768]{2,1,0:T(8,128)(2,1)} %get-tuple-element.25.out_in, ...), custom_call_target="tpu_custom_call" | custom-call | tf_op jit(solution)/shard_map/finish/pallas_call | solution.py:1069
  120.1 1.3 %slice_bitcast_fusion.1 = (f32[24]{0:T(128)}, f32[24]{0:T(128)}, f32[24]{0:T(128)}, f32[24]{0:T(128)}) fusion(f32[16,128]{1,0:T(8,128)} %get-tuple-element.36), kind=kLoop, calls=%fused_computation.1 | loop fusion | bytes 768 | tf_op jit(solution)/shard_map/squeeze | solution.py:1112
  121.4 1.3 %slice_bitcast_fusion = f32[24,8]{0,1:T(8,128)} fusion(f32[16,128]{1,0:T(8,128)} %get-tuple-element.36), kind=kLoop, calls=%fused_computation | loop fusion | bytes 1536 | tf_op jit(solution)/shard_map/transpose | solution.py:1108

commit v8 on v7

--- a/solution.py
+++ b/solution.py
@@ -655,7 +655,7 @@
         attended[at, ds(p * 128, 128)] = mm(probs[t], values).astype(BF)
         return carry
 
-    lax.fori_loop(0, images * pairs, attend, 0, unroll=2)
+    lax.fori_loop(0, images * pairs, attend, 0, unroll=3)
 
     def project_out(k, carry):
         at = ds(k * 256, 256)
@@ -876,7 +876,7 @@
     )
     sums_one = (nothing, nothing)
     for i in range(images - 1):
-        lax.fori_loop(i * pairs, (i + 1) * pairs, attend_back, 0, unroll=2)
+        lax.fori_loop(i * pairs, (i + 1) * pairs, attend_back, 0, unroll=3)
         if i == 0:
             c_out[1]()
         sums_one = input_grads(i, sums_one)

time: 123 us -> 124 us (level)
  no operation moved by 1% of the time
where the time goes in v8:
time: 124 us; the launch traced here: 123 us
  Pallas kernels  120 us (97%)
  local copies, waits for them, and re-layouts  2.62 us (2%)
    pallas_call x1, Pallas kernels, kernel_plan(): pl.pallas_call(block_kernel, out_shape=outs, in_specs=[pl.BlockSpec(memor...  114 us
    pallas_call x1, Pallas kernels, kernel_plan(): pl.pallas_call(finish_kernel, grid=(groups,), out_shape=(shape(*tokens.sh...  5.87 us

profile of v8, /device:TPU:0, one launch (start us, length us, event | category | flops | bytes accessed | tf_op | source)
XLA Modules:
  0.0 123.2 jit_solution(13601888518152116518)
XLA Ops:
  0.6 114.1 %block.1 = (bf16[8,64,768]{2,1,0:T(8,128)(2,1)}, bf16[8,64,768]{2,1,0:T(8,128)(2,1)}, bf16[4,48,1664]{2,1,0:T(8,128)(2,1)}, bf16[64,768]{1,0:T(8,128)(2,1)}, bf1...) custom-call(s32[8]{0:T(128)} %lengths.1, bf16[24,2304]{1,0:T(8,128)(2,1)} %w_qkv.1, ...), custom_call_target="tpu_custom_call" | custom-call | tf_op jit(solution)/shard_map/block/pallas_call | solution.py:1051
  114.7 5.9 %finish.1 = (bf16[8,64,768]{2,1,0:T(8,128)(2,1)}, f32[8,64,768]{2,1,0:T(8,128)}, f32[24,2304]{1,0:T(8,128)}, f32[24,768]{1,0:T(8,128)}, f32[16,128]{1,0:T(8,128)...) custom-call(bf16[8,64,768]{2,1,0:T(8,128)(2,1)} %get-tuple-element.25.out_in, ...), custom_call_target="tpu_custom_call" | custom-call | tf_op jit(solution)/shard_map/finish/pallas_call | solution.py:1069
  120.6 1.3 %slice_bitcast_fusion.1 = (f32[24]{0:T(128)}, f32[24]{0:T(128)}, f32[24]{0:T(128)}, f32[24]{0:T(128)}) fusion(f32[16,128]{1,0:T(8,128)} %get-tuple-element.36), kind=kLoop, calls=%fused_computation.1 | loop fusion | bytes 768 | tf_op jit(solution)/shard_map/squeeze | solution.py:1112
  122.0 1.3 %slice_bitcast_fusion = f32[24,8]{0,1:T(8,128)} fusion(f32[16,128]{1,0:T(8,128)} %get-tuple-element.36), kind=kLoop, calls=%fused_computation | loop fusion | bytes 1536 | tf_op jit(solution)/shard_map/transpose | solution.py:1108
